TPU v7x, 32 devices: a whole 2x2x4 slice. The times are simulated.
32 devices in a mesh: batch: 2 (over core), seq: 16 (over z, y, x).
Axes of the slice: x: 2, y: 2, z: 4, core: 2. Of those that a mesh axis runs over, the one named last changes fastest.
Arguments:
- token_ids: int32 [2, 4096], P('batch', 'seq'), may hold values from 0 to 3
- complement: int32 [4], replicated, may hold values from 0 to 3, each once
- embedding: bfloat16 [4, 1024], replicated, may hold values from -6 to 6
- in_weight: bfloat16 [1024, 2176], replicated, may hold values from -0.1875 to 0.1875
- step_weight: bfloat16 [1024, 16], replicated, may hold values from -0.1875 to 0.1875
- conv_weight: float32 [2, 4, 1152], replicated, may hold values from -3 to 3
- conv_bias: float32 [2, 1152], replicated, may hold values from -3 to 3
- step_bias: float32 [2, 16], replicated, may hold values from -4 to -2
- decay_rate: float32 [2, 16], replicated, as said below
- skip_gain: float32 [2, 16], replicated, may hold values from 0.5 to 1.5
- norm_gain: float32 [2, 1024], replicated, may hold values from 0.1 to 1.9
- out_weight: bfloat16 [1024, 1024], P('seq', 'batch'), may hold values from -0.1875 to 0.1875
Outputs:
- mixer_output: bfloat16 [2, 4096, 1024], P('batch', 'seq')
Inputs may be any that keep to these rules, and one draw needn't show every extreme that they name: `decay_rate`: positive decay rate of each head.
All inputs are finite; a program needn't handle non-finite values.
Results may differ from a plain program's by a relative error of at most 0.0084.
Values may be sent and summed in bfloat16 or wider, within the bound.
No kernel may reach another device: no remote copies, remote signals or barrier semaphores. Data moves between devices by JAX's collectives and lax.ppermute only.
A program may use at most 192 MiB of HBM per device.

v0:
```python
from functools import partial

import jax
import jax.numpy as jnp
from jax import lax
from jax.sharding import PartitionSpec as P

E = 1024
H = 16
HEADDIM = 64
N = 64
BLOCK = 256


exact_mode = lax.Precision.HIGHEST
norm_epsilon = 1e-05


def entering_2(value, axis, combine, identity, reverse):
    length, here = (lax.axis_size(axis), lax.axis_index(axis))
    everything = jax.tree.map(lambda part: lax.all_gather(part, axis), value)
    start = jax.tree.map(
        lambda part, zero: jnp.broadcast_to(jnp.asarray(zero, part.dtype), part.shape),
        value,
        identity,
    )

    def hop(k, before):
        at = length - 1 - k if reverse else k
        reached = at > here if reverse else at < here
        new = combine(before, jax.tree.map(lambda part: part[at], everything))
        return jax.tree.map(lambda a, b: jnp.where(reached, a, b), new, before)

    return lax.fori_loop(0, length, hop, start)


def extended(block, sides, width):
    for axis, dim in sides:
        count = lax.axis_size(axis)
        forward = [(i, i + 1) for i in range(count - 1)]
        backward = [(target, source) for source, target in forward]
        low = lax.ppermute(
            lax.slice_in_dim(block, block.shape[dim] - width, None, axis=dim), axis, forward
        )
        high = lax.ppermute(lax.slice_in_dim(block, 0, width, axis=dim), axis, backward)
        block = jnp.concatenate([low, block, high], axis=dim)
    return block


def block_step(carry_state, inputs):
    values, b_rows, c_rows, step_sizes, decays = inputs
    running = jnp.cumsum(decays, axis=1)
    spread = running[:, :, None] - running[:, None, :]
    positions = jnp.arange(running.shape[1])
    lower_mask = positions[:, None] >= positions[None, :]
    weights = jnp.exp(jnp.where(lower_mask[None], spread, -jnp.inf))
    scores = jnp.dot(
        c_rows.astype(jnp.bfloat16),
        b_rows.astype(jnp.bfloat16).T,
        preferred_element_type=jnp.float32,
    )
    mixing = weights * scores[None] * step_sizes[:, None, :]
    inside = jnp.einsum("hts,shp->thp", mixing, values, precision=exact_mode)
    carried = jnp.einsum("tn,hpn->thp", c_rows, carry_state, precision=exact_mode)
    carried = carried * jnp.exp(running).T[:, :, None]
    to_end = jnp.exp(running[:, -1:] - running) * step_sizes
    fresh_state = jnp.einsum("hs,shp,sn->hpn", to_end, values, b_rows, precision=exact_mode)
    carry_state = carry_state * jnp.exp(running[:, -1])[:, None, None] + fresh_state
    return (carry_state, inside + carried)


def state_scan(values, b_rows, c_rows, step_sizes, decays, block_rows):
    length, head_count, head_width = values.shape
    block_count = length // block_rows
    blocks = (
        values.reshape(block_count, block_rows, head_count, head_width),
        b_rows.reshape(block_count, block_rows, -1),
        c_rows.reshape(block_count, block_rows, -1),
        step_sizes.reshape(block_count, block_rows, head_count).transpose(0, 2, 1),
        decays.reshape(block_count, block_rows, head_count).transpose(0, 2, 1),
    )
    start_state = jnp.zeros((head_count, head_width, b_rows.shape[1]), jnp.float32)
    final_state, outputs = lax.scan(block_step, start_state, blocks)
    return (final_state, outputs.reshape(length, head_count, head_width))


def chain_combine(earlier, later):
    decay_early, state_early = earlier
    decay_late, state_late = later
    return (decay_early * decay_late, decay_late[..., None, None] * state_early + state_late)


def gated_norm(outputs, gate_rows, gain_rows):
    gated = outputs * jax.nn.silu(gate_rows.astype(jnp.float32))
    scale = lax.rsqrt(jnp.mean(gated * gated, axis=-1, keepdims=True) + norm_epsilon)
    return gated * scale * gain_rows[:, None, :]


def complement_of(nucleotides, complement, letters):
    matches = nucleotides[..., None] == letters
    return jnp.sum(jnp.where(matches, complement, 0), axis=-1)


def direction_pass(
    padded, step_raw, conv_weight, conv_bias, step_bias, decay_rate, skip_gain, param_sets, falling
):
    streams, local_len, head_count = step_raw.shape
    kernel = conv_weight.shape[1]
    weight_rows = jnp.stack([conv_weight[set_index] for set_index in param_sets])
    bias_rows = jnp.stack([conv_bias[set_index] for set_index in param_sets])
    step_rows = jnp.stack([step_bias[set_index] for set_index in param_sets])
    rate_rows = jnp.stack([decay_rate[set_index] for set_index in param_sets])
    skip_rows = jnp.stack([skip_gain[set_index] for set_index in param_sets])
    if falling:
        window = jnp.flip(padded[:, kernel - 1 :], axis=1)
        raw_steps = jnp.flip(step_raw, axis=1)
    else:
        window = padded[:, : local_len + kernel - 1]
        raw_steps = step_raw
    conv_total = bias_rows[:, None, :]
    for offset in range(kernel):
        conv_total = conv_total + weight_rows[:, offset][:, None, :] * window[
            :, offset : offset + local_len
        ].astype(jnp.float32)
    conved = jax.nn.silu(conv_total).astype(jnp.bfloat16)
    values = conved[..., :E].astype(jnp.float32).reshape(streams, local_len, H, HEADDIM)
    b_rows = conved[..., E : E + N].astype(jnp.float32)
    c_rows = conved[..., E + N :].astype(jnp.float32)
    step_sizes = jax.nn.softplus(raw_steps + step_rows[:, None, :])
    decays = -rate_rows[:, None, :] * step_sizes
    end_state, outputs = jax.vmap(partial(state_scan, block_rows=BLOCK))(
        values, b_rows, c_rows, step_sizes, decays
    )
    running = jnp.cumsum(decays, axis=1)
    total_decay = jnp.exp(running[:, -1])
    identity = (jnp.ones_like(total_decay), jnp.zeros_like(end_state))
    if falling:
        enter_decay, enter_state = entering_2(
            (total_decay, end_state), "seq", chain_combine, identity, True
        )
    else:
        enter_decay, enter_state = entering_2(
            (total_decay, end_state), "seq", chain_combine, identity, False
        )
    entering = jnp.einsum("stn,shpn->sthp", c_rows, enter_state, precision=exact_mode)
    outputs = outputs + entering * jnp.exp(running)[..., None]
    outputs = outputs + skip_rows[:, None, :, None] * values
    outputs = outputs.reshape(streams, local_len, E)
    if falling:
        outputs = jnp.flip(outputs, axis=1)
    return outputs


def on_device(
    token_ids,
    complement,
    embedding,
    in_weight,
    step_weight,
    conv_weight,
    conv_bias,
    step_bias,
    decay_rate,
    skip_gain,
    norm_gain,
    out_weight,
):
    genomes, local_len = token_ids.shape
    letters = jnp.arange(embedding.shape[0])
    other_ids = complement_of(token_ids, complement, letters)
    rising_sets = [0] * genomes + [1] * genomes
    falling_sets = [1] * genomes + [0] * genomes
    strands = jnp.concatenate([token_ids, other_ids], axis=0)
    streams = strands.shape[0]
    one_hot = (strands.reshape(-1)[:, None] == letters[None, :]).astype(jnp.bfloat16)
    strand_rows = jnp.dot(one_hot, embedding, preferred_element_type=jnp.float32).astype(
        jnp.bfloat16
    )
    projected = jnp.dot(strand_rows, in_weight, preferred_element_type=jnp.float32).astype(
        jnp.bfloat16
    )
    projected = projected.reshape(streams, local_len, -1)
    gate_rows = projected[..., :E]
    conv_input = projected[..., E:]
    step_raw = jnp.dot(strand_rows, step_weight, preferred_element_type=jnp.float32).reshape(
        streams, local_len, -1
    )
    rim_width = conv_weight.shape[1] - 1
    padded = extended(conv_input, (("seq", 1),), rim_width)
    rising = direction_pass(
        padded,
        step_raw,
        conv_weight,
        conv_bias,
        step_bias,
        decay_rate,
        skip_gain,
        rising_sets,
        False,
    )
    rising_normed = gated_norm(
        rising, gate_rows, jnp.stack([norm_gain[set_index] for set_index in rising_sets])
    )
    falling = direction_pass(
        padded,
        step_raw,
        conv_weight,
        conv_bias,
        step_bias,
        decay_rate,
        skip_gain,
        falling_sets,
        True,
    )
    falling_normed = gated_norm(
        falling, gate_rows, jnp.stack([norm_gain[set_index] for set_index in falling_sets])
    )
    mixed_rows = (
        (rising_normed + falling_normed).astype(jnp.bfloat16).reshape(streams * local_len, E)
    )
    columns = lax.all_gather(out_weight, "batch", axis=1, tiled=True)
    strand_out = jnp.dot(
        mixed_rows,
        lax.all_gather(columns, "seq", axis=0, tiled=True),
        preferred_element_type=jnp.float32,
    )
    strand_out = strand_out.astype(jnp.bfloat16).reshape(streams, local_len, -1)
    forward_part = strand_out[:genomes]
    other_part = strand_out[genomes:]
    return (forward_part.astype(jnp.float32) + other_part.astype(jnp.float32)).astype(jnp.bfloat16)


def solution(mesh):
    placed = (
        P("batch", "seq"),
        P(),
        P(),
        P(),
        P(),
        P(),
        P(),
        P(),
        P(),
        P(),
        P(),
        P("seq", "batch"),
    )
    return jax.shard_map(
        on_device, mesh=mesh, in_specs=placed, out_specs=P("batch", "seq", None), check_vma=False
    )
```

profile of v0, /device:TPU:0, one launch (start us, length us, event | category | flops | bytes accessed | tf_op | source)
XLA Modules:
  0.0 563.9 jit_solution(2458599730990283526)
XLA Ops:
  9.2 5.1 convolution_convert_fusion
  22.8 12.7 %slice.230 = bf16[2,256,1152]{1,2,0:T(8,128)(2,1)} reverse(bf16[2,256,1152]{1,2,0:T(8,128)(2,1)S(1)} %copy.148), dimensions={1} | reverse | bytes 2359296 | tf_op jit(solution)/shard_map/slice | solution.py:122
  36.6 3.0 fusion.42
  39.6 18.3 %slice.222 = bf16[2,256,1152]{1,2,0:T(8,128)(2,1)} reverse(bf16[2,256,1152]{1,2,0:T(8,128)(2,1)} %get-tuple-element.343), dimensions={1} | reverse | bytes 2359296 | tf_op jit(solution)/shard_map/slice | solution.py:122
  57.9 18.3 %slice.225 = bf16[2,256,1152]{1,2,0:T(8,128)(2,1)} reverse(bf16[2,256,1152]{1,2,0:T(8,128)(2,1)} %get-tuple-element.345), dimensions={1} | reverse | bytes 2359296 | tf_op jit(solution)/shard_map/slice | solution.py:122
  76.2 12.7 %slice.228 = bf16[2,256,1152]{1,2,0:T(8,128)(2,1)} reverse(bf16[2,256,1152]{1,2,0:T(8,128)(2,1)S(1)} %get-tuple-element.344), dimensions={1} | reverse | bytes 2359296 | tf_op jit(solution)/shard_map/slice | solution.py:122
  88.9 4.1 multiply_convert_fusion
  94.0 2.2 fusion.39
  96.3 5.5 collective-permute-start
  104.8 3.6 multiply_convert_fusion.1
  109.8 2.2 fusion.40
  112.0 2.0 all_gather.32
  116.6 1.8 bitcast_exponential_fusion
  119.1 42.2 %all-gather.2 = f32[32,1,16]{2,1,0:T(1,128)S(1)} all-gather(f32[2,1,16]{2,1,0:T(1,128)S(1)} %bitcast.203), channel_id=4, replica_groups=mesh['batch'=2,'seq'=16] {'seq'}, dimensions={0}, use_global_device_ids=true | all-gather | bytes 2176 | tf_op jit(solution)/shard_map/all_gather | solution.py:21
  165.2 1.8 bitcast_exponential_fusion.1
  167.7 35.6 %all-gather = f32[32,1,16]{2,1,0:T(1,128)S(1)} all-gather(f32[2,1,16]{2,1,0:T(1,128)S(1)} %bitcast.204), channel_id=2, replica_groups=mesh['batch'=2,'seq'=16] {'seq'}, dimensions={0}, use_global_device_ids=true | all-gather | bytes 2176 | tf_op jit(solution)/shard_map/all_gather | solution.py:21
  205.5 2.3 fusion.50
  208.9 3.1 fusion.52
  212.0 1.9 fusion.67
  213.9 78.9 %all-gather.12.cloned.1.call-done = f32[32,16,64,64]{3,2,1,0:T(8,128)} async-done(((f32[2,16,64,64]{3,2,1,0:T(8,128)}), f32[32,16,64,64]{3,2,1,0:T(8,128)}) %all-gather.12.cloned.1.call-update) | async-done | bytes 8388624 | tf_op jit(solution)/shard_map/all_gather | solution.py:21
  292.8 24.6 %while.41 = (s32[]{:T(128)}, f32[2,16,64,64]{3,2,1,0:T(8,128)S(1)}, s32[]{:T(128)}, f32[16,2,16]{2,1,0:T(2,128)S(1)}, f32[16,2,16,64,64]{4,3,2,1,0:T(8,128)}, /*index=5*/s32[]{:T(128)}, s32[]{:T(128)}, s32[]{:T(128)}, s32[]{:T(128)}) while((s32[]{:T(128)}, f32[2,16,64,64]{3,2,1,0:T(8,128)S(1)}, s32[]{:T(128)}, ...), condition=%wide.region_13.14_spmd.clone, body=%wide.region_12.13_spmd.clone.sunk | while | flops 524296 | bytes 1573415 | solution.py:34
  294.3 1.5 fusion.111
  295.8 1.5 fusion.111
  297.3 1.5 fusion.111
  298.9 1.5 fusion.111
  300.4 1.5 fusion.111
  301.9 1.6 fusion.111
  303.6 1.6 fusion.111
  305.3 1.5 fusion.111
  306.8 1.5 fusion.111
  308.3 1.5 fusion.111
  309.8 1.5 fusion.111
  311.3 1.5 fusion.111
  315.9 1.5 fusion.111
  317.4 168.2 %all-gather.10.cloned.1.call-done = f32[32,16,64,64]{3,2,1,0:T(8,128)} async-done(((f32[2,16,64,64]{3,2,1,0:T(8,128)}), f32[32,16,64,64]{3,2,1,0:T(8,128)}) %all-gather.10.cloned.1.call-update) | async-done | bytes 8388624 | tf_op jit(solution)/shard_map/all_gather | solution.py:21
  485.6 24.0 %while.40 = (s32[]{:T(128)}, f32[2,16,64,64]{3,2,1,0:T(8,128)S(1)}, s32[]{:T(128)}, f32[16,2,16]{2,1,0:T(2,128)S(1)}, f32[16,2,16,64,64]{4,3,2,1,0:T(8,128)}, /*index=5*/s32[]{:T(128)}, s32[]{:T(128)}) while((s32[]{:T(128)}, f32[2,16,64,64]{3,2,1,0:T(8,128)S(1)}, s32[]{:T(128)}, f32[16,2,16]{2,1,0:T(2,128)S(1)}, ...), condition=%wide.region_6.7_spmd.clone, body=%wide.region_5.6_spmd.clone.sunk | while | flops 524292 | bytes 1573353 | solution.py:34
  493.1 1.5 fusion.110
  494.6 1.5 fusion.110
  503.6 1.5 fusion.110
  511.6 7.3 %fusion.32 = f32[2,256,16,64]{1,3,2,0:T(8,128)S(1)} fusion(bf16[2,256,16,64]{1,3,2,0:T(8,128)(2,1)S(1)} %bitcast.186, f32[2,256,16,64]{1,3,2,0:T(8,128)S(1)} %fusion.57, f32[2,256,16,64]{1,3,2,0:T(8,128)S(1)} %copy-done.10, f32[2,16,256]{2,1,0:T(8,128)S(1)} %copy-done.23, f32[2,256,256]{2,1,0:T(8,128)} %fusion.64, f32[2,16,256]{2,1,0:T(8,128)S(1)} %copy-done.14, ...), kind=kOutput, calls=%fused_computation.49 | convolution fusion | flops 1622671360 | bytes 8061056 | tf_op jit(solution)/shard_map/vmap()/while/body/eval_jaxpr/hts,shp->thp/dot_general | solution.py:63
  518.9 1.8 copy.130
  520.7 13.7 %rev.11 = f32[2,256,1024]{2,1,0:T(8,128)S(1)} reverse(f32[2,256,1024]{2,1,0:T(8,128)} %copy.130), dimensions={1} | reverse | bytes 4194304 | tf_op jit(solution)/shard_map/jit(_flip)/rev | solution.py:150
  534.5 2.0 fusion.60
  536.5 8.7 %fusion.27 = f32[2,256,16,64]{1,3,2,0:T(8,128)} fusion(bf16[2,256,16,64]{1,3,2,0:T(8,128)(2,1)S(1)} %bitcast.188, f32[2,256,16,64]{1,3,2,0:T(8,128)S(1)} %fusion.60, f32[2,256,16,64]{1,3,2,0:T(8,128)S(1)} %copy-done.9, f32[2,16,256]{2,1,0:T(8,128)S(1)} %copy-done.24, f32[2,256,256]{2,1,0:T(8,128)} %fusion.67, f32[2,16,256]{2,1,0:T(8,128)S(1)} %copy_bitcast_fusion.1, ...), kind=kOutput, calls=%fused_computation.44 | convolution fusion | flops 1622671360 | bytes 8061056 | tf_op jit(solution)/shard_map/vmap()/while/body/eval_jaxpr/hts,shp->thp/dot_general | solution.py:63
  545.2 2.9 copy.119
  548.1 3.0 multiply_reduce_fusion.1
  551.2 2.3 add_convert_fusion
  553.5 2.8 convolution_convert_fusion.1
  (206 shorter events, 55.1 us)
Async XLA Ops:
  6.5 10.6 %copy-start = (bf16[1024,16]{0,1:T(8,128)(2,1)S(1)}, bf16[1024,16]{0,1:T(8,128)(2,1)}, u32[]{:S(2)}) copy-start(bf16[1024,16]{0,1:T(8,128)(2,1)} %param.20) | copy-start | bytes 98308
  6.5 286.3 %all-gather.12.cloned.1.call-start = ((), (), s32[]{:S(2)}) async-start(), calls=%async_computation.2 | async-start | bytes 17825792 | tf_op jit(solution)/shard_map/all_gather | solution.py:21
  9.2 7.8 %copy-start.11 = (f32[2,4,1152]{2,1,0:T(4,128)S(1)}, f32[2,4,1152]{2,1,0:T(4,128)}, u32[]{:S(2)}) copy-start(f32[2,4,1152]{2,1,0:T(4,128)} %param.21) | copy-start | bytes 110596
  9.2 7.8 %copy-start.17 = (f32[2,1152]{1,0:T(2,128)S(1)}, f32[2,1152]{1,0:T(2,128)}, u32[]{:S(2)}) copy-start(f32[2,1152]{1,0:T(2,128)} %param.22) | copy-start | bytes 27652
  9.2 7.8 %copy-start.26 = (f32[2,16]{1,0:T(2,128)S(1)}, f32[2,16]{1,0:T(2,128)}, u32[]{:S(2)}) copy-start(f32[2,16]{1,0:T(2,128)} %param.23) | copy-start | bytes 388
  9.2 7.9 %copy-start.28 = (f32[2,16]{1,0:T(2,128)S(1)}, f32[2,16]{1,0:T(2,128)}, u32[]{:S(2)}) copy-start(f32[2,16]{1,0:T(2,128)} %param.24) | copy-start | bytes 388
  14.4 7.7 %copy-start.4 = (bf16[512,2176]{1,0:T(8,128)(2,1)}, bf16[512,2176]{1,0:T(8,128)(2,1)S(1)}, u32[]{:S(2)}) copy-start(bf16[512,2176]{1,0:T(8,128)(2,1)S(1)} %convolution_convert_fusion) | copy-start | bytes 6684676
  15.7 19.8 %collective-permute-start.1 = (bf16[2,3,1152]{2,0,1:T(2,128)(2,1)}, bf16[2,3,1152]{2,0,1:T(2,128)(2,1)}, u32[]{:S(2)}, u32[]{:S(2)}) collective-permute-start(bf16[2,3,1152]{2,0,1:T(2,128)(2,1)} %copy.149), channel_id=1, source_target_pairs={{1,0},{2,1},{3,2},{4,3},{5,4},{6,5},{7,6},{8,7},{9,8},{10,9},{11,1... | collective-permute-start | bytes 41480 | tf_op jit(solution)/shard_map/ppermute | solution.py:45
  19.9 2.2 copy-start.13
  57.9 31.0 %copy-start.18 = (f32[2,1152]{1,0:T(2,128)S(1)}, f32[2,1152]{1,0:T(2,128)}, u32[]{:S(2)}) copy-start(f32[2,1152]{1,0:T(2,128)} %get-tuple-element.376) | copy-start | bytes 27652
  57.9 31.0 %copy-start.19 = (f32[2,1152]{1,0:T(2,128)S(1)}, f32[2,1152]{1,0:T(2,128)}, u32[]{:S(2)}) copy-start(f32[2,1152]{1,0:T(2,128)} %get-tuple-element.377) | copy-start | bytes 27652
  57.9 31.0 %copy-start.20 = (f32[2,1152]{1,0:T(2,128)S(1)}, f32[2,1152]{1,0:T(2,128)}, u32[]{:S(2)}) copy-start(f32[2,1152]{1,0:T(2,128)} %get-tuple-element.378) | copy-start | bytes 27652
  57.9 31.0 %copy-start.21 = (f32[2,1152]{1,0:T(2,128)S(1)}, f32[2,1152]{1,0:T(2,128)}, u32[]{:S(2)}) copy-start(f32[2,1152]{1,0:T(2,128)} %get-tuple-element.379) | copy-start | bytes 27652
  93.1 1.0 copy-start.5
  93.1 3.2 copy-start.15
  93.1 8.7 %copy-start.29 = (f32[2,16]{1,0:T(2,128)S(1)}, f32[2,16]{1,0:T(2,128)}, u32[]{:S(2)}) copy-start(f32[2,16]{1,0:T(2,128)} %param.24) | copy-start | bytes 388
  93.1 8.7 %copy-start.27 = (f32[2,16]{1,0:T(2,128)S(1)}, f32[2,16]{1,0:T(2,128)}, u32[]{:S(2)}) copy-start(f32[2,16]{1,0:T(2,128)} %param.23) | copy-start | bytes 388
  96.2 389.4 %all-gather.10.cloned.1.call-start = ((), (), s32[]{:S(2)}) async-start(), calls=%async_computation.1 | async-start | bytes 17825792 | tf_op jit(solution)/shard_map/all_gather | solution.py:21
  96.3 8.1 %collective-permute-start = (bf16[2,3,1152]{2,0,1:T(2,128)(2,1)S(1)}, bf16[2,3,1152]{2,0,1:T(2,128)(2,1)S(1)}, u32[]{:S(2)}, u32[]{:S(2)}) collective-permute-start(bf16[2,3,1152]{2,0,1:T(2,128)(2,1)S(1)} %copy.147), channel_id=1, source_target_pairs={{0,1},{1,2},{2,3},{3,4},{4,5},{5,6},{6,7},{7,8},{8,9},{9,10},{10,1... | collective-permute-start | bytes 41480 | tf_op jit(solution)/shard_map/ppermute | solution.py:42
  108.4 1.0 copy-start.3
  108.5 1.3 copy-start.7
  108.5 3.5 copy-start.16
  108.5 5.7 %copy-start.12 = (f32[2,2,2,8,128]{4,3,2,1,0:T(8,128)S(1)}, f32[2,2,2,8,128]{4,3,2,1,0:T(8,128)}, u32[]{:S(2)}) copy-start(f32[2,2,2,8,128]{4,3,2,1,0:T(8,128)} %get-tuple-element.357) | copy-start | bytes 98308
  109.8 52.5 %copy-start.30 = (f32[2,16]{1,0:T(2,128)S(1)}, f32[2,16]{1,0:T(2,128)}, u32[]{:S(2)}) copy-start(f32[2,16]{1,0:T(2,128)} %param.25) | copy-start | bytes 388
  112.0 92.3 %copy-start.22 = (f32[2,1024]{1,0:T(2,128)S(1)}, f32[2,1024]{1,0:T(2,128)}, u32[]{:S(2)}) copy-start(f32[2,1024]{1,0:T(2,128)} %param.26) | copy-start | bytes 24580
  112.0 441.5 %all-gather.8.cloned.1.call-start = ((), (), s32[]{:S(2)}) async-start(), calls=%async_computation | async-start | bytes 2228224 | tf_op jit(solution)/shard_map/all_gather | solution.py:224
  509.6 1.2 copy-start.6
  509.6 1.9 copy-start.10
  509.7 1.9 copy-start.14
  509.7 1.9 copy-start.23
  509.7 1.9 copy-start.32
  534.4 2.0 copy-start.8
  534.4 2.0 copy-start.9
  534.4 2.0 copy-start.24
  534.4 2.0 copy-start.25
  534.5 2.0 copy-start.31
  548.1 3.1 copy-start.2
  553.5 3.9 copy-start.1
Sparse Core Ops, SparseCore 0:
  96.4 196.3 all-gather.11
  295.6 189.9 all-gather.9
  488.4 58.8 all-gather.7
where the time goes:
time: 571 us; the launch traced here: 564 us
  waiting for transfers between devices  247 us (43%)
  local copies, waits for them, and re-layouts  99.5 us (17%)
  blocking collectives  79.8 us (14%)
  other arithmetic  74.5 us (13%)
  matrix products  41.2 us (7%)
  between operations  13.8 us (2%)
  starting transfers between devices  6.83 us (1%)
    all_gather x2, waiting for transfers between devices, entering_2(): everything = jax.tree.map(lambda part: lax.all_gather(part, axis), value)  247 us
    all_gather x2, blocking collectives, entering_2(): everything = jax.tree.map(lambda part: lax.all_gather(part, axis), value)  77.8 us
    slice x4, local copies, waits for them, and re-layouts, direction_pass(): window[:, offset:offset + local_len].astype(jnp.float32)  62 us
    select_n x32, other arithmetic, hop(): return jax.tree.map(lambda a, b: jnp.where(reached, a, b), new, before)  47.2 us
    dot_general x2, matrix products, block_step(): inside = jnp.einsum('hts,shp->thp', mixing, values, precision=exact_mode)  16 us
    rev x1, local copies, waits for them, and re-layouts, direction_pass(): outputs = jnp.flip(outputs, axis=1)  13.7 us
  transfers between devices with their start and end apart: 5, of which 2 were waited for; matrix products, arithmetic and copies ran while one was open for 25% of the time, Pallas kernels for 0%

commit v1 on v0

v1 whole, which is shorter than its diff:
```python
from functools import partial

import jax
import jax.numpy as jnp
import ml_dtypes
import numpy as np
from jax import lax
from jax.experimental import pallas as pl
from jax.experimental.pallas import tpu as pltpu
from jax.sharding import PartitionSpec as P

BLOCK = 256
CHUNK = 64
LANES = 128
WIDE = 256
LOG2E = 1.4426950408889634
EPSILON = 1e-05
F32 = jnp.float32
BF16 = jnp.bfloat16

TN = (((0,), (0,)), ((), ()))
NT = (((1,), (1,)), ((), ()))
NN = (((1,), (0,)), ((), ()))


def dot(a, b, dims=NN):
    return lax.dot_general(a, b, dims, preferred_element_type=F32)


def iota(shape, dim):
    return lax.broadcasted_iota(jnp.int32, shape, dim)


def split3(x):
    high = x.astype(BF16)
    rest = x - high.astype(F32)
    middle = rest.astype(BF16)
    low = (rest - middle.astype(F32)).astype(BF16)
    return high, middle, low


def silu(x):
    return x / (1.0 + jnp.exp(-x))


def word_plan(letters, taps):
    starts = {taps: 0}
    rows = letters**taps
    for length in range(taps - 1, 0, -1):
        starts[length] = rows
        rows += letters**length
    return starts, rows, -(-rows // 32) * 32


def word_letters(letters, taps):
    starts, rows, padded = word_plan(letters, taps)
    table = np.full((padded, taps), -1, np.int64)
    for length, start in starts.items():
        codes = np.arange(letters**length)
        for back in range(length):
            table[start : start + letters**length, taps - 1 - back] = codes // letters**back % letters
    return table


def word_select(letters, taps):
    table = word_letters(letters, taps)
    part = -(-letters * taps // 16) * 16
    select = np.zeros((table.shape[0], 4 * part), np.float32)
    for tap in range(taps):
        rows = np.nonzero(table[:, tap] >= 0)[0]
        for copy in range(3):
            select[rows, copy * part + tap * letters + table[rows, tap]] = 1
    select[:, 3 * part : 3 * part + 3] = 1
    last = np.zeros((table.shape[0], 32), np.float32)
    rows = np.nonzero(table[:, taps - 1] >= 0)[0]
    for copy in range(2):
        last[rows, copy * 16 + table[rows, taps - 1]] = 1
    return select.astype(ml_dtypes.bfloat16), last.astype(ml_dtypes.bfloat16)


PASSES = ((False, 0, 0), (False, 1, 1), (True, 0, 1), (True, 1, 0))


def letter_rows(table, letters, rows, complement):
    row = iota((rows, 1), 0) % letters
    picked = row
    if complement is not None:
        picked = jnp.zeros_like(row)
        for letter in range(letters):
            picked = jnp.where(row == letter, complement(letter), picked)
    result = jnp.broadcast_to(table[0:1], (rows, table.shape[1]))
    for letter in range(1, letters):
        result = jnp.where(picked == letter, table[letter : letter + 1], result)
    return result


def pack_split(x, copies):
    return jnp.concatenate(split3(x)[:copies], axis=0)


def tables_kernel(
    complement_ref,
    embedding_ref,
    in_weight_ref,
    step_weight_ref,
    conv_weight_ref,
    conv_bias_ref,
    step_bias_ref,
    rate_ref,
    skip_ref,
    select_ref,
    last_ref,
    spread_ref,
    words_ref,
    stepped_ref,
    gates_ref,
    decay_ref,
    log_step_ref,
    skip_out_ref,
    narrow_decay_ref,
    narrow_step_ref,
    tall_decay_ref,
):
    letters, width = embedding_ref.shape
    taps = conv_weight_ref.shape[1]
    heads = step_weight_ref.shape[1]
    inner = spread_ref.shape[1]
    state = (conv_weight_ref.shape[2] - inner) // 2
    part = select_ref.shape[1] // 4
    embedding = jnp.concatenate(
        [embedding_ref[...], jnp.zeros((16 - letters, width), BF16)], axis=0
    )
    projected = dot(embedding, in_weight_ref[...]).astype(BF16).astype(F32)
    raw = dot(embedding, step_weight_ref[...])
    complement = lambda letter: complement_ref[letter]
    spread = spread_ref[...]

    def widen(x):
        return sum(dot(piece, spread) for piece in split3(x))

    row = iota((16, heads), 0)
    vectors = jnp.zeros((16, heads), F32)
    for index in range(2):
        vectors = jnp.where(row == index, step_bias_ref[index : index + 1, :], vectors)
        vectors = jnp.where(row == 2 + index, rate_ref[index : index + 1, :], vectors)
        vectors = jnp.where(row == 4 + index, skip_ref[index : index + 1, :], vectors)
    wide_vectors = widen(vectors)
    wide_raw = widen(raw)

    def step_tables(raw_rows, vector_rows, strand, param):
        rows = letter_rows(raw_rows, letters, 8, complement if strand else None)
        shifted = rows + vector_rows[param : param + 1]
        step = jnp.maximum(shifted, 0.0) + jnp.log1p(jnp.exp(-jnp.abs(shifted)))
        decay = -vector_rows[2 + param : 3 + param] * step * LOG2E
        return step, decay, jnp.log2(step)

    gate = silu(projected[:, :inner])
    for strand in range(2):
        rows = letter_rows(gate, letters, 16, complement if strand else None)
        rows = jnp.where(iota((16, 1), 0) < letters, rows, 0.0)
        gates_ref[strand] = pack_split(rows, 2)

    for index, (falls, strand, param) in enumerate(PASSES):
        step, decay, log_step = step_tables(wide_raw, wide_vectors, strand, param)
        decay_ref[index] = decay
        log_step_ref[index] = log_step
        skip_out_ref[index] = jnp.broadcast_to(wide_vectors[4 + param : 5 + param], (8, inner))
        narrow_step, narrow_decay, narrow_log = step_tables(raw, vectors, strand, param)
        narrow_decay_ref[index] = narrow_decay
        narrow_step_ref[index] = narrow_log
        square = jnp.concatenate([narrow_decay, jnp.zeros((8, LANES - heads), F32)], axis=1)
        square = jnp.concatenate([square, jnp.zeros((LANES - 8, LANES), F32)], axis=0)
        tall_decay_ref[index] = square.T[:heads]

        inputs = letter_rows(projected[:, inner:], letters, part, complement if strand else None)
        tap_row = iota((part, 1), 0) // letters
        weights = jnp.zeros((part, inputs.shape[1]), F32)
        for tap in range(taps):
            weights = jnp.where(tap_row == tap, conv_weight_ref[param, tap : tap + 1, :], weights)
        bias = conv_bias_ref[param : param + 1, :]
        bias_rows = jnp.zeros((part, inputs.shape[1]), F32)
        for place, piece in enumerate(split3(bias)):
            bias_rows = jnp.where(iota((part, 1), 0) == place, piece.astype(F32), bias_rows)
        products = jnp.concatenate([*split3(weights * inputs), bias_rows.astype(BF16)], axis=0)
        conved = silu(dot(select_ref[...], products))
        values = conved[:, :inner].astype(BF16)
        rest = conved[:, inner:]
        lane = iota(rest.shape, 1)
        words_ref[index, :, :inner] = values
        words_ref[index, :, inner : inner + LANES] = jnp.where(lane < state, rest, 0.0).astype(BF16)
        words_ref[index, :, inner + LANES :] = jnp.where(
            lane < state, pltpu.roll(rest, LANES - state, 1), 0.0
        ).astype(BF16)
        step_rows = jnp.concatenate([step, jnp.zeros((8, inner), F32)], axis=0)
        word_steps = dot(last_ref[...], pack_split(step_rows, 2))
        stepped_ref[index] = (values.astype(F32) * word_steps).astype(BF16)


def mixer_kernel(
    letters,
    taps,
    state,
    here_ref,
    tokens_ref,
    words_ref,
    stepped_ref,
    gates_ref,
    decay_ref,
    log_step_ref,
    skip_ref,
    narrow_decay_ref,
    narrow_step_ref,
    tall_decay_ref,
    gain_ref,
    spread_ref,
    mixed_ref,
    state_ref,
    conved_ref,
    total_ref,
):
    here = here_ref[0]
    blocks = tokens_ref.shape[0]
    rows = mixed_ref.shape[0]
    own = rows // BLOCK
    heads, inner = spread_ref.shape
    head = inner // heads
    word_rows = words_ref.shape[1]
    starts, _, _ = word_plan(letters, taps)
    first, past = here * own, (here + 1) * own

    place = iota((blocks, blocks), 1)
    place = (here ^ (place // own)) * own + place % own
    target = iota((blocks, blocks), 0)
    tokens = tokens_ref[...].astype(F32).astype(BF16)
    around = []
    for offset in (-1, 0, 1):
        pick = (place == target + offset).astype(F32).astype(BF16)
        around.append(dot(pick, tokens))
    before, middle, after = (x.astype(jnp.int32) for x in around)
    position = iota((blocks, BLOCK), 0) * BLOCK + iota((blocks, BLOCK), 1)

    def word_index(both, shifts, at_end):
        codes = jnp.zeros((blocks, BLOCK), jnp.int32)
        result = None
        scale = 1
        for back in range(taps):
            start = BLOCK if shifts > 0 else 0
            turned = both if back == 0 else pltpu.roll(both, back if shifts > 0 else 2 * BLOCK - back, 1)
            codes = codes + scale * turned[:, start : start + BLOCK]
            scale *= letters
            found = starts[back + 1] + codes
            result = found if result is None else jnp.where(at_end >= back, found, result)
        return result

    rise_index = word_index(jnp.concatenate([before, middle], axis=1), 1, position)
    fall_index = word_index(
        jnp.concatenate([middle, after], axis=1), -1, blocks * BLOCK - 1 - position
    )

    hot = [(middle == letter).astype(F32) for letter in range(letters)]
    stack = jnp.concatenate(hot, axis=0).astype(BF16)
    up = (iota((BLOCK, BLOCK), 0) <= iota((BLOCK, BLOCK), 1)).astype(F32).astype(BF16)
    running = dot(stack, up)
    block_sum = dot(stack, jnp.ones((BLOCK, BLOCK), BF16)).astype(BF16)
    col = iota((blocks, blocks), 1)
    to_rise = ((col >= target) & (col < first)).astype(F32).astype(BF16)
    to_fall = ((col >= past) & (col < target)).astype(F32).astype(BF16)
    block_of = iota((blocks, BLOCK), 0)
    counts = []
    for letter in range(letters):
        part = slice(letter * blocks, (letter + 1) * blocks)
        rise = dot(to_rise, block_sum[part]) - running[part]
        fall = dot(to_fall, block_sum[part]) + running[part] - hot[letter]
        counts.append(jnp.where(block_of < first, rise, fall))
    index = jnp.where(block_of < first, rise_index, fall_index)

    rise_tall = jnp.concatenate([tall_decay_ref[0], tall_decay_ref[1]], axis=0)
    fall_tall = jnp.concatenate([tall_decay_ref[2], tall_decay_ref[3]], axis=0)
    word = iota((word_rows, BLOCK), 0)
    word_weights = jnp.zeros((word_rows, 4 * heads), F32)
    for block in range(blocks):
        rises, falls = block < first, block >= past
        tall = jnp.where(rises, rise_tall, fall_tall)
        power = sum(counts[l][block : block + 1] * tall[:, l : l + 1] for l in range(letters))
        weight = jnp.exp2(power)
        both = jnp.concatenate(
            [jnp.where(rises, weight, 0.0), jnp.where(falls, weight, 0.0)], axis=0
        ).astype(BF16)
        match = (word == index[block : block + 1]).astype(F32).astype(BF16)
        word_weights = word_weights + dot(match, both, NT)
    word_weights = word_weights.astype(BF16)
    spread = spread_ref[...]
    pass_of = iota((4 * heads, inner), 0) // heads
    spread4 = jnp.concatenate([spread] * 4, axis=0)
    for index4 in range(4):
        spread_one = jnp.where(pass_of == index4, spread4.astype(F32), 0.0).astype(BF16)
        weighted = (dot(word_weights, spread_one) * stepped_ref[index4].astype(F32)).astype(BF16)
        entering = dot(words_ref[index4, :, inner : inner + LANES], weighted, TN)
        state_ref[index4] = entering[:state]

    own_tokens, own_match = [], []
    for part in range(own):
        is_row = block_of == first + part
        take = lambda x: jnp.sum(jnp.where(is_row, x, 0), axis=0, keepdims=True)
        own_tokens.append(take(middle))
        pair = []
        for found in (rise_index, fall_index):
            pair.append((word == take(found)).astype(F32).astype(BF16))
        own_match.append(pair)
    for part in range(own):
        for index4, (falls, strand, param) in enumerate(PASSES):
            conved_ref[index4, part * BLOCK : (part + 1) * BLOCK, :] = dot(
                own_match[part][int(falls)], words_ref[index4], TN
            ).astype(BF16)

    per_block = BLOCK // CHUNK
    chunks = rows // CHUNK
    t = iota((CHUNK, LANES), 0)
    lane = iota((CHUNK, LANES), 1)
    half = lane % CHUNK
    u_row = iota((LANES, LANES), 0)
    u_half = iota((LANES, LANES), 1) % CHUNK
    lane_row = iota((1, LANES), 1)

    def window(chunk):
        block, inside = chunk // per_block, chunk % per_block
        pair = inside // 2
        side = inside % 2
        return own_tokens[block][:, pair * LANES : (pair + 1) * LANES], side * CHUNK

    def letter_counts(chunk, falls):
        tokens_row, base = window(chunk)
        u = lane - base
        in_chunk = (u >= 0) & (u < CHUNK)
        reach = in_chunk & ((u >= t) if falls else (u <= t))
        left = jnp.concatenate(
            [jnp.where(reach & (tokens_row == l), 1.0, 0.0) for l in range(letters)], axis=0
        ).astype(BF16)
        v = u_row - base
        beyond = (v < u_half) if falls else (v > u_half)
        right = jnp.concatenate(
            [jnp.where(beyond, 1.0, 0.0), jnp.ones((LANES, LANES), F32)], axis=1
        ).astype(BF16)
        both = dot(left, right)
        between = [both[l * CHUNK : (l + 1) * CHUNK, :LANES] for l in range(letters)]
        running = [both[l * CHUNK : (l + 1) * CHUNK, LANES:] for l in range(letters)]
        return between, running

    for step in range(chunks):
        for falls in (False, True):
            chunk = chunks - 1 - step if falls else step
            at = slice(chunk * CHUNK, (chunk + 1) * CHUNK)
            between, running = letter_counts(chunk, falls)
            _, other = letter_counts(chunk, not falls)
            edge = 0 if falls else CHUNK - 1
            sums = [r[edge : edge + 1] for r in running]
            is_letter = [r + o - s for r, o, s in zip(running, other, sums)]
            tokens_row, base = window(chunk)
            turned = pltpu.roll(tokens_row, CHUNK, 1)
            doubled = jnp.where((lane_row >= base) & (lane_row < base + CHUNK), tokens_row, turned)
            hot_cols = jnp.zeros((CHUNK, LANES), F32)
            for l in range(letters):
                hot_cols = jnp.where((lane == l) | (lane == 16 + l), is_letter[l], hot_cols)
            hot_cols = hot_cols[:, :32].astype(BF16)
            causal = (half >= t) if falls else (half <= t)
            for index4, (pass_falls, strand, param) in enumerate(PASSES):
                if pass_falls != falls:
                    continue
                values = conved_ref[index4, at, :inner]
                b_rows = conved_ref[index4, at, inner : inner + LANES]
                c_rows = conved_ref[index4, at, inner + LANES :]
                scores = dot(c_rows, jnp.concatenate([b_rows, b_rows], axis=0), NT)
                scores = jnp.where(causal, scores, 0.0)
                narrow_decay = narrow_decay_ref[index4]
                narrow_log = narrow_step_ref[index4]
                width = slice(0, heads)
                power = sum(running[l][:, width] * narrow_decay[l : l + 1] for l in range(letters))
                from_start = jnp.exp2(power).astype(BF16)
                power = sum(
                    (sums[l] - running[l])[:, width] * narrow_decay[l : l + 1] for l in range(letters)
                )
                logs = jnp.zeros((CHUNK, heads), F32)
                for l in range(letters):
                    logs = jnp.where(is_letter[l][:, width] > 0.5, narrow_log[l : l + 1], logs)
                to_end = jnp.exp2(power + logs).astype(BF16)
                from_start = dot(from_start, spread)
                to_end = dot(to_end, spread)
                old = state_ref[index4]
                carried = dot(c_rows[:, :state], old.astype(BF16))
                fresh = dot(b_rows, (values.astype(F32) * to_end).astype(BF16), TN)[:state]
                outputs = []
                for group in range(inner // WIDE):
                    mixing = []
                    for tile in range(WIDE // LANES):
                        lanes = slice(
                            group * WIDE + tile * LANES, group * WIDE + (tile + 1) * LANES
                        )
                        power = log_step_ref[index4, 0:1, lanes]
                        for l in range(1, letters):
                            power = jnp.where(
                                doubled == l, log_step_ref[index4, l : l + 1, lanes], power
                            )
                        for l in range(letters):
                            power = power + between[l] * decay_ref[index4, l : l + 1, lanes]
                        mixing.append((jnp.exp2(power) * scores).astype(BF16))
                    mixing = jnp.concatenate(mixing, axis=1)
                    wide = slice(group * WIDE, (group + 1) * WIDE)
                    group_values = values[:, wide]
                    head_of = iota((CHUNK, WIDE), 1) // head
                    stacked = jnp.concatenate(
                        [
                            jnp.where(head_of == h, group_values.astype(F32), 0.0).astype(BF16)
                            for h in range(WIDE // head)
                        ],
                        axis=0,
                    )
                    inside = dot(mixing, stacked)
                    outputs.append(
                        inside
                        + carried[:, wide] * from_start[:, wide]
                        + skip_ref[index4, 0:1, wide] * group_values.astype(F32)
                    )
                total_decay = jnp.zeros((1, inner), F32)
                for l in range(letters):
                    total = jnp.concatenate([sums[l]] * (inner // LANES), axis=1)
                    total_decay = total_decay + total * decay_ref[index4, l : l + 1]
                state_ref[index4] = old * jnp.exp2(total_decay) + fresh
                gated = jnp.concatenate(outputs, axis=1) * dot(hot_cols, gates_ref[strand])
                mean = jnp.sum(gated * gated, axis=1, keepdims=True) * (1.0 / inner)
                normed = gated * lax.rsqrt(mean + EPSILON) * gain_ref[param : param + 1]
                visited = index4 in (1, 3) or 2 * step >= chunks
                if visited:
                    total_ref[at, :] += normed
                else:
                    total_ref[at, :] = normed
    mixed_ref[...] = total_ref[...].astype(BF16)


def output_kernel(masks, sides, here_ref, side_ref, mixed_ref, *refs):
    pieces = refs[: len(masks)]
    out_ref, weight_ref, sem = refs[len(masks) :]
    here, side = here_ref[0], side_ref[0]
    copies = []
    for piece, piece_masks, piece_side in zip(pieces, masks, sides):
        depth, width = piece.shape[1:]
        for k, mask in enumerate(piece_masks):
            row = pl.multiple_of((here ^ mask) * depth, depth)
            lane = pl.multiple_of((side ^ piece_side) * width, width)
            copies.append(
                pltpu.make_async_copy(
                    piece.at[k], weight_ref.at[pl.ds(row, depth), pl.ds(lane, width)], sem
                )
            )
    for copy in copies:
        copy.start()
    for copy in copies:
        copy.wait()
    out_ref[...] = dot(mixed_ref[...], weight_ref[...]).astype(BF16)


def swap(x, axis, mask):
    count = lax.axis_size(axis)
    return lax.ppermute(x, axis, [(i, i ^ mask) for i in range(count)])


def vmem():
    return pl.BlockSpec(memory_space=pltpu.VMEM)


def smem():
    return pl.BlockSpec(memory_space=pltpu.SMEM)


def on_device(
    token_ids,
    complement,
    embedding,
    in_weight,
    step_weight,
    conv_weight,
    conv_bias,
    step_bias,
    decay_rate,
    skip_gain,
    norm_gain,
    out_weight,
):
    genomes, rows = token_ids.shape
    letters, width = embedding.shape
    taps = conv_weight.shape[1]
    heads = step_weight.shape[1]
    inner = norm_gain.shape[1]
    state = (conv_weight.shape[2] - inner) // 2
    count, sides = lax.axis_size("seq"), lax.axis_size("batch")
    here = lax.axis_index("seq").astype(jnp.int32)[None]
    side = lax.axis_index("batch").astype(jnp.int32)[None]
    depth, columns = out_weight.shape

    token_rows = -(-genomes * rows // columns)
    padded_rows = -(-token_rows // 16) * 16
    flat = token_ids.astype(BF16).reshape(-1)
    flat = jnp.pad(flat, (0, padded_rows * columns - flat.shape[0]))
    load = jnp.concatenate([out_weight, flat.reshape(padded_rows, columns)], axis=0)[None]

    line = [mask for mask in range(0, count, 4)]
    lines = jnp.concatenate([load] + [swap(load, "seq", mask) for mask in line[1:]], axis=0)
    half = len(line) // 2
    from_x, from_y = swap(lines, "seq", 1), swap(lines, "seq", 2)
    corner_low = swap(from_y[:half], "seq", 1)
    corner_high = swap(from_x[half:], "seq", 2)
    pieces = [
        (lines, line),
        (from_x, [m ^ 1 for m in line]),
        (from_y, [m ^ 2 for m in line]),
        (corner_low, [m ^ 3 for m in line[:half]]),
        (corner_high, [m ^ 3 for m in line[half:]]),
    ]
    weights = jnp.concatenate([piece for piece, _ in pieces], axis=0)
    masks = [m for _, piece_masks in pieces for m in piece_masks]
    held = [weights[:, :depth]]
    held_sides = [0]
    mask = 1
    while mask < sides:
        held = held + [swap(x, "batch", mask) for x in held]
        held_sides = held_sides + [s ^ mask for s in held_sides]
        mask *= 2

    travelled = weights[:, depth:].reshape(count, -1)[:, : genomes * rows]
    order = np.argsort(masks)
    travelled = jnp.concatenate([travelled[int(k)][None] for k in order], axis=0)
    travelled = travelled.astype(jnp.int32).reshape(count, genomes, rows)

    select, last = word_select(letters, taps)
    word_rows = select.shape[0]
    spread = np.repeat(np.eye(heads, dtype=np.float32), inner // heads, axis=1).astype(
        ml_dtypes.bfloat16
    )
    table_columns = inner + 2 * LANES
    shapes = [
        ((4, word_rows, table_columns), BF16),
        ((4, word_rows, inner), BF16),
        ((2, 32, inner), BF16),
        ((4, 8, inner), F32),
        ((4, 8, inner), F32),
        ((4, 8, inner), F32),
        ((4, 8, heads), F32),
        ((4, 8, heads), F32),
        ((4, heads, LANES), F32),
    ]
    tables = pl.pallas_call(
        tables_kernel,
        out_shape=[jax.ShapeDtypeStruct(*shape) for shape in shapes],
        in_specs=[smem()] + [vmem()] * 11,
        out_specs=[vmem()] * len(shapes),
        compiler_params=pltpu.CompilerParams(vmem_limit_bytes=20 * 2**20),
        cost_estimate=pl.CostEstimate(flops=3 * 10**9, bytes_accessed=16 * 2**20, transcendentals=2**21),
        name="tables",
    )(
        complement,
        embedding,
        in_weight,
        step_weight,
        conv_weight,
        conv_bias,
        step_bias,
        decay_rate,
        skip_gain,
        select,
        last,
        spread,
    )
    results = []
    for genome in range(genomes):
        tokens = travelled[:, genome].reshape(-1, BLOCK)
        mixed = pl.pallas_call(
            partial(mixer_kernel, letters, taps, state),
            out_shape=jax.ShapeDtypeStruct((rows, inner), BF16),
            in_specs=[smem()] + [vmem()] * 12,
            out_specs=vmem(),
            scratch_shapes=[
                pltpu.VMEM((4, state, inner), F32),
                pltpu.VMEM((4, rows, table_columns), BF16),
                pltpu.VMEM((rows, inner), F32),
            ],
            compiler_params=pltpu.CompilerParams(vmem_limit_bytes=20 * 2**20),
            cost_estimate=pl.CostEstimate(
                flops=6 * 10**9, bytes_accessed=24 * 2**20, transcendentals=2**21
            ),
            name="mixer",
        )(here, tokens, *tables, norm_gain, spread)
        result = pl.pallas_call(
            partial(output_kernel, [masks] * len(held), held_sides),
            out_shape=jax.ShapeDtypeStruct((rows, columns * sides), BF16),
            in_specs=[smem(), smem(), vmem()] + [pl.BlockSpec(memory_space=pl.ANY)] * len(held),
            out_specs=vmem(),
            scratch_shapes=[
                pltpu.VMEM((depth * count, columns * sides), BF16),
                pltpu.SemaphoreType.DMA,
            ],
            compiler_params=pltpu.CompilerParams(vmem_limit_bytes=8 * 2**20),
            name="output",
        )(here, side, mixed, *held)
        results.append(result)
    return jnp.stack(results)


def solution(mesh):
    placed = (P("batch", "seq"),) + (P(),) * 10 + (P("seq", "batch"),)
    return jax.shard_map(
        on_device, mesh=mesh, in_specs=placed, out_specs=P("batch", "seq", None), check_vma=False
    )
```

time: 571 us -> 57 us (0.10); the launches traced: 564 us -> 56.6 us
  waiting for transfers between devices: 247 us -> 14.3 us
  local copies, waits for them, and re-layouts: 99.5 us -> 8.67 us
  blocking collectives: 79.8 us -> 0 us
  other arithmetic: 74.5 us -> 2.45 us
  matrix products: 41.2 us -> 0 us
  Pallas kernels: 0 us -> 20 us
  between operations: 13.8 us -> 0.49 us
    all_gather x3 -> x0, waiting for transfers between devices: 247 us -> none  [the longest x2 247 us: entering_2(): everything = jax.tree.map(lambda part: lax.all_gather(part, axis), value)]
    all_gather x3 -> x0, blocking collectives: 79.8 us -> none  [the longest x2 77.8 us: entering_2(): everything = jax.tree.map(lambda part: lax.all_gather(part, axis), value)]
    slice x17 -> x5, local copies, waits for them, and re-layouts: 63.9 us -> 0.15 us  [the longest x1 0.09 us: on_device(): held = [weights[:, :depth]]]
    select_n x32 -> x0, other arithmetic: 47.2 us -> none  [hop(): return jax.tree.map(lambda a, b: jnp.where(reached, a, b), new, before)]
    dot_general x14 -> x0, matrix products: 41.2 us -> none  [the longest x2 16 us: block_step(): inside = jnp.einsum('hts,shp->thp', mixing, values, precision=exact_mode)]
    pallas_call x0 -> x3, Pallas kernels: none -> 20 us  [the longest x1 13.8 us: on_device(): pl.pallas_call(partial(mixer_kernel, letters, taps, state), out_shape=jax...]
    ppermute x2 -> x8, waiting for transfers between devices: 0.01 us -> 14.3 us  [swap(): return lax.ppermute(x, axis, [(i, i ^ mask) for i in range(count)])]
    rev x2 -> x0, local copies, waits for them, and re-layouts: 13.9 us -> none  [the longest x1 13.7 us: direction_pass(): outputs = jnp.flip(outputs, axis=1)]
  transfers between devices with their start and end apart: 5 -> 8, of which waited for: 2 -> 4; matrix products, arithmetic and copies ran while one was open for 25% -> 4% of each run, Pallas kernels for 0% -> 32%
where the time goes in v1:
time: 57 us; the launch traced here: 56.6 us
  Pallas kernels  20 us (35%)
  waiting for transfers between devices  14.3 us (25%)
  starting transfers between devices  10.7 us (19%)
  local copies, waits for them, and re-layouts  8.67 us (15%)
  other arithmetic  2.45 us (4%)
    ppermute x8, waiting for transfers between devices, swap(): return lax.ppermute(x, axis, [(i, i ^ mask) for i in range(count)])  14.3 us
    pallas_call x1, Pallas kernels, on_device(): pl.pallas_call(partial(mixer_kernel, letters, taps, state), out_shape=jax...  13.8 us
    ppermute x8, starting transfers between devices, swap(): return lax.ppermute(x, axis, [(i, i ^ mask) for i in range(count)])  10.7 us
    unnamed x40, local copies, waits for them, and re-layouts  8.41 us
    pallas_call x1, Pallas kernels, on_device(): pl.pallas_call(tables_kernel, out_shape=[jax.ShapeDtypeStruct(*shape) for...  4.26 us
    pallas_call x1, Pallas kernels, on_device(): pl.pallas_call(partial(output_kernel, [masks] * len(held), held_sides), o...  1.97 us
  transfers between devices with their start and end apart: 8, of which 4 were waited for; matrix products, arithmetic and copies ran while one was open for 4% of the time, Pallas kernels for 32%

profile of v1, /device:TPU:0, one launch (start us, length us, event | category | flops | bytes accessed | tf_op | source)
XLA Modules:
  0.0 56.6 jit_solution(13183605175216016611)
XLA Ops:
  0.0 0.7 %convert_reduce_fusion = bf16[256]{0:T(256)(128)(2,1)S(1)} fusion(s32[1,256]{1,0:T(1,128)} %param.15), kind=kLoop, calls=%fused_computation.10 | loop fusion | flops 256 | bytes 1536 | tf_op jit(solution)/shard_map/convert_element_type | solution.py:501
  0.7 0.8 %maximum_bitcast_fusion = bf16[1,80,512]{2,1,0:T(8,128)(2,1)S(1)} fusion(bf16[16,512]{1,0:T(8,128)(2,1)S(1)} %reshape.10, bf16[64,512]{1,0:T(8,128)(2,1)} %param.26), kind=kLoop, calls=%fused_computation.1 | loop fusion | flops 163840 | bytes 163840 | tf_op jit(solution)/shard_map/broadcast_in_dim | solution.py:503
  1.6 3.0 %collective-permute-start = (bf16[1,80,512]{2,1,0:T(8,128)(2,1)S(1)}, bf16[1,80,512]{2,1,0:T(8,128)(2,1)S(1)}, u32[]{:S(2)}, u32[]{:S(2)}) collective-permute-start(bf16[1,80,512]{2,1,0:T(8,128)(2,1)S(1)} %maximum_bitcast_fusion), channel_id=1, source_target_pairs={{0,4},{1,5},{2,6},{3,7},{4,0},{5,1},{6,2},{7,3},{8,12},{9,13},{10,... | collective-permute-start | bytes 245768 | tf_op jit(solution)/shard_map/ppermute | solution.py:463
  4.6 2.6 %collective-permute-start.1 = (bf16[1,80,512]{2,1,0:T(8,128)(2,1)S(1)}, bf16[1,80,512]{2,1,0:T(8,128)(2,1)S(1)}, u32[]{:S(2)}, u32[]{:S(2)}) collective-permute-start(bf16[1,80,512]{2,1,0:T(8,128)(2,1)S(1)} %maximum_bitcast_fusion), channel_id=1, source_target_pairs={{0,8},{1,9},{2,10},{3,11},{4,12},{5,13},{6,14},{7,15},{8,0},{9,1},... | collective-permute-start | bytes 245768 | tf_op jit(solution)/shard_map/ppermute | solution.py:463
  7.2 0.0 collective-permute-start.2
  7.2 0.9 %copy.16.step_weight_ref = bf16[1024,16]{1,0:T(8,128)(2,1)S(1)} copy(bf16[1024,16]{0,1:T(8,128)(2,1)} %param.19) | data formatting | bytes 65536 | tf_op args[4]
  8.1 0.8 %constant_dynamic-update-slice_fusion.7 = bf16[16,80,512]{2,1,0:T(8,128)(2,1)S(1)} fusion(bf16[16,512]{1,0:T(8,128)(2,1)S(1)} %reshape.10, bf16[64,512]{1,0:T(8,128)(2,1)} %param.26), kind=kLoop, calls=%fused_computation.9 | loop fusion | flops 163839 | bytes 163840
  9.0 0.0 collective-permute-done
  9.0 4.8 %collective-permute-done.1 = bf16[1,80,512]{2,1,0:T(8,128)(2,1)S(1)} collective-permute-done((bf16[1,80,512]{2,1,0:T(8,128)(2,1)S(1)}, bf16[1,80,512]{2,1,0:T(8,128)(2,1)S(1)}, u32[]{:S(2)}, u32[]{:S(2)}) %collective-permute-start.1) | collective-permute-done | bytes 81952 | tf_op jit(solution)/shard_map/ppermute | solution.py:463
  13.8 0.0 collective-permute-done.2
  13.9 1.6 %collective-permute-start.3 = (bf16[4,80,512]{2,1,0:T(8,128)(2,1)S(1)}, bf16[4,80,512]{2,1,0:T(8,128)(2,1)S(1)}, u32[]{:S(2)}, u32[]{:S(2)}) collective-permute-start(bf16[4,80,512]{2,1,0:T(8,128)(2,1)S(1)} %pad_maximum_fusion), channel_id=1, source_target_pairs={{0,1},{1,0},{2,3},{3,2},{4,5},{5,4},{6,7},{7,6},{8,9},{9,8},{10,11... | collective-permute-start | bytes 983048 | tf_op jit(solution)/shard_map/ppermute | solution.py:463
  15.4 1.5 %collective-permute-start.4 = (bf16[4,80,512]{2,1,0:T(8,128)(2,1)S(1)}, bf16[4,80,512]{2,1,0:T(8,128)(2,1)S(1)}, u32[]{:S(2)}, u32[]{:S(2)}) collective-permute-start(bf16[4,80,512]{2,1,0:T(8,128)(2,1)S(1)} %pad_maximum_fusion), channel_id=1, source_target_pairs={{0,2},{1,3},{2,0},{3,1},{4,6},{5,7},{6,4},{7,5},{8,10},{9,11},{10,... | collective-permute-start | bytes 983048 | tf_op jit(solution)/shard_map/ppermute | solution.py:463
  16.9 0.0 copy-start.11
  17.0 5.9 %collective-permute-done.4 = bf16[4,80,512]{2,1,0:T(8,128)(2,1)S(1)} collective-permute-done((bf16[4,80,512]{2,1,0:T(8,128)(2,1)S(1)}, bf16[4,80,512]{2,1,0:T(8,128)(2,1)S(1)}, u32[]{:S(2)}, u32[]{:S(2)}) %collective-permute-start.4) | collective-permute-done | bytes 327712 | tf_op jit(solution)/shard_map/ppermute | solution.py:463
  22.9 0.4 collective-permute-start.5
  23.3 0.0 collective-permute-done.3
  23.3 1.6 %collective-permute-start.6 = (bf16[2,80,512]{2,1,0:T(8,128)(2,1)S(1)}, bf16[2,80,512]{2,1,0:T(8,128)(2,1)S(1)}, u32[]{:S(2)}, u32[]{:S(2)}) collective-permute-start(bf16[2,80,512]{2,1,0:T(8,128)(2,1)S(1)} %slice.98), channel_id=1, source_target_pairs={{0,2},{1,3},{2,0},{3,1},{4,6},{5,7},{6,4},{7,5},{8,10},{9,11},{10,... | collective-permute-start | bytes 491528 | tf_op jit(solution)/shard_map/ppermute | solution.py:463
  24.9 0.0 copy-start.1
  24.9 0.0 copy-start.2
  24.9 0.0 copy-start.3
  24.9 0.0 copy-start.5
  25.0 0.0 copy-start.6
  25.0 0.0 copy-start.7
  25.0 0.0 copy-start.8
  25.0 0.0 copy-start.9
  25.0 0.0 copy-start.10
  25.0 3.2 %collective-permute-done.5 = bf16[2,80,512]{2,1,0:T(8,128)(2,1)S(1)} collective-permute-done((bf16[2,80,512]{2,1,0:T(8,128)(2,1)S(1)}, bf16[2,80,512]{2,1,0:T(8,128)(2,1)S(1)}, u32[]{:S(2)}, u32[]{:S(2)}) %collective-permute-start.5) | collective-permute-done | bytes 163872 | tf_op jit(solution)/shard_map/ppermute | solution.py:463
  28.3 0.4 collective-permute-done.6
  28.7 0.1 slice.116.refs_0_
  28.8 0.0 copy-start.4
  28.8 0.1 collective-permute-start.7
  28.9 0.0 copy-done.11
  28.9 0.0 copy-done
  28.9 0.0 copy-done.1
  28.9 0.0 copy-done.2
  28.9 0.0 copy-done.3
  28.9 0.0 copy-done.5
  29.0 4.3 %tables.1 = (bf16[4,352,1280]{2,1,0:T(8,128)(2,1)S(1)}, bf16[4,352,1024]{2,1,0:T(8,128)(2,1)S(1)}, bf16[2,32,1024]{2,1,0:T(8,128)(2,1)S(1)}, f32[4,8,1024]{2,1,0...) custom-call(s32[4]{0:T(128)S(1)} %copy-done.8, ...), custom_call_target="tpu_custom_call" | custom-call | flops 3000000000 | bytes 16777216 | tf_op jit(solution)/shard_map/tables/pallas_call | solution.py:550
  33.2 0.0 copy-start.12
  33.2 1.8 %copy-done.12 = bf16[4,352,1280]{2,1,0:T(8,128)(2,1)} copy-done((bf16[4,352,1280]{2,1,0:T(8,128)(2,1)}, bf16[4,352,1280]{2,1,0:T(8,128)(2,1)S(1)}, u32[]{:S(2)}) %copy-start.12) | copy-done | bytes 3604504
  35.0 1.6 %copy-done.14 = bf16[4,352,1024]{2,1,0:T(8,128)(2,1)} copy-done((bf16[4,352,1024]{2,1,0:T(8,128)(2,1)}, bf16[4,352,1024]{2,1,0:T(8,128)(2,1)S(1)}, u32[]{:S(2)}) %copy-start.14) | copy-done | bytes 2883608
  36.6 0.2 copy.17
  36.8 0.1 concatenate.16
  36.9 2.0 %copy-done.13 = bf16[4,352,1280]{2,1,0:T(8,128)(2,1)S(1)} copy-done((bf16[4,352,1280]{2,1,0:T(8,128)(2,1)S(1)}, bf16[4,352,1280]{2,1,0:T(8,128)(2,1)}, u32[]{:S(2)}) %copy-start.13) | copy-done | bytes 3604504
  38.9 1.8 %copy-done.15 = bf16[4,352,1024]{2,1,0:T(8,128)(2,1)S(1)} copy-done((bf16[4,352,1024]{2,1,0:T(8,128)(2,1)S(1)}, bf16[4,352,1024]{2,1,0:T(8,128)(2,1)}, u32[]{:S(2)}) %copy-start.15) | copy-done | bytes 2883608
  40.7 13.8 %mixer.1.mixed_ref = bf16[256,1024]{1,0:T(8,128)(2,1)S(1)} custom-call(s32[1]{0:T(128)} %bitcast.here_ref, s32[16,256]{1,0:T(8,128)S(1)} %convert_element_type.9.tokens_ref, bf16[4,352,1280]{2,1,0:T(8,128)(2,1)S(1)} %copy-done.13, bf16[4,352,1024]{2,1,0:T(8,128)(2,1)S(1)} %copy-done.15, bf16[2,32,1024]{2,1,0:T(8,128)(2,1)S(1)} %get-tuple-element.16.gates_ref, ...), custom_call_target="tpu_custom_call" | custom-call | flops 6000000000 | bytes 25165824 | tf_op jit(solution)/shard_map/mixer/pallas_call | solution.py:575
  54.5 0.0 collective-permute-done.7.refs_1_
  54.5 2.0 %output.1 = bf16[256,1024]{1,0:T(8,128)(2,1)} custom-call(s32[1]{0:T(128)} %bitcast.here_ref, s32[1]{0:T(128)} %bitcast.1.side_ref, bf16[256,1024]{1,0:T(8,128)(2,1)S(1)} %mixer.1.mixed_ref, bf16[16,64,512]{2,1,0:T(8,128)(2,1)S(1)} %slice.116.refs_0_, bf16[16,64,512]{2,1,0:T(8,128)(2,1)S(1)} %collective-permute-done.7.refs_1_), custom_call_target="tpu_custom_call" | custom-call | tf_op jit(solution)/shard_map/output/pallas_call | solution.py:591
  (25 shorter events, 0.3 us)
Async XLA Ops:
  1.6 7.4 %collective-permute-start = (bf16[1,80,512]{2,1,0:T(8,128)(2,1)S(1)}, bf16[1,80,512]{2,1,0:T(8,128)(2,1)S(1)}, u32[]{:S(2)}, u32[]{:S(2)}) collective-permute-start(bf16[1,80,512]{2,1,0:T(8,128)(2,1)S(1)} %maximum_bitcast_fusion), channel_id=1, source_target_pairs={{0,4},{1,5},{2,6},{3,7},{4,0},{5,1},{6,2},{7,3},{8,12},{9,13},{10,... | collective-permute-start | bytes 245768 | tf_op jit(solution)/shard_map/ppermute | solution.py:463
  4.6 9.2 %collective-permute-start.1 = (bf16[1,80,512]{2,1,0:T(8,128)(2,1)S(1)}, bf16[1,80,512]{2,1,0:T(8,128)(2,1)S(1)}, u32[]{:S(2)}, u32[]{:S(2)}) collective-permute-start(bf16[1,80,512]{2,1,0:T(8,128)(2,1)S(1)} %maximum_bitcast_fusion), channel_id=1, source_target_pairs={{0,8},{1,9},{2,10},{3,11},{4,12},{5,13},{6,14},{7,15},{8,0},{9,1},... | collective-permute-start | bytes 245768 | tf_op jit(solution)/shard_map/ppermute | solution.py:463
  7.2 6.6 %collective-permute-start.2 = (bf16[1,80,512]{2,1,0:T(8,128)(2,1)S(1)}, bf16[1,80,512]{2,1,0:T(8,128)(2,1)S(1)}, u32[]{:S(2)}, u32[]{:S(2)}) collective-permute-start(bf16[1,80,512]{2,1,0:T(8,128)(2,1)S(1)} %maximum_bitcast_fusion), channel_id=1, source_target_pairs={{0,12},{1,13},{2,14},{3,15},{4,8},{5,9},{6,10},{7,11},{8,4},{9,5},... | collective-permute-start | bytes 245768 | tf_op jit(solution)/shard_map/ppermute | solution.py:463
  13.9 9.4 %collective-permute-start.3 = (bf16[4,80,512]{2,1,0:T(8,128)(2,1)S(1)}, bf16[4,80,512]{2,1,0:T(8,128)(2,1)S(1)}, u32[]{:S(2)}, u32[]{:S(2)}) collective-permute-start(bf16[4,80,512]{2,1,0:T(8,128)(2,1)S(1)} %pad_maximum_fusion), channel_id=1, source_target_pairs={{0,1},{1,0},{2,3},{3,2},{4,5},{5,4},{6,7},{7,6},{8,9},{9,8},{10,11... | collective-permute-start | bytes 983048 | tf_op jit(solution)/shard_map/ppermute | solution.py:463
  15.4 7.5 %collective-permute-start.4 = (bf16[4,80,512]{2,1,0:T(8,128)(2,1)S(1)}, bf16[4,80,512]{2,1,0:T(8,128)(2,1)S(1)}, u32[]{:S(2)}, u32[]{:S(2)}) collective-permute-start(bf16[4,80,512]{2,1,0:T(8,128)(2,1)S(1)} %pad_maximum_fusion), channel_id=1, source_target_pairs={{0,2},{1,3},{2,0},{3,1},{4,6},{5,7},{6,4},{7,5},{8,10},{9,11},{10,... | collective-permute-start | bytes 983048 | tf_op jit(solution)/shard_map/ppermute | solution.py:463
  16.9 11.9 %copy-start.11 = (bf16[16,1024]{1,0:T(8,128)(2,1)S(1)}, bf16[16,1024]{1,0:T(8,128)(2,1)}, u32[]{:S(2)}) copy-start(bf16[16,1024]{1,0:T(8,128)(2,1)} %constant.20.clone.spread_ref) | copy-start | bytes 98308
  22.9 6.0 %copy-start = (bf16[1024,2176]{1,0:T(8,128)(2,1)S(1)}, bf16[1024,2176]{1,0:T(8,128)(2,1)}, u32[]{:S(2)}) copy-start(bf16[1024,2176]{1,0:T(8,128)(2,1)} %in_weight_ref.1) | copy-start | bytes 13369348
  22.9 5.4 %collective-permute-start.5 = (bf16[2,80,512]{2,1,0:T(8,128)(2,1)S(1)}, bf16[2,80,512]{2,1,0:T(8,128)(2,1)S(1)}, u32[]{:S(2)}, u32[]{:S(2)}) collective-permute-start(bf16[2,80,512]{2,1,0:T(8,128)(2,1)S(1)} %slice.97), channel_id=1, source_target_pairs={{0,1},{1,0},{2,3},{3,2},{4,5},{5,4},{6,7},{7,6},{8,9},{9,8},{10,11... | collective-permute-start | bytes 491528 | tf_op jit(solution)/shard_map/ppermute | solution.py:463
  23.3 5.4 %collective-permute-start.6 = (bf16[2,80,512]{2,1,0:T(8,128)(2,1)S(1)}, bf16[2,80,512]{2,1,0:T(8,128)(2,1)S(1)}, u32[]{:S(2)}, u32[]{:S(2)}) collective-permute-start(bf16[2,80,512]{2,1,0:T(8,128)(2,1)S(1)} %slice.98), channel_id=1, source_target_pairs={{0,2},{1,3},{2,0},{3,1},{4,6},{5,7},{6,4},{7,5},{8,10},{9,11},{10,... | collective-permute-start | bytes 491528 | tf_op jit(solution)/shard_map/ppermute | solution.py:463
  24.9 4.0 %copy-start.1 = (f32[2,4,1152]{2,1,0:T(4,128)S(1)}, f32[2,4,1152]{2,1,0:T(4,128)}, u32[]{:S(2)}) copy-start(f32[2,4,1152]{2,1,0:T(4,128)} %conv_weight_ref.1) | copy-start | bytes 110596
  24.9 4.0 %copy-start.2 = (f32[2,1152]{1,0:T(2,128)S(1)}, f32[2,1152]{1,0:T(2,128)}, u32[]{:S(2)}) copy-start(f32[2,1152]{1,0:T(2,128)} %conv_bias_ref.1) | copy-start | bytes 27652
  24.9 4.0 %copy-start.3 = (bf16[4,1024]{1,0:T(4,128)(2,1)S(1)}, bf16[4,1024]{1,0:T(4,128)(2,1)}, u32[]{:S(2)}) copy-start(bf16[4,1024]{1,0:T(4,128)(2,1)} %embedding_ref.1) | copy-start | bytes 24580
  24.9 4.0 %copy-start.5 = (f32[2,16]{1,0:T(2,128)S(1)}, f32[2,16]{1,0:T(2,128)}, u32[]{:S(2)}) copy-start(f32[2,16]{1,0:T(2,128)} %step_bias_ref.1) | copy-start | bytes 388
  25.0 4.0 %copy-start.6 = (f32[2,16]{1,0:T(2,128)S(1)}, f32[2,16]{1,0:T(2,128)}, u32[]{:S(2)}) copy-start(f32[2,16]{1,0:T(2,128)} %rate_ref.1) | copy-start | bytes 388
  25.0 4.0 %copy-start.7 = (f32[2,16]{1,0:T(2,128)S(1)}, f32[2,16]{1,0:T(2,128)}, u32[]{:S(2)}) copy-start(f32[2,16]{1,0:T(2,128)} %skip_ref.1) | copy-start | bytes 388
  25.0 4.0 %copy-start.8 = (s32[4]{0:T(128)S(1)}, s32[4]{0:T(128)}, u32[]{:S(2)}) copy-start(s32[4]{0:T(128)} %complement_ref.1) | copy-start | bytes 52
  25.0 4.0 %copy-start.9 = (bf16[352,64]{1,0:T(8,128)(2,1)S(1)}, bf16[352,64]{1,0:T(8,128)(2,1)}, u32[]{:S(2)}) copy-start(bf16[352,64]{1,0:T(8,128)(2,1)} %constant.18.clone.select_ref) | copy-start | bytes 135172
  25.0 3.9 %copy-start.10 = (bf16[352,32]{1,0:T(8,128)(2,1)S(1)}, bf16[352,32]{1,0:T(8,128)(2,1)}, u32[]{:S(2)}) copy-start(bf16[352,32]{1,0:T(8,128)(2,1)} %constant.19.clone.last_ref) | copy-start | bytes 67588
  28.8 8.1 %copy-start.4 = (f32[2,1024]{1,0:T(2,128)S(1)}, f32[2,1024]{1,0:T(2,128)}, u32[]{:S(2)}) copy-start(f32[2,1024]{1,0:T(2,128)} %gain_ref.1) | copy-start | bytes 24580
  28.8 25.7 %collective-permute-start.7 = (bf16[16,64,512]{2,1,0:T(8,128)(2,1)S(1)}, bf16[16,64,512]{2,1,0:T(8,128)(2,1)S(1)}, u32[]{:S(2)}, u32[]{:S(2)}) collective-permute-start(bf16[16,64,512]{2,1,0:T(8,128)(2,1)S(1)} %slice.116.refs_0_), channel_id=1, source_target_pairs={{0,16},{16,0},{1,17},{17,1},{2,18},{18,2},{3,19},{19,3},{4,20},{20... | collective-permute-start | bytes 3145736 | tf_op jit(solution)/shard_map/ppermute | solution.py:463
  33.2 1.8 %copy-start.12 = (bf16[4,352,1280]{2,1,0:T(8,128)(2,1)}, bf16[4,352,1280]{2,1,0:T(8,128)(2,1)S(1)}, u32[]{:S(2)}) copy-start(bf16[4,352,1280]{2,1,0:T(8,128)(2,1)S(1)} %get-tuple-element.14.words_ref) | copy-start | bytes 10813444
  35.0 1.6 %copy-start.14 = (bf16[4,352,1024]{2,1,0:T(8,128)(2,1)}, bf16[4,352,1024]{2,1,0:T(8,128)(2,1)S(1)}, u32[]{:S(2)}) copy-start(bf16[4,352,1024]{2,1,0:T(8,128)(2,1)S(1)} %get-tuple-element.15.stepped_ref) | copy-start | bytes 8650756
  36.9 2.0 %copy-start.13 = (bf16[4,352,1280]{2,1,0:T(8,128)(2,1)S(1)}, bf16[4,352,1280]{2,1,0:T(8,128)(2,1)}, u32[]{:S(2)}) copy-start(bf16[4,352,1280]{2,1,0:T(8,128)(2,1)} %copy-done.12) | copy-start | bytes 10813444
  38.9 1.8 %copy-start.15 = (bf16[4,352,1024]{2,1,0:T(8,128)(2,1)S(1)}, bf16[4,352,1024]{2,1,0:T(8,128)(2,1)}, u32[]{:S(2)}) copy-start(bf16[4,352,1024]{2,1,0:T(8,128)(2,1)} %copy-done.14) | copy-start | bytes 8650756

commit v2 on v0

v2 whole, which is shorter than its diff:
```python
from functools import partial

import jax
import jax.numpy as jnp
import ml_dtypes
import numpy as np
from jax import lax
from jax.experimental import pallas as pl
from jax.experimental.pallas import tpu as pltpu
from jax.sharding import PartitionSpec as P

BLOCK = 256
CHUNK = 64
LANES = 128
WIDE = 256
LOG2E = 1.4426950408889634
EPSILON = 1e-05
VMEM_BYTES = 64 * 2**20
F32 = jnp.float32
BF16 = jnp.bfloat16

TN = (((0,), (0,)), ((), ()))
NT = (((1,), (1,)), ((), ()))
NN = (((1,), (0,)), ((), ()))


def dot(a, b, dims=NN):
    return lax.dot_general(a, b, dims, preferred_element_type=F32)


def iota(shape, dim):
    return lax.broadcasted_iota(jnp.int32, shape, dim)


def split3(x):
    high = x.astype(BF16)
    rest = x - high.astype(F32)
    middle = rest.astype(BF16)
    low = (rest - middle.astype(F32)).astype(BF16)
    return high, middle, low


def silu(x):
    return x / (1.0 + jnp.exp(-x))


def word_plan(letters, taps):
    starts = {taps: 0}
    rows = letters**taps
    for length in range(taps - 1, 0, -1):
        starts[length] = rows
        rows += letters**length
    return starts, rows, -(-rows // 32) * 32


def word_letters(letters, taps):
    starts, rows, padded = word_plan(letters, taps)
    table = np.full((padded, taps), -1, np.int64)
    for length, start in starts.items():
        codes = np.arange(letters**length)
        for back in range(length):
            table[start : start + letters**length, taps - 1 - back] = codes // letters**back % letters
    return table


def word_select(letters, taps):
    table = word_letters(letters, taps)
    part = -(-letters * taps // 16) * 16
    select = np.zeros((table.shape[0], 4 * part), np.float32)
    for tap in range(taps):
        rows = np.nonzero(table[:, tap] >= 0)[0]
        for copy in range(3):
            select[rows, copy * part + tap * letters + table[rows, tap]] = 1
    select[:, 3 * part : 3 * part + 3] = 1
    last = np.zeros((table.shape[0], 32), np.float32)
    rows = np.nonzero(table[:, taps - 1] >= 0)[0]
    for copy in range(2):
        last[rows, copy * 16 + table[rows, taps - 1]] = 1
    return select.astype(ml_dtypes.bfloat16), last.astype(ml_dtypes.bfloat16)


PASSES = ((False, 0, 0), (False, 1, 1), (True, 0, 1), (True, 1, 0))


def letter_rows(table, letters, rows, complement):
    row = iota((rows, 1), 0) % letters
    picked = row
    if complement is not None:
        picked = jnp.zeros_like(row)
        for letter in range(letters):
            picked = jnp.where(row == letter, complement(letter), picked)
    result = jnp.broadcast_to(table[0:1], (rows, table.shape[1]))
    for letter in range(1, letters):
        result = jnp.where(picked == letter, table[letter : letter + 1], result)
    return result


def pack_split(x, copies):
    return jnp.concatenate(split3(x)[:copies], axis=0)


def start_all(pairs, sems):
    copies = [
        pltpu.make_async_copy(source, target, sems.at[k]) for k, (source, target) in enumerate(pairs)
    ]
    for copy in copies:
        copy.start()
    return copies


def word_index(both, start, size, falls, starts, taps, letters, before_end):
    lanes = both.shape[1]
    codes, result, scale = None, None, 1
    for back in range(taps):
        turned = both if back == 0 else pltpu.roll(both, lanes - back if falls else back, 1)
        part = scale * turned[:, start : start + size]
        codes = part if codes is None else codes + part
        scale *= letters
        found = starts[back + 1] + codes
        result = found if result is None else jnp.where(before_end >= back, found, result)
    return result


def spread_rows(spread, index, count):
    heads = spread.shape[0]
    stacked = jnp.concatenate([spread] * count, axis=0)
    return jnp.where(iota(stacked.shape, 0) // heads == index, stacked, jnp.zeros_like(stacked))


def mixer_kernel(
    letters,
    taps,
    state,
    count,
    here_ref,
    complement_ref,
    tokens_hbm,
    spread_hbm,
    embedding_hbm,
    step_weight_hbm,
    step_bias_hbm,
    rate_hbm,
    skip_hbm,
    last_hbm,
    select_hbm,
    conv_weight_hbm,
    conv_bias_hbm,
    gain_hbm,
    in_weight_hbm,
    mixed_hbm,
    tokens_ref,
    spread_ref,
    embedding_ref,
    step_weight_ref,
    step_bias_ref,
    rate_ref,
    skip_ref,
    last_ref,
    select_ref,
    conv_weight_ref,
    conv_bias_ref,
    gain_ref,
    in_weight_ref,
    mixed_ref,
    words_ref,
    gates_ref,
    coefs_ref,
    exponent_ref,
    match_ref,
    weight_ref,
    base_ref,
    gated_ref,
    in_sems,
    out_sem,
):
    reads = start_all(
        (
            (tokens_hbm, tokens_ref),
            (spread_hbm, spread_ref),
            (embedding_hbm, embedding_ref),
            (step_weight_hbm, step_weight_ref),
            (step_bias_hbm, step_bias_ref),
            (rate_hbm, rate_ref),
            (skip_hbm, skip_ref),
            (last_hbm, last_ref),
            (select_hbm, select_ref),
            (conv_weight_hbm, conv_weight_ref),
            (conv_bias_hbm, conv_bias_ref),
            (gain_hbm, gain_ref),
            (in_weight_hbm, in_weight_ref),
        ),
        in_sems,
    )
    here = here_ref[0]
    rows = tokens_ref.shape[1]
    own = rows // BLOCK
    blocks = count * own
    heads, inner = spread_ref.shape
    head = inner // heads
    word_rows = select_ref.shape[0]
    part_rows = select_ref.shape[1] // 4
    starts, _, _ = word_plan(letters, taps)
    first, past = here * own, (here + 1) * own
    chunks = BLOCK // CHUNK
    as_bf16 = lambda mask: jnp.where(mask, 1.0, 0.0).astype(BF16)
    complement = lambda letter: complement_ref[letter]

    reads[0].wait()
    tokens16 = tokens_ref[...].astype(F32).astype(BF16)
    source, target = iota((blocks, count), 1) ^ here, iota((blocks, count), 0)
    around = jnp.zeros((3 * blocks, BLOCK), F32)
    for part in range(own):
        block = source * own + part
        pick = jnp.concatenate([as_bf16(block == target + k) for k in (-1, 0, 1)], axis=0)
        around = around + dot(pick, tokens16[:, part * BLOCK : (part + 1) * BLOCK])
    around = around.astype(jnp.int32)
    before, middle, after = (around[k * blocks : (k + 1) * blocks] for k in range(3))
    position = iota((blocks, BLOCK), 0) * BLOCK + iota((blocks, BLOCK), 1)
    rise_index = word_index(
        jnp.concatenate([before, middle], axis=1), BLOCK, BLOCK, False, starts, taps, letters, position
    )
    fall_index = word_index(
        jnp.concatenate([middle, after], axis=1),
        0,
        BLOCK,
        True,
        starts,
        taps,
        letters,
        blocks * BLOCK - 1 - position,
    )
    block_of = iota((blocks, BLOCK), 0)
    middle_word = word_rows // 2
    word = (iota((word_rows, BLOCK), 0) - middle_word).astype(F32).astype(BF16)
    index = jnp.where(block_of < first, rise_index, fall_index) - middle_word
    index = index.astype(F32).astype(BF16)
    one, zero = jnp.ones((), BF16), jnp.zeros((), BF16)
    for block in range(blocks):
        match_ref[:, block * BLOCK : (block + 1) * BLOCK] = jnp.where(
            word == index[block : block + 1], one, zero
        )

    letter_hot = [jnp.where(middle == letter, 1.0, 0.0) for letter in range(letters)]
    stack = jnp.concatenate(letter_hot, axis=0).astype(BF16)
    t = iota((BLOCK, BLOCK), 0)
    u = iota((BLOCK, BLOCK), 1)
    sums = dot(stack, jnp.concatenate([as_bf16(t <= u), jnp.ones((BLOCK, BLOCK), BF16)], axis=1))
    running, block_sum = sums[:, :BLOCK], sums[:, BLOCK:].astype(BF16)
    col, row = iota((blocks, blocks), 1), iota((blocks, blocks), 0)
    to_rise = as_bf16((col >= row) & (col < first))
    to_fall = as_bf16((col >= past) & (col < row))
    both_ways = jnp.concatenate([to_rise, to_fall], axis=0)
    counts = []
    for letter in range(letters):
        part = slice(letter * blocks, (letter + 1) * blocks)
        far = dot(both_ways, block_sum[part])
        rise = far[:blocks] - running[part]
        fall = far[blocks:] + running[part] - letter_hot[letter]
        counts.append(jnp.where(block_of < first, rise, fall))

    same = (t // CHUNK) == (u // CHUNK)
    until, since = as_bf16(same & (u <= t)), as_bf16(same & (u >= t))
    half = iota((BLOCK, LANES), 1) % CHUNK
    inside_row = iota((BLOCK, LANES), 0) % CHUNK
    lane = iota((BLOCK, LANES), 1)
    hot_lane = jnp.where(lane < 48, (lane % 16).astype(F32), -1.0)
    word_lane = iota((BLOCK, word_rows), 1).astype(F32)
    small_half = iota((CHUNK, LANES), 1) % CHUNK
    small_row = iota((CHUNK, LANES), 0)
    small_lane = iota((CHUNK, LANES), 1)
    row_lane = iota((1, LANES), 1)
    beyond = (as_bf16(inside_row > half), as_bf16(inside_row < half))
    row8 = iota((8, BLOCK), 0)
    prepared = []
    for part in range(own):
        mine = block_of == first + part
        take = lambda x: jnp.sum(jnp.where(mine, x, 0), axis=0, keepdims=True)
        token_row = take(middle).astype(F32)
        facts = jnp.where(row8 == 0, take(rise_index), take(fall_index)).astype(F32)
        facts = jnp.where(row8 == 2, token_row, facts)
        facts = jnp.concatenate([facts, jnp.zeros((LANES - 8, BLOCK), F32)], axis=0).T
        matches = [
            jnp.where(word_lane == facts[:, d : d + 1], 1.0, 0.0).astype(BF16) for d in range(2)
        ]
        hot = jnp.where(hot_lane == facts[:, 2:3], 1.0, 0.0)
        hot16 = hot.astype(BF16)
        tallies = dot(jnp.concatenate([until, since], axis=0), hot16)
        hot_rows = [jnp.where(token_row == l, 1.0, 0.0) for l in range(letters)]
        between = []
        for d, reach in enumerate((until, since)):
            left = jnp.concatenate([reach * h.astype(BF16) for h in hot_rows], axis=0)
            between.append(dot(left, beyond[d]))
        totals = jnp.concatenate(
            [jnp.where(u[:1] // CHUNK == i, h, 0.0) for i in range(chunks) for h in hot_rows],
            axis=0,
        ).astype(BF16)
        totals = dot(totals, jnp.ones((BLOCK, LANES), BF16))
        doubled = []
        for i in range(chunks):
            window = token_row[:, (i // 2) * LANES : (i // 2 + 1) * LANES]
            keep = (row_lane // CHUNK) == i % 2
            doubled.append(jnp.where(keep, window, pltpu.roll(window, CHUNK, 1)))
        prepared.append((matches, hot, hot16, tallies, between, totals, doubled))

    for copy in reads[1:8]:
        copy.wait()
    spread = spread_ref[...]
    width = embedding_ref.shape[1]
    embedding = jnp.concatenate(
        [embedding_ref[...], jnp.zeros((16 - letters, width), BF16)], axis=0
    )
    raw = dot(embedding, step_weight_ref[...], NT)

    def widen(x):
        return sum(dot(piece, spread) for piece in split3(x))

    row = iota((16, heads), 0)
    vectors = jnp.zeros((16, heads), F32)
    for k in range(2):
        vectors = jnp.where(row == k, step_bias_ref[k : k + 1, :], vectors)
        vectors = jnp.where(row == 2 + k, rate_ref[k : k + 1, :], vectors)
        vectors = jnp.where(row == 4 + k, skip_ref[k : k + 1, :], vectors)
    wide_both = widen(jnp.concatenate([raw, vectors], axis=0))
    wide_raw, wide_vectors = wide_both[:16], wide_both[16:]

    def step_tables(raw_rows, vector_rows, strand, param):
        rows8 = letter_rows(raw_rows, letters, 8, complement if strand else None)
        shifted = rows8 + vector_rows[param : param + 1]
        step = jnp.maximum(shifted, 0.0) + jnp.log1p(jnp.exp(-jnp.abs(shifted)))
        decay = -vector_rows[2 + param : 3 + param] * step * LOG2E
        return step, decay, jnp.log2(step)

    lane8 = iota((8, LANES), 1)
    exponents = [jnp.zeros((8, LANES), F32)] * 3
    talls = []
    for index4, (falls, strand, param) in enumerate(PASSES):
        _, decay, log_step = step_tables(wide_raw, wide_vectors, strand, param)
        coefs_ref[index4, 0:8] = decay
        coefs_ref[index4, 8:16] = log_step
        coefs_ref[index4, 16:24] = jnp.broadcast_to(wide_vectors[4 + param : 5 + param], (8, inner))
        step, decay, log_step = step_tables(raw, vectors, strand, param)
        for place, narrow in enumerate((decay, log_step, step)):
            wide = jnp.concatenate([narrow, jnp.zeros((8, LANES - heads), F32)], axis=1)
            wide = pltpu.roll(wide, index4 * heads, 1) if index4 else wide
            mine = (lane8 >= index4 * heads) & (lane8 < (index4 + 1) * heads)
            exponents[place] = jnp.where(mine, wide, exponents[place])
    only = iota((8, LANES), 0) < letters
    tall = jnp.concatenate([exponents[0], jnp.zeros((LANES - 8, LANES), F32)], axis=0).T
    exponents = [
        jnp.concatenate([jnp.where(only, x, 0.0), jnp.zeros((8, LANES), F32)], axis=0)
        for x in exponents
    ]
    for place in range(2):
        rest = jnp.zeros((LANES - 48, LANES), BF16)
        exponent_ref[place] = jnp.concatenate([*split3(exponents[place]), rest], axis=0)
    word_steps = dot(last_ref[...], pack_split(exponents[2], 2))

    talls = [
        [
            jnp.broadcast_to(tall[k * 2 * heads : (k + 1) * 2 * heads, l : l + 1], (2 * heads, BLOCK))
            for l in range(letters)
        ]
        for k in range(2)
    ]
    for block in range(blocks):
        rises, falls = block < first, block >= past
        power = sum(
            counts[l][block : block + 1] * jnp.where(rises, talls[0][l], talls[1][l])
            for l in range(letters)
        )
        weight = jnp.exp2(power)
        lanes = slice(block * BLOCK, (block + 1) * BLOCK)
        weight_ref[: 2 * heads, lanes] = jnp.where(rises, weight, 0.0).astype(BF16)
        weight_ref[2 * heads :, lanes] = jnp.where(falls, weight, 0.0).astype(BF16)
    word_weights = dot(match_ref[...], weight_ref[...], NT)
    word_weights = (word_weights * word_steps[:, : 4 * heads]).astype(BF16)

    narrows = []
    for matches, hot, hot16, tallies, between, totals, doubled in prepared:
        up, down = tallies[:BLOCK], tallies[BLOCK:]
        powers = dot(
            jnp.concatenate([up, down, down - hot, up - hot], axis=0).astype(BF16), exponent_ref[0]
        )
        power = lambda k: powers[k * BLOCK : (k + 1) * BLOCK]
        rising = lane < 2 * heads
        from_start = jnp.exp2(jnp.where(rising, power(0), power(1)))
        steps = dot(hot16, exponent_ref[1])
        to_end = jnp.exp2(jnp.where(rising, power(2), power(3)) + steps)
        narrows.append(
            jnp.concatenate([from_start, to_end], axis=0).astype(BF16)[:, : 4 * heads]
        )

    for copy in reads[8:]:
        copy.wait()
    projected = dot(embedding, in_weight_ref[...]).astype(BF16).astype(F32)
    gate = silu(projected[:, :inner])
    for strand in range(2):
        gate_rows = letter_rows(gate, letters, 16, complement if strand else None)
        gate_rows = jnp.where(iota((16, 1), 0) < letters, gate_rows, 0.0)
        gates_ref[strand] = pack_split(gate_rows, 2)

    block_chunk = t // CHUNK
    lane_chunk = u // CHUNK
    head_of = iota((CHUNK, WIDE), 1) // head
    head_masks = [as_bf16(head_of == h) for h in range(WIDE // head)]
    scales = []
    for index4, (falls, strand, param) in enumerate(PASSES):
        d = int(falls)
        inputs = letter_rows(
            projected[:, inner:], letters, part_rows, complement if strand else None
        )
        tap_row = iota((part_rows, 1), 0) // letters
        weights = jnp.zeros((part_rows, inputs.shape[1]), F32)
        for tap in range(taps):
            weights = jnp.where(tap_row == tap, conv_weight_ref[param, tap : tap + 1, :], weights)
        bias_rows = jnp.zeros((part_rows, inputs.shape[1]), F32)
        for place, piece in enumerate(split3(conv_bias_ref[param : param + 1, :])):
            bias_rows = jnp.where(iota((part_rows, 1), 0) == place, piece.astype(F32), bias_rows)
        products = jnp.concatenate([*split3(weights * inputs), bias_rows.astype(BF16)], axis=0)
        conved = silu(dot(select_ref[...], products))
        words_ref[:, :inner] = conved[:, :inner].astype(BF16)
        rest = conved[:, inner:]
        rest_lane = iota(rest.shape, 1)
        words_ref[:, inner : inner + LANES] = jnp.where(
            rest_lane < state, pltpu.roll(rest, LANES - state, 1), 0.0
        ).astype(BF16)
        turned = rest.T[:state].astype(BF16)
        to_lanes = spread_rows(spread, index4, 4)
        weighted = (dot(word_weights, to_lanes) * conved[:, :inner]).astype(BF16)
        held = dot(turned, weighted)

        decay = [coefs_ref[index4, l : l + 1] for l in range(letters)]
        log_step = [coefs_ref[index4, 8 + l : 9 + l] for l in range(letters)]
        skip = coefs_ref[index4, 16:17]
        squares = []
        for part in range(own - 1, -1, -1) if falls else range(own):
            matches, _, hot16, _, between, totals, doubled = prepared[part]
            match, at = matches[d], part * BLOCK
            order = range(chunks - 1, -1, -1) if falls else range(chunks)
            bt = dot(turned, match, NT)
            c_rows = dot(match, words_ref[:, inner : inner + LANES])
            values = dot(match, words_ref[:, :inner])
            spreads = dot(narrows[part], to_lanes)
            all_scores = dot(c_rows.astype(BF16)[:, :state], bt.astype(BF16))
            bt_lane = iota(bt.shape, 1) // CHUNK
            bt_chunks = jnp.concatenate(
                [jnp.where(bt_lane == i, bt, 0.0).astype(BF16) for i in range(chunks)], axis=0
            )
            fresh = dot(bt_chunks, (values * spreads[BLOCK:]).astype(BF16))
            values16 = values.astype(BF16)
            scores = []
            for i in range(chunks):
                lanes = slice((i // 2) * LANES, (i // 2 + 1) * LANES)
                window = all_scores[i * CHUNK : (i + 1) * CHUNK, lanes]
                keep = (small_lane // CHUNK) == i % 2
                both = jnp.where(keep, window, pltpu.roll(window, CHUNK, 1))
                causal = (small_half >= small_row) if falls else (small_half <= small_row)
                scores.append(jnp.where(causal, both, 0.0))
            entering = [None] * chunks
            for i in order:
                entering[i] = held.astype(BF16)
                power_sum = jnp.zeros((1, inner), F32)
                for l in range(letters):
                    row = totals[i * letters + l : i * letters + l + 1]
                    row = jnp.concatenate([row] * (inner // LANES), axis=1)
                    power_sum = power_sum + row * decay[l]
                held = fresh[i * state : (i + 1) * state] + held * jnp.exp2(power_sum)
            twice = c_rows + pltpu.roll(c_rows, state, 1)
            c_chunks = jnp.concatenate([twice] * (chunks * state // LANES), axis=1)
            c_chunks = jnp.where(block_chunk == lane_chunk, c_chunks, 0.0).astype(BF16)
            carried = dot(c_chunks, jnp.concatenate(entering, axis=0))
            base_ref[...] = carried * spreads[:BLOCK] + skip * values
            square = [None] * chunks
            for group in range(inner // WIDE):
                wide = slice(group * WIDE, (group + 1) * WIDE)
                mixed, stacked = [], []
                for i in range(chunks):
                    mixing = []
                    for tile in range(WIDE // LANES):
                        low = group * WIDE + tile * LANES
                        lanes = slice(low, low + LANES)
                        total = log_step[0][:, lanes]
                        for l in range(1, letters):
                            total = jnp.where(doubled[i] == l, log_step[l][:, lanes], total)
                        for l in range(letters):
                            apart = between[d][l * BLOCK + i * CHUNK : l * BLOCK + (i + 1) * CHUNK]
                            total = total + apart * decay[l][:, lanes]
                        mixing.append((jnp.exp2(total) * scores[i]).astype(BF16))
                    mixed.append(jnp.concatenate(mixing, axis=1))
                    chunk_values = values16[i * CHUNK : (i + 1) * CHUNK, wide]
                    stacked.append(
                        jnp.concatenate([chunk_values * mask for mask in head_masks], axis=0)
                    )
                inside = [dot(m, v) for m, v in zip(mixed, stacked)]
                gate = dot(hot16[:, :32], gates_ref[strand, :, wide])
                for i in range(chunks):
                    chunk = slice(i * CHUNK, (i + 1) * CHUNK)
                    gated = (inside[i] + base_ref[chunk, wide]) * gate[chunk]
                    gated_ref[index4, at + i * CHUNK : at + (i + 1) * CHUNK, wide] = gated
                    part_sum = jnp.sum(gated * gated, axis=1, keepdims=True)
                    square[i] = part_sum if square[i] is None else square[i] + part_sum
            squares.append(jnp.concatenate(square, axis=0))
        squares = squares[::-1] if falls else squares
        scales.append(lax.rsqrt(jnp.concatenate(squares, axis=0) * (1.0 / inner) + EPSILON))
    for group in range(inner // WIDE):
        wide = slice(group * WIDE, (group + 1) * WIDE)
        total = None
        for index4, (falls, strand, param) in enumerate(PASSES):
            normed = gated_ref[index4, :, wide] * scales[index4] * gain_ref[param : param + 1, wide]
            total = normed if total is None else total + normed
        mixed_ref[:, wide] = total.astype(BF16)
    copy = pltpu.make_async_copy(mixed_ref, mixed_hbm, out_sem)
    copy.start()
    copy.wait()


def output_kernel(depth, places, here_ref, mixed_hbm, *refs):
    pieces = refs[: len(places)]
    out_ref, weight_ref, mixed_ref, sem = refs[len(places) :]
    here = here_ref[0]
    pairs = [(mixed_hbm, mixed_ref)]
    for piece, masks in zip(pieces, places):
        for k, mask in enumerate(masks):
            row = pl.multiple_of((here ^ mask) * depth, depth)
            pairs.append((piece.at[k], weight_ref.at[pl.ds(row, depth)]))
    for copy in start_all(pairs, sem):
        copy.wait()
    out_ref[...] = dot(mixed_ref[...], weight_ref[...]).astype(BF16)


def swap(x, axis, mask):
    count = lax.axis_size(axis)
    return lax.ppermute(x, axis, [(i, i ^ mask) for i in range(count)])


def vmem():
    return pl.BlockSpec(memory_space=pltpu.VMEM)


def hbm():
    return pl.BlockSpec(memory_space=pltpu.HBM)


def smem():
    return pl.BlockSpec(memory_space=pltpu.SMEM)


def on_device(
    token_ids,
    complement,
    embedding,
    in_weight,
    step_weight,
    conv_weight,
    conv_bias,
    step_bias,
    decay_rate,
    skip_gain,
    norm_gain,
    out_weight,
):
    genomes, rows = token_ids.shape
    letters, width = embedding.shape
    taps = conv_weight.shape[1]
    heads = step_weight.shape[1]
    inner = norm_gain.shape[1]
    state = (conv_weight.shape[2] - inner) // 2
    count, sides = lax.axis_size("seq"), lax.axis_size("batch")
    here = lax.axis_index("seq").astype(jnp.int32)[None]
    side = lax.axis_index("batch").astype(jnp.int32)[None]
    depth, columns = out_weight.shape

    bits = [1 << k for k in range(count.bit_length() - 1)]
    join = lambda *x: jnp.concatenate(x, axis=0)
    moved = lambda masks, mask: [m ^ mask for m in masks]
    tokens, token_bits = token_ids[None], list(bits)
    line, line_masks = out_weight[None], [0]
    for mask in bits[:1:-1]:
        arrived = swap(line, "seq", mask)
        if token_bits:
            tokens = join(tokens, swap(tokens, "seq", token_bits.pop(0)))
        line = join(line, arrived)
        line_masks = line_masks + moved(line_masks, mask)
        line, tokens = lax.optimization_barrier((line, tokens))
    while token_bits:
        tokens = join(tokens, swap(tokens, "seq", token_bits.pop(0)))
    across_plane = [swap(line, "seq", mask) for mask in (1, 2, 3)]
    places = [line_masks] + [moved(line_masks, mask) for mask in (1, 2, 3)]

    select, last = word_select(letters, taps)
    word_rows = select.shape[0]
    spread = np.repeat(np.eye(heads, dtype=np.float32), inner // heads, axis=1).astype(
        ml_dtypes.bfloat16
    )
    mixed = []
    for genome in range(genomes):
        inputs = (
            tokens[:, genome],
            spread,
            embedding,
            step_weight.T,
            step_bias,
            decay_rate,
            skip_gain,
            last,
            select,
            conv_weight,
            conv_bias,
            norm_gain,
            in_weight,
        )
        mixed.append(
            pl.pallas_call(
                partial(mixer_kernel, letters, taps, state, count),
                out_shape=jax.ShapeDtypeStruct((rows, inner), BF16),
                in_specs=[smem(), smem()] + [hbm()] * len(inputs),
                out_specs=hbm(),
                scratch_shapes=[pltpu.VMEM(x.shape, x.dtype) for x in inputs]
                + [
                    pltpu.VMEM((rows, inner), BF16),
                    pltpu.VMEM((word_rows, inner + LANES), BF16),
                    pltpu.VMEM((2, 32, inner), BF16),
                    pltpu.VMEM((4, 24, inner), F32),
                    pltpu.VMEM((2, LANES, LANES), BF16),
                    pltpu.VMEM((word_rows, count * rows), BF16),
                    pltpu.VMEM((4 * heads, count * rows), BF16),
                    pltpu.VMEM((BLOCK, inner), F32),
                    pltpu.VMEM((4, rows, inner), F32),
                    pltpu.SemaphoreType.DMA((len(inputs),)),
                    pltpu.SemaphoreType.DMA,
                ],
                compiler_params=pltpu.CompilerParams(vmem_limit_bytes=VMEM_BYTES),
                cost_estimate=pl.CostEstimate(
                    flops=10**10, bytes_accessed=50 * 2**20, transcendentals=2**22
                ),
                name="mixer",
            )(here, complement, *inputs)
        )
    line, across_plane, mixed = lax.optimization_barrier((line, across_plane, mixed))
    pieces = [line, *across_plane]
    sets = [(pieces, 0)]
    mask = 1
    while mask < sides:
        sets = sets + [([swap(x, "batch", mask) for x in found], s ^ mask) for found, s in sets]
        mask *= 2

    def project(found, mixed):
        return pl.pallas_call(
            partial(output_kernel, depth, places),
            out_shape=jax.ShapeDtypeStruct((rows, columns), BF16),
            in_specs=[smem()] + [hbm()] * (1 + len(found)),
            out_specs=vmem(),
            scratch_shapes=[
                pltpu.VMEM((depth * count, columns), BF16),
                pltpu.VMEM((rows, inner), BF16),
                pltpu.SemaphoreType.DMA((count + 1,)),
            ],
            compiler_params=pltpu.CompilerParams(vmem_limit_bytes=16 * 2**20),
            cost_estimate=pl.CostEstimate(
                flops=2 * rows * inner * columns, bytes_accessed=2**22, transcendentals=0
            ),
            name="output",
        )(here, mixed, *found)

    results = []
    for genome in range(genomes):
        parts = [project(found, mixed[genome]) for found, _ in sets]
        ordered = []
        for k in range(sides):
            chosen = parts[0]
            for part, (_, part_side) in zip(parts, sets):
                chosen = jnp.where((side[0] ^ part_side) == k, part, chosen)
            ordered.append(chosen)
        results.append(jnp.concatenate(ordered, axis=1))
    return jnp.stack(results)


def solution(mesh):
    placed = (P("batch", "seq"),) + (P(),) * 10 + (P("seq", "batch"),)
    return jax.shard_map(
        on_device, mesh=mesh, in_specs=placed, out_specs=P("batch", "seq", None), check_vma=False
    )
```

time: 571 us -> 51 us (0.09); the launches traced: 564 us -> 50.8 us
  waiting for transfers between devices: 247 us -> 6.91 us
  local copies, waits for them, and re-layouts: 99.5 us -> 1.04 us
  blocking collectives: 79.8 us -> 0 us
  other arithmetic: 74.5 us -> 3.8 us
  matrix products: 41.2 us -> 0 us
  Pallas kernels: 0 us -> 21.6 us
  between operations: 13.8 us -> 0.11 us
  starting transfers between devices: 6.83 us -> 17.3 us
    all_gather x3 -> x0, waiting for transfers between devices: 247 us -> none  [the longest x2 247 us: entering_2(): everything = jax.tree.map(lambda part: lax.all_gather(part, axis), value)]
    all_gather x3 -> x0, blocking collectives: 79.8 us -> none  [the longest x2 77.8 us: entering_2(): everything = jax.tree.map(lambda part: lax.all_gather(part, axis), value)]
    slice x17 -> x0, local copies, waits for them, and re-layouts: 63.9 us -> none  [the longest x4 62 us: direction_pass(): window[:, offset:offset + local_len].astype(jnp.float32)]
    select_n x32 -> x1, other arithmetic: 47.2 us -> 0.05 us  [on_device(): chosen = jnp.where(side[0] ^ part_side == k, part, chosen)]
    dot_general x14 -> x0, matrix products: 41.2 us -> none  [the longest x2 16 us: block_step(): inside = jnp.einsum('hts,shp->thp', mixing, values, precision=exact_mode)]
    pallas_call x0 -> x3, Pallas kernels: none -> 21.6 us  [the longest x1 17.6 us: on_device(): pl.pallas_call(partial(mixer_kernel, letters, taps, state, count), out_sh...]
    rev x2 -> x0, local copies, waits for them, and re-layouts: 13.9 us -> none  [the longest x1 13.7 us: direction_pass(): outputs = jnp.flip(outputs, axis=1)]
    convert_element_type x4 -> x0, other arithmetic: 10.9 us -> none  [the longest x2 7.65 us: direction_pass(): conved = jax.nn.silu(conv_total).astype(jnp.bfloat16)]
  transfers between devices with their start and end apart: 5 -> 13, of which waited for: 2 -> 4; matrix products, arithmetic and copies ran while one was open for 25% -> 3% of each run, Pallas kernels for 0% -> 38%
where the time goes in v2:
time: 51 us; the launch traced here: 50.8 us
  Pallas kernels  21.6 us (42%)
  starting transfers between devices  17.3 us (34%)
  waiting for transfers between devices  6.91 us (14%)
  other arithmetic  3.8 us (7%)
  local copies, waits for them, and re-layouts  1.04 us (2%)
    pallas_call x1, Pallas kernels, on_device(): pl.pallas_call(partial(mixer_kernel, letters, taps, state, count), out_sh...  17.6 us
    ppermute x13, starting transfers between devices, swap(): return lax.ppermute(x, axis, [(i, i ^ mask) for i in range(count)])  17.3 us
    ppermute x13, waiting for transfers between devices, swap(): return lax.ppermute(x, axis, [(i, i ^ mask) for i in range(count)])  6.91 us
    pallas_call x2, Pallas kernels, project(): pl.pallas_call(partial(output_kernel, depth, places), out_shape=jax.Shape...  3.97 us
    concatenate x5, other arithmetic, on_device(): join = lambda *x: jnp.concatenate(x, axis=0)  2.28 us
    unnamed x2, local copies, waits for them, and re-layouts  1.04 us
  transfers between devices with their start and end apart: 13, of which 4 were waited for; matrix products, arithmetic and copies ran while one was open for 3% of the time, Pallas kernels for 38%

profile of v2, /device:TPU:0, one launch (start us, length us, event | category | flops | bytes accessed | tf_op | source)
XLA Modules:
  0.0 50.8 jit_solution(10594043224195286301)
XLA Ops:
  0.0 2.9 %collective-permute-start.1 = (s32[1,1,256]{2,0,1:T(1,128)}, s32[1,1,256]{2,0,1:T(1,128)S(1)}, u32[]{:S(2)}, u32[]{:S(2)}) collective-permute-start(s32[1,1,256]{2,0,1:T(1,128)} %bitcast.10), channel_id=1, source_target_pairs={{0,1},{1,0},{2,3},{3,2},{4,5},{5,4},{6,7},{7,6},{8,9},{9,8},{10,11... | collective-permute-start | bytes 3080 | tf_op jit(solution)/shard_map/ppermute | solution.py:533
  2.9 2.6 %collective-permute-start = (bf16[1,64,512]{2,1,0:T(8,128)(2,1)}, bf16[1,64,512]{2,1,0:T(8,128)(2,1)S(1)}, u32[]{:S(2)}, u32[]{:S(2)}) collective-permute-start(bf16[1,64,512]{2,1,0:T(8,128)(2,1)} %bitcast.8), channel_id=1, source_target_pairs={{0,8},{1,9},{2,10},{3,11},{4,12},{5,13},{6,14},{7,15},{8,0},{9,1},... | collective-permute-start | bytes 196616 | tf_op jit(solution)/shard_map/ppermute | solution.py:533
  5.5 0.0 collective-permute-done.1
  5.5 0.7 %pad_add_fusion.2 = s32[2,1,256]{2,0,1:T(2,128)S(1)} fusion(s32[1,1,256]{2,0,1:T(1,128)S(1)} %collective-permute-done.1, s32[1,1,256]{2,0,1:T(1,128)} %bitcast.11), kind=kLoop, calls=%fused_computation.8 | loop fusion | flops 512 | bytes 4096 | tf_op jit(solution)/shard_map/concatenate | solution.py:574
  6.2 2.4 %collective-permute-done = bf16[1,64,512]{2,1,0:T(8,128)(2,1)S(1)} collective-permute-done((bf16[1,64,512]{2,1,0:T(8,128)(2,1)}, bf16[1,64,512]{2,1,0:T(8,128)(2,1)S(1)}, u32[]{:S(2)}, u32[]{:S(2)}) %collective-permute-start) | collective-permute-done | bytes 65568 | tf_op jit(solution)/shard_map/ppermute | solution.py:533
  8.6 0.9 %pad_maximum_fusion.1 = bf16[2,64,512]{2,1,0:T(8,128)(2,1)S(1)} fusion(bf16[1,64,512]{2,1,0:T(8,128)(2,1)S(1)} %collective-permute-done, bf16[1,64,512]{2,1,0:T(8,128)(2,1)} %bitcast.9), kind=kLoop, calls=%fused_computation.4 | loop fusion | flops 65536 | bytes 262144 | tf_op jit(solution)/shard_map/concatenate | solution.py:574
  9.5 1.3 %collective-permute-start.2 = (bf16[2,64,512]{2,1,0:T(8,128)(2,1)S(1)}, bf16[2,64,512]{2,1,0:T(8,128)(2,1)S(1)}, u32[]{:S(2)}, u32[]{:S(2)}) collective-permute-start(bf16[2,64,512]{2,1,0:T(8,128)(2,1)S(1)} %pad_maximum_fusion.1), channel_id=1, source_target_pairs={{0,4},{1,5},{2,6},{3,7},{4,0},{5,1},{6,2},{7,3},{8,12},{9,13},{10,... | collective-permute-start | bytes 393224 | tf_op jit(solution)/shard_map/ppermute | solution.py:533
  10.8 1.5 %collective-permute-start.3 = (s32[2,1,256]{2,0,1:T(2,128)S(1)}, s32[2,1,256]{2,0,1:T(2,128)S(1)}, u32[]{:S(2)}, u32[]{:S(2)}) collective-permute-start(s32[2,1,256]{2,0,1:T(2,128)S(1)} %pad_add_fusion.2), channel_id=1, source_target_pairs={{0,2},{1,3},{2,0},{3,1},{4,6},{5,7},{6,4},{7,5},{8,10},{9,11},{10,... | collective-permute-start | bytes 6152 | tf_op jit(solution)/shard_map/ppermute | solution.py:533
  12.3 2.1 %collective-permute-done.3 = s32[2,1,256]{2,0,1:T(2,128)S(1)} collective-permute-done((s32[2,1,256]{2,0,1:T(2,128)S(1)}, s32[2,1,256]{2,0,1:T(2,128)S(1)}, u32[]{:S(2)}, u32[]{:S(2)}) %collective-permute-start.3) | collective-permute-done | bytes 2080 | tf_op jit(solution)/shard_map/ppermute | solution.py:533
  14.4 0.1 collective-permute-done.2
  14.5 0.7 %pad_maximum_fusion.refs_0_ = bf16[4,64,512]{2,1,0:T(8,128)(2,1)} fusion(bf16[2,64,512]{2,1,0:T(8,128)(2,1)S(1)} %collective-permute-done.2, bf16[2,64,512]{2,1,0:T(8,128)(2,1)S(1)} %pad_maximum_fusion.1), kind=kLoop, calls=%fused_computation.1 | loop fusion | flops 131072 | bytes 524288 | tf_op jit(solution)/shard_map/concatenate | solution.py:574
  15.2 1.3 %collective-permute-start.7 = (s32[4,1,256]{2,0,1:T(4,128)S(1)}, s32[4,1,256]{2,0,1:T(4,128)S(1)}, u32[]{:S(2)}, u32[]{:S(2)}) collective-permute-start(s32[4,1,256]{2,0,1:T(4,128)S(1)} %pad_add_fusion.1), channel_id=1, source_target_pairs={{0,4},{1,5},{2,6},{3,7},{4,0},{5,1},{6,2},{7,3},{8,12},{9,13},{10,... | collective-permute-start | bytes 12296 | tf_op jit(solution)/shard_map/ppermute | solution.py:533
  16.5 2.3 %collective-permute-done.7 = s32[4,1,256]{2,0,1:T(4,128)S(1)} collective-permute-done((s32[4,1,256]{2,0,1:T(4,128)S(1)}, s32[4,1,256]{2,0,1:T(4,128)S(1)}, u32[]{:S(2)}, u32[]{:S(2)}) %collective-permute-start.7) | collective-permute-done | bytes 4128 | tf_op jit(solution)/shard_map/ppermute | solution.py:533
  18.9 3.1 %collective-permute-start.8 = (s32[8,1,256]{2,0,1:T(8,128)S(1)}, s32[8,1,256]{2,0,1:T(8,128)S(1)}, u32[]{:S(2)}, u32[]{:S(2)}) collective-permute-start(s32[8,1,256]{2,0,1:T(8,128)S(1)} %pad_add_fusion), channel_id=1, source_target_pairs={{0,8},{1,9},{2,10},{3,11},{4,12},{5,13},{6,14},{7,15},{8,0},{9,1},... | collective-permute-start | bytes 24584 | tf_op jit(solution)/shard_map/ppermute | solution.py:533
  21.9 0.5 %collective-permute-start.4 = (bf16[4,64,512]{2,1,0:T(8,128)(2,1)}, bf16[4,64,512]{2,1,0:T(8,128)(2,1)}, u32[]{:S(2)}, u32[]{:S(2)}) collective-permute-start(bf16[4,64,512]{2,1,0:T(8,128)(2,1)} %pad_maximum_fusion.refs_0_), channel_id=1, source_target_pairs={{0,1},{1,0},{2,3},{3,2},{4,5},{5,4},{6,7},{7,6},{8,9},{9,8},{10,11... | collective-permute-start | bytes 786440 | tf_op jit(solution)/shard_map/ppermute | solution.py:533
  22.5 1.5 %collective-permute-start.5 = (bf16[4,64,512]{2,1,0:T(8,128)(2,1)}, bf16[4,64,512]{2,1,0:T(8,128)(2,1)}, u32[]{:S(2)}, u32[]{:S(2)}) collective-permute-start(bf16[4,64,512]{2,1,0:T(8,128)(2,1)} %pad_maximum_fusion.refs_0_), channel_id=1, source_target_pairs={{0,2},{1,3},{2,0},{3,1},{4,6},{5,7},{6,4},{7,5},{8,10},{9,11},{10,... | collective-permute-start | bytes 786440 | tf_op jit(solution)/shard_map/ppermute | solution.py:533
  24.0 1.4 %collective-permute-start.6 = (bf16[4,64,512]{2,1,0:T(8,128)(2,1)}, bf16[4,64,512]{2,1,0:T(8,128)(2,1)}, u32[]{:S(2)}, u32[]{:S(2)}) collective-permute-start(bf16[4,64,512]{2,1,0:T(8,128)(2,1)} %pad_maximum_fusion.refs_0_), channel_id=1, source_target_pairs={{0,3},{1,2},{2,1},{3,0},{4,7},{5,6},{6,5},{7,4},{8,11},{9,10},{10,... | collective-permute-start | bytes 786440 | tf_op jit(solution)/shard_map/ppermute | solution.py:533
  25.4 0.0 collective-permute-done.8
  25.4 0.6 %add_bitcast_fusion.tokens_hbm = s32[16,256]{1,0:T(8,128)} fusion(s32[8,1,256]{2,0,1:T(8,128)S(1)} %collective-permute-done.8, s32[4,1,256]{2,0,1:T(4,128)S(1)} %collective-permute-done.7, s32[4,1,256]{2,0,1:T(4,128)S(1)} %pad_add_fusion.1), kind=kLoop, calls=%fused_computation.5 | loop fusion | flops 8192 | bytes 32768 | tf_op jit(solution)/shard_map/squeeze | solution.py:598
  26.0 17.6 %mixer.1.mixed_hbm = bf16[256,1024]{1,0:T(8,128)(2,1)} custom-call(s32[1]{0:T(128)} %bitcast.here_ref, s32[4]{0:T(128)} %complement_ref.1, s32[16,256]{1,0:T(8,128)} %add_bitcast_fusion.tokens_hbm, bf16[16,1024]{1,0:T(8,128)(2,1)} %constant.19.clone.spread_hbm, bf16[4,1024]{1,0:T(4,128)(2,1)} %embedding_hbm.1, bf16[16,1024]{1,0:T(8,128)(2,1)} %bitcast.12, ...), custom_call_target="tpu_custom_call" | custom-call | flops 10000000000 | bytes 52428800 | tf_op jit(solution)/shard_map/mixer/pallas_call | solution.py:613
  43.6 0.0 collective-permute-done.4.refs_1_
  43.7 0.0 collective-permute-done.5.refs_2_
  43.7 0.0 collective-permute-done.6.refs_3_
  43.7 0.1 collective-permute-start.10
  43.8 0.5 collective-permute-start.11
  44.3 0.1 collective-permute-start.12
  44.3 0.4 collective-permute-start.9
  44.8 0.0 copy-start
  44.8 1.0 %copy-done = bf16[256,1024]{1,0:T(8,128)(2,1)S(1)} copy-done((bf16[256,1024]{1,0:T(8,128)(2,1)S(1)}, bf16[256,1024]{1,0:T(8,128)(2,1)}, u32[]{:S(2)}) %copy-start) | copy-done | bytes 524312
  45.8 1.9 %output.3 = bf16[256,512]{1,0:T(8,128)(2,1)S(1)} custom-call(s32[1]{0:T(128)} %bitcast.here_ref, bf16[256,1024]{1,0:T(8,128)(2,1)S(1)} %copy-done, bf16[4,64,512]{2,1,0:T(8,128)(2,1)} %pad_maximum_fusion.refs_0_, bf16[4,64,512]{2,1,0:T(8,128)(2,1)} %collective-permute-done.4.refs_1_, bf16[4,64,512]{2,1,0:T(8,128)(2,1)} %collective-permute-done.5.refs_2_, ...), custom_call_target="tpu_custom_call" | custom-call | flops 268435456 | bytes 4194304 | tf_op jit(solution)/shard_map/output/pallas_call | solution.py:648
  47.7 0.0 collective-permute-done.10.refs_1_
  47.7 0.0 collective-permute-done.11.refs_2_
  47.7 0.0 collective-permute-done.12.refs_3_
  47.7 0.0 collective-permute-done.9.refs_0_
  47.7 2.1 %output.2 = bf16[256,512]{1,0:T(8,128)(2,1)S(1)} custom-call(s32[1]{0:T(128)} %bitcast.here_ref, bf16[256,1024]{1,0:T(8,128)(2,1)S(1)} %copy-done, bf16[4,64,512]{2,1,0:T(8,128)(2,1)S(1)} %collective-permute-done.9.refs_0_, bf16[4,64,512]{2,1,0:T(8,128)(2,1)S(1)} %collective-permute-done.10.refs_1_, bf16[4,64,512]{2,1,0:T(8,128)(2,1)S(1)} %collective-permute-done.11.refs_2_, ...), custom_call_target="tpu_custom_call" | custom-call | flops 268435456 | bytes 4194304 | tf_op jit(solution)/shard_map/output/pallas_call | solution.py:648
  49.9 0.9 %maximum_bitcast_fusion = bf16[1,256,1024]{2,1,0:T(8,128)(2,1)} fusion(bf16[256,512]{1,0:T(8,128)(2,1)S(1)} %get-tuple-element.24, bf16[256,512]{1,0:T(8,128)(2,1)S(1)} %get-tuple-element.23), kind=kLoop, calls=%fused_computation | loop fusion | flops 1048576 | bytes 1048576 | tf_op jit(solution)/shard_map/stack | solution.py:675
  (3 shorter events, 0.1 us)
Async XLA Ops:
  0.0 5.5 %collective-permute-start.1 = (s32[1,1,256]{2,0,1:T(1,128)}, s32[1,1,256]{2,0,1:T(1,128)S(1)}, u32[]{:S(2)}, u32[]{:S(2)}) collective-permute-start(s32[1,1,256]{2,0,1:T(1,128)} %bitcast.10), channel_id=1, source_target_pairs={{0,1},{1,0},{2,3},{3,2},{4,5},{5,4},{6,7},{7,6},{8,9},{9,8},{10,11... | collective-permute-start | bytes 3080 | tf_op jit(solution)/shard_map/ppermute | solution.py:533
  2.9 5.7 %collective-permute-start = (bf16[1,64,512]{2,1,0:T(8,128)(2,1)}, bf16[1,64,512]{2,1,0:T(8,128)(2,1)S(1)}, u32[]{:S(2)}, u32[]{:S(2)}) collective-permute-start(bf16[1,64,512]{2,1,0:T(8,128)(2,1)} %bitcast.8), channel_id=1, source_target_pairs={{0,8},{1,9},{2,10},{3,11},{4,12},{5,13},{6,14},{7,15},{8,0},{9,1},... | collective-permute-start | bytes 196616 | tf_op jit(solution)/shard_map/ppermute | solution.py:533
  9.5 5.0 %collective-permute-start.2 = (bf16[2,64,512]{2,1,0:T(8,128)(2,1)S(1)}, bf16[2,64,512]{2,1,0:T(8,128)(2,1)S(1)}, u32[]{:S(2)}, u32[]{:S(2)}) collective-permute-start(bf16[2,64,512]{2,1,0:T(8,128)(2,1)S(1)} %pad_maximum_fusion.1), channel_id=1, source_target_pairs={{0,4},{1,5},{2,6},{3,7},{4,0},{5,1},{6,2},{7,3},{8,12},{9,13},{10,... | collective-permute-start | bytes 393224 | tf_op jit(solution)/shard_map/ppermute | solution.py:533
  10.8 3.6 %collective-permute-start.3 = (s32[2,1,256]{2,0,1:T(2,128)S(1)}, s32[2,1,256]{2,0,1:T(2,128)S(1)}, u32[]{:S(2)}, u32[]{:S(2)}) collective-permute-start(s32[2,1,256]{2,0,1:T(2,128)S(1)} %pad_add_fusion.2), channel_id=1, source_target_pairs={{0,2},{1,3},{2,0},{3,1},{4,6},{5,7},{6,4},{7,5},{8,10},{9,11},{10,... | collective-permute-start | bytes 6152 | tf_op jit(solution)/shard_map/ppermute | solution.py:533
  15.2 3.6 %collective-permute-start.7 = (s32[4,1,256]{2,0,1:T(4,128)S(1)}, s32[4,1,256]{2,0,1:T(4,128)S(1)}, u32[]{:S(2)}, u32[]{:S(2)}) collective-permute-start(s32[4,1,256]{2,0,1:T(4,128)S(1)} %pad_add_fusion.1), channel_id=1, source_target_pairs={{0,4},{1,5},{2,6},{3,7},{4,0},{5,1},{6,2},{7,3},{8,12},{9,13},{10,... | collective-permute-start | bytes 12296 | tf_op jit(solution)/shard_map/ppermute | solution.py:533
  18.9 6.6 %collective-permute-start.8 = (s32[8,1,256]{2,0,1:T(8,128)S(1)}, s32[8,1,256]{2,0,1:T(8,128)S(1)}, u32[]{:S(2)}, u32[]{:S(2)}) collective-permute-start(s32[8,1,256]{2,0,1:T(8,128)S(1)} %pad_add_fusion), channel_id=1, source_target_pairs={{0,8},{1,9},{2,10},{3,11},{4,12},{5,13},{6,14},{7,15},{8,0},{9,1},... | collective-permute-start | bytes 24584 | tf_op jit(solution)/shard_map/ppermute | solution.py:533
  21.9 21.7 %collective-permute-start.4 = (bf16[4,64,512]{2,1,0:T(8,128)(2,1)}, bf16[4,64,512]{2,1,0:T(8,128)(2,1)}, u32[]{:S(2)}, u32[]{:S(2)}) collective-permute-start(bf16[4,64,512]{2,1,0:T(8,128)(2,1)} %pad_maximum_fusion.refs_0_), channel_id=1, source_target_pairs={{0,1},{1,0},{2,3},{3,2},{4,5},{5,4},{6,7},{7,6},{8,9},{9,8},{10,11... | collective-permute-start | bytes 786440 | tf_op jit(solution)/shard_map/ppermute | solution.py:533
  22.5 21.2 %collective-permute-start.5 = (bf16[4,64,512]{2,1,0:T(8,128)(2,1)}, bf16[4,64,512]{2,1,0:T(8,128)(2,1)}, u32[]{:S(2)}, u32[]{:S(2)}) collective-permute-start(bf16[4,64,512]{2,1,0:T(8,128)(2,1)} %pad_maximum_fusion.refs_0_), channel_id=1, source_target_pairs={{0,2},{1,3},{2,0},{3,1},{4,6},{5,7},{6,4},{7,5},{8,10},{9,11},{10,... | collective-permute-start | bytes 786440 | tf_op jit(solution)/shard_map/ppermute | solution.py:533
  24.0 19.7 %collective-permute-start.6 = (bf16[4,64,512]{2,1,0:T(8,128)(2,1)}, bf16[4,64,512]{2,1,0:T(8,128)(2,1)}, u32[]{:S(2)}, u32[]{:S(2)}) collective-permute-start(bf16[4,64,512]{2,1,0:T(8,128)(2,1)} %pad_maximum_fusion.refs_0_), channel_id=1, source_target_pairs={{0,3},{1,2},{2,1},{3,0},{4,7},{5,6},{6,5},{7,4},{8,11},{9,10},{10,... | collective-permute-start | bytes 786440 | tf_op jit(solution)/shard_map/ppermute | solution.py:533
  43.7 4.0 %collective-permute-start.10 = (bf16[4,64,512]{2,1,0:T(8,128)(2,1)}, bf16[4,64,512]{2,1,0:T(8,128)(2,1)S(1)}, u32[]{:S(2)}, u32[]{:S(2)}) collective-permute-start(bf16[4,64,512]{2,1,0:T(8,128)(2,1)} %collective-permute-done.4.refs_1_), channel_id=1, source_target_pairs={{0,16},{16,0},{1,17},{17,1},{2,18},{18,2},{3,19},{19,3},{4,20},{20... | collective-permute-start | bytes 786440 | tf_op jit(solution)/shard_map/ppermute | solution.py:533
  43.8 3.9 %collective-permute-start.11 = (bf16[4,64,512]{2,1,0:T(8,128)(2,1)}, bf16[4,64,512]{2,1,0:T(8,128)(2,1)S(1)}, u32[]{:S(2)}, u32[]{:S(2)}) collective-permute-start(bf16[4,64,512]{2,1,0:T(8,128)(2,1)} %collective-permute-done.5.refs_2_), channel_id=1, source_target_pairs={{0,16},{16,0},{1,17},{17,1},{2,18},{18,2},{3,19},{19,3},{4,20},{20... | collective-permute-start | bytes 786440 | tf_op jit(solution)/shard_map/ppermute | solution.py:533
  44.3 3.4 %collective-permute-start.12 = (bf16[4,64,512]{2,1,0:T(8,128)(2,1)}, bf16[4,64,512]{2,1,0:T(8,128)(2,1)S(1)}, u32[]{:S(2)}, u32[]{:S(2)}) collective-permute-start(bf16[4,64,512]{2,1,0:T(8,128)(2,1)} %collective-permute-done.6.refs_3_), channel_id=1, source_target_pairs={{0,16},{16,0},{1,17},{17,1},{2,18},{18,2},{3,19},{19,3},{4,20},{20... | collective-permute-start | bytes 786440 | tf_op jit(solution)/shard_map/ppermute | solution.py:533
  44.3 3.4 %collective-permute-start.9 = (bf16[4,64,512]{2,1,0:T(8,128)(2,1)}, bf16[4,64,512]{2,1,0:T(8,128)(2,1)S(1)}, u32[]{:S(2)}, u32[]{:S(2)}) collective-permute-start(bf16[4,64,512]{2,1,0:T(8,128)(2,1)} %pad_maximum_fusion.refs_0_), channel_id=1, source_target_pairs={{0,16},{16,0},{1,17},{17,1},{2,18},{18,2},{3,19},{19,3},{4,20},{20... | collective-permute-start | bytes 786440 | tf_op jit(solution)/shard_map/ppermute | solution.py:533
  44.8 1.0 %copy-start = (bf16[256,1024]{1,0:T(8,128)(2,1)S(1)}, bf16[256,1024]{1,0:T(8,128)(2,1)}, u32[]{:S(2)}) copy-start(bf16[256,1024]{1,0:T(8,128)(2,1)} %mixer.1.mixed_hbm) | copy-start | bytes 1572868

commit v3 on v2

--- a/solution.py
+++ b/solution.py
@@ -44,38 +44,18 @@
     return x / (1.0 + jnp.exp(-x))
 
 
-def word_plan(letters, taps):
-    starts = {taps: 0}
-    rows = letters**taps
-    for length in range(taps - 1, 0, -1):
-        starts[length] = rows
-        rows += letters**length
-    return starts, rows, -(-rows // 32) * 32
-
-
-def word_letters(letters, taps):
-    starts, rows, padded = word_plan(letters, taps)
-    table = np.full((padded, taps), -1, np.int64)
-    for length, start in starts.items():
-        codes = np.arange(letters**length)
-        for back in range(length):
-            table[start : start + letters**length, taps - 1 - back] = codes // letters**back % letters
-    return table
-
-
 def word_select(letters, taps):
-    table = word_letters(letters, taps)
     part = -(-letters * taps // 16) * 16
-    select = np.zeros((table.shape[0], 4 * part), np.float32)
-    for tap in range(taps):
-        rows = np.nonzero(table[:, tap] >= 0)[0]
+    codes = np.arange(letters**taps)
+    select = np.zeros((len(codes), 4 * part), np.float32)
+    last = np.zeros((len(codes), 32), np.float32)
+    for back in range(taps):
+        letter = codes // letters**back % letters
         for copy in range(3):
-            select[rows, copy * part + tap * letters + table[rows, tap]] = 1
+            select[codes, copy * part + (taps - 1 - back) * letters + letter] = 1
     select[:, 3 * part : 3 * part + 3] = 1
-    last = np.zeros((table.shape[0], 32), np.float32)
-    rows = np.nonzero(table[:, taps - 1] >= 0)[0]
     for copy in range(2):
-        last[rows, copy * 16 + table[rows, taps - 1]] = 1
+        last[codes, copy * 16 + codes % letters] = 1
     return select.astype(ml_dtypes.bfloat16), last.astype(ml_dtypes.bfloat16)
 
 
@@ -108,17 +88,34 @@
     return copies
 
 
-def word_index(both, start, size, falls, starts, taps, letters, before_end):
+def word_index(both, start, size, falls, taps, letters, before_end):
     lanes = both.shape[1]
-    codes, result, scale = None, None, 1
+    codes, scale = None, 1
     for back in range(taps):
         turned = both if back == 0 else pltpu.roll(both, lanes - back if falls else back, 1)
         part = scale * turned[:, start : start + size]
         codes = part if codes is None else codes + part
         scale *= letters
-        found = starts[back + 1] + codes
-        result = found if result is None else jnp.where(before_end >= back, found, result)
-    return result
+    return jnp.where(before_end < taps - 1, scale + before_end, codes)
+
+
+def first_words(tokens, letters, taps, part, width):
+    row, col = iota((16, width), 0), iota((16, width), 1)
+    inner_col = col % part
+    found = (col >= 3 * part) & (col < 3 * part + 3)
+    for length in range(1, taps):
+        for back in range(length):
+            want = (taps - 1 - back) * letters + tokens[length - 1 - back]
+            found = found | ((row == length - 1) & (col < 3 * part) & (inner_col == want))
+    return jnp.where(found & (row < taps - 1), 1.0, 0.0).astype(BF16)
+
+
+def first_last(tokens, letters, taps):
+    row, col = iota((16, 32), 0), iota((16, 32), 1) % 16
+    found = jnp.zeros((16, 32), jnp.bool_)
+    for length in range(1, taps):
+        found = found | ((row == length - 1) & (col == tokens[length - 1]))
+    return jnp.where(found, 1.0, 0.0).astype(BF16)
 
 
 def spread_rows(spread, index, count):
@@ -134,48 +131,52 @@
     count,
     here_ref,
     complement_ref,
-    tokens_hbm,
-    spread_hbm,
-    embedding_hbm,
-    step_weight_hbm,
-    step_bias_hbm,
-    rate_hbm,
-    skip_hbm,
-    last_hbm,
-    select_hbm,
-    conv_weight_hbm,
-    conv_bias_hbm,
-    gain_hbm,
-    in_weight_hbm,
-    mixed_hbm,
-    tokens_ref,
-    spread_ref,
-    embedding_ref,
-    step_weight_ref,
-    step_bias_ref,
-    rate_ref,
-    skip_ref,
-    last_ref,
-    select_ref,
-    conv_weight_ref,
-    conv_bias_ref,
-    gain_ref,
-    in_weight_ref,
-    mixed_ref,
-    words_ref,
-    gates_ref,
-    coefs_ref,
-    exponent_ref,
-    match_ref,
-    weight_ref,
-    base_ref,
-    gated_ref,
-    in_sems,
-    out_sem,
+    *refs,
 ):
+    token_hbms, refs = refs[:4], refs[4:]
+    (
+        spread_hbm,
+        embedding_hbm,
+        step_weight_hbm,
+        step_bias_hbm,
+        rate_hbm,
+        skip_hbm,
+        last_hbm,
+        select_hbm,
+        conv_weight_hbm,
+        conv_bias_hbm,
+        gain_hbm,
+        in_weight_hbm,
+        mixed_hbm,
+        tokens_ref,
+        spread_ref,
+        embedding_ref,
+        step_weight_ref,
+        step_bias_ref,
+        rate_ref,
+        skip_ref,
+        last_ref,
+        select_ref,
+        conv_weight_ref,
+        conv_bias_ref,
+        gain_ref,
+        in_weight_ref,
+        mixed_ref,
+        words_ref,
+        gates_ref,
+        coefs_ref,
+        exponent_ref,
+        match_ref,
+        weight_ref,
+        base_ref,
+        gated_ref,
+        gate_ref,
+        in_sems,
+        out_sem,
+    ) = refs
     reads = start_all(
         (
-            (tokens_hbm, tokens_ref),
+            *((hbm, tokens_ref.at[k]) for k, hbm in enumerate(token_hbms)),
             (spread_hbm, spread_ref),
             (embedding_hbm, embedding_ref),
             (step_weight_hbm, step_weight_ref),
@@ -192,22 +193,23 @@
         in_sems,
     )
     here = here_ref[0]
-    rows = tokens_ref.shape[1]
+    rows = tokens_ref.shape[2]
     own = rows // BLOCK
     blocks = count * own
     heads, inner = spread_ref.shape
     head = inner // heads
-    word_rows = select_ref.shape[0]
+    full = select_ref.shape[0]
     part_rows = select_ref.shape[1] // 4
-    starts, _, _ = word_plan(letters, taps)
     first, past = here * own, (here + 1) * own
     chunks = BLOCK // CHUNK
     as_bf16 = lambda mask: jnp.where(mask, 1.0, 0.0).astype(BF16)
     complement = lambda letter: complement_ref[letter]
 
-    reads[0].wait()
-    tokens16 = tokens_ref[...].astype(F32).astype(BF16)
-    source, target = iota((blocks, count), 1) ^ here, iota((blocks, count), 0)
+    for copy in reads[:4]:
+        copy.wait()
+    tokens16 = jnp.concatenate([tokens_ref[k] for k in range(4)], axis=0).astype(F32).astype(BF16)
+    place, target = iota((blocks, count), 1), iota((blocks, count), 0)
+    source = here ^ (place % (count // 4) * 4 + place // (count // 4))
     around = jnp.zeros((3 * blocks, BLOCK), F32)
     for part in range(own):
         block = source * own + part
@@ -217,28 +219,35 @@
     before, middle, after = (around[k * blocks : (k + 1) * blocks] for k in range(3))
     position = iota((blocks, BLOCK), 0) * BLOCK + iota((blocks, BLOCK), 1)
     rise_index = word_index(
-        jnp.concatenate([before, middle], axis=1), BLOCK, BLOCK, False, starts, taps, letters, position
+        jnp.concatenate([before, middle], axis=1), BLOCK, BLOCK, False, taps, letters, position
     )
     fall_index = word_index(
         jnp.concatenate([middle, after], axis=1),
         0,
         BLOCK,
         True,
-        starts,
         taps,
         letters,
         blocks * BLOCK - 1 - position,
     )
     block_of = iota((blocks, BLOCK), 0)
-    middle_word = word_rows // 2
-    word = (iota((word_rows, BLOCK), 0) - middle_word).astype(F32).astype(BF16)
+    middle_word = full // 2
+    word = (iota((full + 16, BLOCK), 0) - middle_word).astype(F32).astype(BF16)
     index = jnp.where(block_of < first, rise_index, fall_index) - middle_word
     index = index.astype(F32).astype(BF16)
     one, zero = jnp.ones((), BF16), jnp.zeros((), BF16)
     for block in range(blocks):
         match_ref[:, block * BLOCK : (block + 1) * BLOCK] = jnp.where(
-            word == index[block : block + 1], one, zero
+            word[:full] == index[block : block + 1], one, zero
         )
+    ends = [
+        jnp.where(word[full:] == index[block : block + 1], one, zero) for block in (0, blocks - 1)
+    ]
+
+    end_tokens = (
+        [middle[:1, k : k + 1] for k in range(taps - 1)],
+        [middle[blocks - 1 :, BLOCK - 1 - k : BLOCK - k] for k in range(taps - 1)],
+    )
 
     letter_hot = [jnp.where(middle == letter, 1.0, 0.0) for letter in range(letters)]
     stack = jnp.concatenate(letter_hot, axis=0).astype(BF16)
@@ -264,7 +273,8 @@
     inside_row = iota((BLOCK, LANES), 0) % CHUNK
     lane = iota((BLOCK, LANES), 1)
     hot_lane = jnp.where(lane < 48, (lane % 16).astype(F32), -1.0)
-    word_lane = iota((BLOCK, word_rows), 1).astype(F32)
+    word_lane = iota((BLOCK, full), 1).astype(F32)
+    end_lane = (iota((16, 16), 1) + full).astype(F32)
     small_half = iota((CHUNK, LANES), 1) % CHUNK
     small_row = iota((CHUNK, LANES), 0)
     small_lane = iota((CHUNK, LANES), 1)
@@ -281,6 +291,10 @@
         facts = jnp.concatenate([facts, jnp.zeros((LANES - 8, BLOCK), F32)], axis=0).T
         matches = [
             jnp.where(word_lane == facts[:, d : d + 1], 1.0, 0.0).astype(BF16) for d in range(2)
+        ]
+        matches += [
+            jnp.where(end_lane == facts[at : at + 16, d : d + 1], 1.0, 0.0).astype(BF16)
+            for d, at in ((0, 0), (1, BLOCK - 16))
         ]
         hot = jnp.where(hot_lane == facts[:, 2:3], 1.0, 0.0)
         hot16 = hot.astype(BF16)
@@ -302,7 +316,7 @@
             doubled.append(jnp.where(keep, window, pltpu.roll(window, CHUNK, 1)))
         prepared.append((matches, hot, hot16, tallies, between, totals, doubled))
 
-    for copy in reads[1:8]:
+    for copy in reads[4:11]:
         copy.wait()
     spread = spread_ref[...]
     width = embedding_ref.shape[1]
@@ -353,7 +367,8 @@
     for place in range(2):
         rest = jnp.zeros((LANES - 48, LANES), BF16)
         exponent_ref[place] = jnp.concatenate([*split3(exponents[place]), rest], axis=0)
-    word_steps = dot(last_ref[...], pack_split(exponents[2], 2))
+    lasts = [last_ref[...]] + [first_last(x, letters, taps) for x in end_tokens]
+    word_steps = dot(jnp.concatenate(lasts, axis=0), pack_split(exponents[2], 2))
 
     talls = [
         [
@@ -373,7 +388,15 @@
         weight_ref[: 2 * heads, lanes] = jnp.where(rises, weight, 0.0).astype(BF16)
         weight_ref[2 * heads :, lanes] = jnp.where(falls, weight, 0.0).astype(BF16)
     word_weights = dot(match_ref[...], weight_ref[...], NT)
+    end_weights = [
+        dot(end, weight_ref[:, block * BLOCK : (block + 1) * BLOCK], NT)
+        for end, block in zip(ends, (0, blocks - 1))
+    ]
+    word_weights = jnp.concatenate([word_weights, *end_weights], axis=0)
     word_weights = (word_weights * word_steps[:, : 4 * heads]).astype(BF16)
+    end_selects = [
+        first_words(x, letters, taps, part_rows, 4 * part_rows) for x in end_tokens
+    ]
 
     narrows = []
     for matches, hot, hot16, tallies, between, totals, doubled in prepared:
@@ -382,15 +405,26 @@
             jnp.concatenate([up, down, down - hot, up - hot], axis=0).astype(BF16), exponent_ref[0]
         )
         power = lambda k: powers[k * BLOCK : (k + 1) * BLOCK]
-        rising = lane < 2 * heads
-        from_start = jnp.exp2(jnp.where(rising, power(0), power(1)))
         steps = dot(hot16, exponent_ref[1])
-        to_end = jnp.exp2(jnp.where(rising, power(2), power(3)) + steps)
-        narrows.append(
-            jnp.concatenate([from_start, to_end], axis=0).astype(BF16)[:, : 4 * heads]
-        )
-
-    for copy in reads[8:]:
+        chunk_power = [power(0)[(i + 1) * CHUNK - 1 : (i + 1) * CHUNK] for i in range(chunks)]
+        found = []
+        for falls in (False, True):
+            ends_at = power(2 + falls) + steps
+            pieces = [power(int(falls))]
+            for i in range(chunks + 1):
+                target = chunks - 1 - i if falls else i
+                if i == chunks and own == 1:
+                    continue
+                for j in range(chunks):
+                    passed = range(target + 1, j) if falls else range(j + 1, target)
+                    if (j > target) if falls else (j < target):
+                        pieces.append(
+                            ends_at[j * CHUNK : (j + 1) * CHUNK] + sum(chunk_power[m] for m in passed)
+                        )
+            found.append(jnp.exp2(jnp.concatenate(pieces, axis=0)).astype(BF16)[:, : 4 * heads])
+        narrows.append(found)
+
+    for copy in reads[11:]:
         copy.wait()
     projected = dot(embedding, in_weight_ref[...]).astype(BF16).astype(F32)
     gate = silu(projected[:, :inner])
@@ -417,7 +451,8 @@
         for place, piece in enumerate(split3(conv_bias_ref[param : param + 1, :])):
             bias_rows = jnp.where(iota((part_rows, 1), 0) == place, piece.astype(F32), bias_rows)
         products = jnp.concatenate([*split3(weights * inputs), bias_rows.astype(BF16)], axis=0)
-        conved = silu(dot(select_ref[...], products))
+        select = jnp.concatenate([select_ref[...], end_selects[d]], axis=0)
+        conved = silu(dot(select, products))
         words_ref[:, :inner] = conved[:, :inner].astype(BF16)
         rest = conved[:, inner:]
         rest_lane = iota(rest.shape, 1)
@@ -426,7 +461,10 @@
         ).astype(BF16)
         turned = rest.T[:state].astype(BF16)
         to_lanes = spread_rows(spread, index4, 4)
-        weighted = (dot(word_weights, to_lanes) * conved[:, :inner]).astype(BF16)
+        own_weights = jnp.concatenate(
+            [word_weights[:full], word_weights[full + 16 * d : full + 16 * (d + 1)]], axis=0
+        )
+        weighted = (dot(own_weights, to_lanes) * conved[:, :inner]).astype(BF16)
         held = dot(turned, weighted)
 
         decay = [coefs_ref[index4, l : l + 1] for l in range(letters)]
@@ -435,18 +473,27 @@
         squares = []
         for part in range(own - 1, -1, -1) if falls else range(own):
             matches, _, hot16, _, between, totals, doubled = prepared[part]
-            match, at = matches[d], part * BLOCK
+            match, end_match, at = matches[d], matches[2 + d], part * BLOCK
+
+            def looked_up(columns):
+                found = dot(match, words_ref[:full, columns])
+                more = dot(end_match, words_ref[full:, columns])
+                if falls:
+                    return jnp.concatenate([found[: BLOCK - 16], found[BLOCK - 16 :] + more], axis=0)
+                return jnp.concatenate([found[:16] + more, found[16:]], axis=0)
+
             order = range(chunks - 1, -1, -1) if falls else range(chunks)
-            bt = dot(turned, match, NT)
-            c_rows = dot(match, words_ref[:, inner : inner + LANES])
-            values = dot(match, words_ref[:, :inner])
-            spreads = dot(narrows[part], to_lanes)
-            all_scores = dot(c_rows.astype(BF16)[:, :state], bt.astype(BF16))
-            bt_lane = iota(bt.shape, 1) // CHUNK
-            bt_chunks = jnp.concatenate(
-                [jnp.where(bt_lane == i, bt, 0.0).astype(BF16) for i in range(chunks)], axis=0
-            )
-            fresh = dot(bt_chunks, (values * spreads[BLOCK:]).astype(BF16))
+            end_bt = dot(turned[:, full:], end_match, NT)
+            bt = dot(turned[:, :full], match, NT)
+            if falls:
+                bt = jnp.concatenate([bt[:, : BLOCK - 16], bt[:, BLOCK - 16 :] + end_bt], axis=1)
+            else:
+                bt = jnp.concatenate([bt[:, :16] + end_bt, bt[:, 16:]], axis=1)
+            c_rows = looked_up(slice(inner, inner + LANES))
+            values = looked_up(slice(0, inner))
+            spreads = dot(narrows[part][d], to_lanes)
+            c16, bt16 = c_rows.astype(BF16)[:, :state], bt.astype(BF16)
+            all_scores = dot(c16, bt16)
             values16 = values.astype(BF16)
             scores = []
             for i in range(chunks):
@@ -456,20 +503,38 @@
                 both = jnp.where(keep, window, pltpu.roll(window, CHUNK, 1))
                 causal = (small_half >= small_row) if falls else (small_half <= small_row)
                 scores.append(jnp.where(causal, both, 0.0))
-            entering = [None] * chunks
+            twice = c_rows + pltpu.roll(c_rows, state, 1)
+            c_chunks = jnp.concatenate([twice] * (chunks * state // LANES), axis=1)
+            earlier = (lane_chunk > block_chunk) if falls else (lane_chunk < block_chunk)
+            left = jnp.where(earlier, all_scores, 0.0)
+            left = jnp.where(lane_chunk == block_chunk, c_chunks, left).astype(BF16)
+            used = BLOCK
+            power_sum = None
+            pairs = LANES // CHUNK
             for i in order:
-                entering[i] = held.astype(BF16)
-                power_sum = jnp.zeros((1, inner), F32)
+                decayed = held if power_sum is None else held * jnp.exp2(power_sum)
+                blocks_of = [jnp.zeros((CHUNK, inner), BF16)] * chunks
+                blocks_of[i] = decayed.astype(BF16)
+                others = range(i + 1, chunks) if falls else range(i)
+                for j in others:
+                    rows_of = slice(j * CHUNK, (j + 1) * CHUNK)
+                    blocks_of[j] = (values[rows_of] * spreads[used : used + CHUNK]).astype(BF16)
+                    used += CHUNK
+                low = (i // pairs) * pairs if falls else 0
+                high = chunks if falls else (i // pairs + 1) * pairs
+                chunk = slice(i * CHUNK, (i + 1) * CHUNK)
+                carried = dot(
+                    left[chunk, low * CHUNK : high * CHUNK],
+                    jnp.concatenate(blocks_of[low:high], axis=0),
+                )
+                base_ref[chunk] = carried * spreads[chunk] + skip * values[chunk]
                 for l in range(letters):
                     row = totals[i * letters + l : i * letters + l + 1]
-                    row = jnp.concatenate([row] * (inner // LANES), axis=1)
-                    power_sum = power_sum + row * decay[l]
-                held = fresh[i * state : (i + 1) * state] + held * jnp.exp2(power_sum)
-            twice = c_rows + pltpu.roll(c_rows, state, 1)
-            c_chunks = jnp.concatenate([twice] * (chunks * state // LANES), axis=1)
-            c_chunks = jnp.where(block_chunk == lane_chunk, c_chunks, 0.0).astype(BF16)
-            carried = dot(c_chunks, jnp.concatenate(entering, axis=0))
-            base_ref[...] = carried * spreads[:BLOCK] + skip * values
+                    row = jnp.concatenate([row] * (inner // LANES), axis=1) * decay[l]
+                    power_sum = row if power_sum is None else power_sum + row
+            if own > 1:
+                fresh = dot(bt16, (values * spreads[used : used + BLOCK]).astype(BF16))
+                held = held * jnp.exp2(power_sum) + fresh
             square = [None] * chunks
             for group in range(inner // WIDE):
                 wide = slice(group * WIDE, (group + 1) * WIDE)
@@ -492,7 +557,11 @@
                         jnp.concatenate([chunk_values * mask for mask in head_masks], axis=0)
                     )
                 inside = [dot(m, v) for m, v in zip(mixed, stacked)]
-                gate = dot(hot16[:, :32], gates_ref[strand, :, wide])
+                if index4 == strand:
+                    gate_ref[strand, at : at + BLOCK, wide] = dot(
+                        hot16[:, :32], gates_ref[strand, :, wide]
+                    )
+                gate = gate_ref[strand, at : at + BLOCK, wide]
                 for i in range(chunks):
                     chunk = slice(i * CHUNK, (i + 1) * CHUNK)
                     gated = (inside[i] + base_ref[chunk, wide]) * gate[chunk]
@@ -504,20 +573,22 @@
         scales.append(lax.rsqrt(jnp.concatenate(squares, axis=0) * (1.0 / inner) + EPSILON))
     for group in range(inner // WIDE):
         wide = slice(group * WIDE, (group + 1) * WIDE)
-        total = None
-        for index4, (falls, strand, param) in enumerate(PASSES):
-            normed = gated_ref[index4, :, wide] * scales[index4] * gain_ref[param : param + 1, wide]
-            total = normed if total is None else total + normed
+        total = 0.0
+        for param in range(2):
+            part = sum(
+                gated_ref[k, :, wide] * scales[k] for k in range(len(PASSES)) if PASSES[k][2] == param
+            )
+            total = total + part * gain_ref[param : param + 1, wide]
         mixed_ref[:, wide] = total.astype(BF16)
     copy = pltpu.make_async_copy(mixed_ref, mixed_hbm, out_sem)
     copy.start()
     copy.wait()
 
 
-def output_kernel(depth, places, here_ref, mixed_hbm, *refs):
+def output_kernel(depth, places, flip, here_ref, side_ref, mixed_hbm, *refs):
     pieces = refs[: len(places)]
-    out_ref, weight_ref, mixed_ref, sem = refs[len(places) :]
-    here = here_ref[0]
+    out_hbm, weight_ref, mixed_ref, out_ref, sem, out_sem = refs[-6:]
+    here, side = here_ref[0], side_ref[0]
     pairs = [(mixed_hbm, mixed_ref)]
     for piece, masks in zip(pieces, places):
         for k, mask in enumerate(masks):
@@ -526,6 +597,11 @@
     for copy in start_all(pairs, sem):
         copy.wait()
     out_ref[...] = dot(mixed_ref[...], weight_ref[...]).astype(BF16)
+    columns = out_ref.shape[1]
+    lane = pl.multiple_of((side ^ flip) * columns, columns)
+    copy = pltpu.make_async_copy(out_ref, out_hbm.at[:, pl.ds(lane, columns)], out_sem)
+    copy.start()
+    copy.wait()
 
 
 def swap(x, axis, mask):
@@ -570,20 +646,21 @@
     side = lax.axis_index("batch").astype(jnp.int32)[None]
     depth, columns = out_weight.shape
 
-    bits = [1 << k for k in range(count.bit_length() - 1)]
     join = lambda *x: jnp.concatenate(x, axis=0)
     moved = lambda masks, mask: [m ^ mask for m in masks]
-    tokens, token_bits = token_ids[None], list(bits)
     line, line_masks = out_weight[None], [0]
-    for mask in bits[:1:-1]:
+    tokens = token_ids[None]
+    token_line = [swap(tokens, "seq", mask) for mask in range(count - 4, 0, -4)]
+    mask = count // 2
+    while mask > 2:
         arrived = swap(line, "seq", mask)
-        if token_bits:
-            tokens = join(tokens, swap(tokens, "seq", token_bits.pop(0)))
+        if mask == count // 2:
+            arrived, token_line = lax.optimization_barrier((arrived, token_line))
+            token_line = join(tokens, *token_line[::-1])
+            tokens = [token_line] + [swap(token_line, "seq", m) for m in (1, 2, 3)]
         line = join(line, arrived)
         line_masks = line_masks + moved(line_masks, mask)
-        line, tokens = lax.optimization_barrier((line, tokens))
-    while token_bits:
-        tokens = join(tokens, swap(tokens, "seq", token_bits.pop(0)))
+        mask //= 2
     across_plane = [swap(line, "seq", mask) for mask in (1, 2, 3)]
     places = [line_masks] + [moved(line_masks, mask) for mask in (1, 2, 3)]
 
@@ -595,7 +672,7 @@
     mixed = []
     for genome in range(genomes):
         inputs = (
-            tokens[:, genome],
+            *(x[:, genome] for x in tokens),
             spread,
             embedding,
             step_weight.T,
@@ -615,17 +692,19 @@
                 out_shape=jax.ShapeDtypeStruct((rows, inner), BF16),
                 in_specs=[smem(), smem()] + [hbm()] * len(inputs),
                 out_specs=hbm(),
-                scratch_shapes=[pltpu.VMEM(x.shape, x.dtype) for x in inputs]
+                scratch_shapes=[pltpu.VMEM((4, *inputs[0].shape), jnp.int32)]
+                + [pltpu.VMEM(x.shape, x.dtype) for x in inputs[4:]]
                 + [
                     pltpu.VMEM((rows, inner), BF16),
-                    pltpu.VMEM((word_rows, inner + LANES), BF16),
+                    pltpu.VMEM((word_rows + 16, inner + LANES), BF16),
                     pltpu.VMEM((2, 32, inner), BF16),
                     pltpu.VMEM((4, 24, inner), F32),
                     pltpu.VMEM((2, LANES, LANES), BF16),
-                    pltpu.VMEM((word_rows, count * rows), BF16),
+                    pltpu.VMEM((letters**taps, count * rows), BF16),
                     pltpu.VMEM((4 * heads, count * rows), BF16),
                     pltpu.VMEM((BLOCK, inner), F32),
                     pltpu.VMEM((4, rows, inner), F32),
+                    pltpu.VMEM((2, rows, inner), F32),
                     pltpu.SemaphoreType.DMA((len(inputs),)),
                     pltpu.SemaphoreType.DMA,
                 ],
@@ -644,35 +723,35 @@
         sets = sets + [([swap(x, "batch", mask) for x in found], s ^ mask) for found, s in sets]
         mask *= 2
 
-    def project(found, mixed):
+    def project(found, flip, mixed, out):
+        operands = (here, side, mixed, *found) + (() if out is None else (out,))
         return pl.pallas_call(
-            partial(output_kernel, depth, places),
-            out_shape=jax.ShapeDtypeStruct((rows, columns), BF16),
-            in_specs=[smem()] + [hbm()] * (1 + len(found)),
-            out_specs=vmem(),
+            partial(output_kernel, depth, places, flip),
+            out_shape=jax.ShapeDtypeStruct((rows, columns * sides), BF16),
+            in_specs=[smem(), smem()] + [hbm()] * (len(operands) - 2),
+            out_specs=hbm(),
             scratch_shapes=[
                 pltpu.VMEM((depth * count, columns), BF16),
                 pltpu.VMEM((rows, inner), BF16),
+                pltpu.VMEM((rows, columns), BF16),
                 pltpu.SemaphoreType.DMA((count + 1,)),
+                pltpu.SemaphoreType.DMA,
             ],
-            compiler_params=pltpu.CompilerParams(vmem_limit_bytes=16 * 2**20),
+            input_output_aliases={} if out is None else {len(operands) - 1: 0},
+            compiler_params=pltpu.CompilerParams(vmem_limit_bytes=VMEM_BYTES),
             cost_estimate=pl.CostEstimate(
                 flops=2 * rows * inner * columns, bytes_accessed=2**22, transcendentals=0
             ),
             name="output",
-        )(here, mixed, *found)
+        )(*operands)
 
     results = []
     for genome in range(genomes):
-        parts = [project(found, mixed[genome]) for found, _ in sets]
-        ordered = []
-        for k in range(sides):
-            chosen = parts[0]
-            for part, (_, part_side) in zip(parts, sets):
-                chosen = jnp.where((side[0] ^ part_side) == k, part, chosen)
-            ordered.append(chosen)
-        results.append(jnp.concatenate(ordered, axis=1))
-    return jnp.stack(results)
+        out = None
+        for found, flip in sets:
+            out = project(found, flip, mixed[genome], out)
+        results.append(out[None])
+    return join(*results) if genomes > 1 else results[0]
 
 
 def solution(mesh):

time: 51 us -> 46.5 us (0.912)
  waiting for transfers between devices: 6.91 us -> 2.46 us
  starting transfers between devices: 17.3 us -> 17.9 us
    ppermute x13 -> x15, waiting for transfers between devices: 6.91 us -> 2.46 us  [swap(): return lax.ppermute(x, axis, [(i, i ^ mask) for i in range(count)])]
    concatenate x5 -> x3, other arithmetic: 2.28 us -> 3.7 us  [on_device(): join = lambda *x: jnp.concatenate(x, axis=0)]
    pallas_call x1, Pallas kernels: 17.6 us -> 16.2 us  [on_device(): pl.pallas_call(partial(mixer_kernel, letters, taps, state, count), out_sh...]
    pallas_call x2, Pallas kernels: 3.97 us -> 5.18 us  [project(): pl.pallas_call(partial(output_kernel, depth, places, flip), out_shape=jax...]
    another operation x1 -> x0, other arithmetic: 0.86 us -> none  [on_device(): return jnp.stack(results)]
    squeeze x1 -> x0, other arithmetic: 0.61 us -> none  [on_device(): tokens[:, genome]]
    ppermute x13 -> x15, starting transfers between devices: 17.3 us -> 17.9 us  [swap(): return lax.ppermute(x, axis, [(i, i ^ mask) for i in range(count)])]
    unnamed x2 -> x6, local copies, waits for them, and re-layouts: 1.04 us -> 0.69 us
  transfers between devices with their start and end apart: 13 -> 15, of which waited for: 4 -> 3; matrix products, arithmetic and copies ran while one was open for 3% -> 6% of each run, Pallas kernels for 38% -> 41%
where the time goes in v3:
time: 46.5 us; the launch traced here: 46.2 us
  Pallas kernels  21.4 us (46%)
  starting transfers between devices  17.9 us (38%)
  other arithmetic  3.7 us (8%)
  waiting for transfers between devices  2.46 us (5%)
  local copies, waits for them, and re-layouts  0.69 us (1%)
    ppermute x15, starting transfers between devices, swap(): return lax.ppermute(x, axis, [(i, i ^ mask) for i in range(count)])  17.9 us
    pallas_call x1, Pallas kernels, on_device(): pl.pallas_call(partial(mixer_kernel, letters, taps, state, count), out_sh...  16.2 us
    pallas_call x2, Pallas kernels, project(): pl.pallas_call(partial(output_kernel, depth, places, flip), out_shape=jax...  5.18 us
    concatenate x3, other arithmetic, on_device(): join = lambda *x: jnp.concatenate(x, axis=0)  3.7 us
    ppermute x15, waiting for transfers between devices, swap(): return lax.ppermute(x, axis, [(i, i ^ mask) for i in range(count)])  2.46 us
  transfers between devices with their start and end apart: 15, of which 3 were waited for; matrix products, arithmetic and copies ran while one was open for 6% of the time, Pallas kernels for 41%

profile of v3, /device:TPU:0, one launch (start us, length us, event | category | flops | bytes accessed | tf_op | source)
XLA Modules:
  0.0 46.2 jit_solution(16670887502514488805)
XLA Ops:
  0.0 4.0 %collective-permute-start = (bf16[1,64,512]{2,1,0:T(8,128)(2,1)}, bf16[1,64,512]{2,1,0:T(8,128)(2,1)S(1)}, u32[]{:S(2)}, u32[]{:S(2)}) collective-permute-start(bf16[1,64,512]{2,1,0:T(8,128)(2,1)} %bitcast.11), channel_id=1, source_target_pairs={{0,8},{1,9},{2,10},{3,11},{4,12},{5,13},{6,14},{7,15},{8,0},{9,1},... | collective-permute-start | bytes 196616 | tf_op jit(solution)/shard_map/ppermute | solution.py:609
  4.0 1.3 %collective-permute-start.1 = (s32[1,1,256]{2,0,1:T(1,128)}, s32[1,1,256]{2,0,1:T(1,128)S(1)}, u32[]{:S(2)}, u32[]{:S(2)}) collective-permute-start(s32[1,1,256]{2,0,1:T(1,128)} %bitcast.14), channel_id=1, source_target_pairs={{0,12},{1,13},{2,14},{3,15},{4,8},{5,9},{6,10},{7,11},{8,4},{9,5},... | collective-permute-start | bytes 3080 | tf_op jit(solution)/shard_map/ppermute | solution.py:609
  5.4 1.7 %collective-permute-start.2 = (s32[1,1,256]{2,0,1:T(1,128)}, s32[1,1,256]{2,0,1:T(1,128)S(1)}, u32[]{:S(2)}, u32[]{:S(2)}) collective-permute-start(s32[1,1,256]{2,0,1:T(1,128)} %bitcast.15), channel_id=1, source_target_pairs={{0,8},{1,9},{2,10},{3,11},{4,12},{5,13},{6,14},{7,15},{8,0},{9,1},... | collective-permute-start | bytes 3080 | tf_op jit(solution)/shard_map/ppermute | solution.py:609
  7.1 1.3 %collective-permute-start.3 = (s32[1,1,256]{2,0,1:T(1,128)}, s32[1,1,256]{2,0,1:T(1,128)S(1)}, u32[]{:S(2)}, u32[]{:S(2)}) collective-permute-start(s32[1,1,256]{2,0,1:T(1,128)} %bitcast.16), channel_id=1, source_target_pairs={{0,4},{1,5},{2,6},{3,7},{4,0},{5,1},{6,2},{7,3},{8,12},{9,13},{10,... | collective-permute-start | bytes 3080 | tf_op jit(solution)/shard_map/ppermute | solution.py:609
  8.4 1.2 %collective-permute-done.1 = s32[1,1,256]{2,0,1:T(1,128)S(1)} collective-permute-done((s32[1,1,256]{2,0,1:T(1,128)}, s32[1,1,256]{2,0,1:T(1,128)S(1)}, u32[]{:S(2)}, u32[]{:S(2)}) %collective-permute-start.1) | collective-permute-done | bytes 1056 | tf_op jit(solution)/shard_map/ppermute | solution.py:609
  9.6 0.4 collective-permute-done.2
  10.1 0.8 %collective-permute-done.3 = s32[1,1,256]{2,0,1:T(1,128)S(1)} collective-permute-done((s32[1,1,256]{2,0,1:T(1,128)}, s32[1,1,256]{2,0,1:T(1,128)S(1)}, u32[]{:S(2)}, u32[]{:S(2)}) %collective-permute-start.3) | collective-permute-done | bytes 1056 | tf_op jit(solution)/shard_map/ppermute | solution.py:609
  10.9 0.0 collective-permute-done
  10.9 0.9 %pad_maximum_fusion.1 = bf16[2,64,512]{2,1,0:T(8,128)(2,1)S(1)} fusion(bf16[1,64,512]{2,1,0:T(8,128)(2,1)S(1)} %collective-permute-done, bf16[1,64,512]{2,1,0:T(8,128)(2,1)} %bitcast.12), kind=kLoop, calls=%fused_computation.1 | loop fusion | flops 65536 | bytes 262144 | tf_op jit(solution)/shard_map/concatenate | solution.py:649
  11.7 1.4 %collective-permute-start.4 = (bf16[2,64,512]{2,1,0:T(8,128)(2,1)S(1)}, bf16[2,64,512]{2,1,0:T(8,128)(2,1)S(1)}, u32[]{:S(2)}, u32[]{:S(2)}) collective-permute-start(bf16[2,64,512]{2,1,0:T(8,128)(2,1)S(1)} %pad_maximum_fusion.1), channel_id=1, source_target_pairs={{0,4},{1,5},{2,6},{3,7},{4,0},{5,1},{6,2},{7,3},{8,12},{9,13},{10,... | collective-permute-start | bytes 393224 | tf_op jit(solution)/shard_map/ppermute | solution.py:609
  13.1 1.3 %pad_add_fusion = (s32[4,1,256]{2,0,1:T(4,128)S(1)}, s32[4,256]{1,0:T(4,128)}) fusion(s32[1,1,256]{2,0,1:T(1,128)S(1)} %collective-permute-done.1, s32[1,1,256]{2,0,1:T(1,128)S(1)} %collective-permute-done.2, s32[1,1,256]{2,0,1:T(1,128)S(1)} %collective-permute-done.3, s32[1,1,256]{2,0,1:T(1,128)} %bitcast.17), kind=kLoop, calls=%fused_computation.2 | loop fusion | flops 3072 | bytes 12288 | tf_op jit(solution)/shard_map/concatenate | solution.py:649
  14.4 1.5 %collective-permute-start.8 = (s32[4,1,256]{2,0,1:T(4,128)S(1)}, s32[4,1,256]{2,0,1:T(4,128)S(1)}, u32[]{:S(2)}, u32[]{:S(2)}) collective-permute-start(s32[4,1,256]{2,0,1:T(4,128)S(1)} %get-tuple-element.23), channel_id=1, source_target_pairs={{0,1},{1,0},{2,3},{3,2},{4,5},{5,4},{6,7},{7,6},{8,9},{9,8},{10,11... | collective-permute-start | bytes 12296 | tf_op jit(solution)/shard_map/ppermute | solution.py:609
  15.9 1.5 %collective-permute-start.9 = (s32[4,1,256]{2,0,1:T(4,128)S(1)}, s32[4,1,256]{2,0,1:T(4,128)S(1)}, u32[]{:S(2)}, u32[]{:S(2)}) collective-permute-start(s32[4,1,256]{2,0,1:T(4,128)S(1)} %get-tuple-element.23), channel_id=1, source_target_pairs={{0,2},{1,3},{2,0},{3,1},{4,6},{5,7},{6,4},{7,5},{8,10},{9,11},{10,... | collective-permute-start | bytes 12296 | tf_op jit(solution)/shard_map/ppermute | solution.py:609
  17.4 0.5 %collective-permute-start.10 = (s32[4,1,256]{2,0,1:T(4,128)S(1)}, s32[4,1,256]{2,0,1:T(4,128)S(1)}, u32[]{:S(2)}, u32[]{:S(2)}) collective-permute-start(s32[4,1,256]{2,0,1:T(4,128)S(1)} %get-tuple-element.23), channel_id=1, source_target_pairs={{0,3},{1,2},{2,1},{3,0},{4,7},{5,6},{6,5},{7,4},{8,11},{9,10},{10,... | collective-permute-start | bytes 12296 | tf_op jit(solution)/shard_map/ppermute | solution.py:609
  17.9 0.0 collective-permute-done.4
  17.9 1.6 %pad_maximum_fusion.refs_0_ = bf16[4,64,512]{2,1,0:T(8,128)(2,1)} fusion(bf16[2,64,512]{2,1,0:T(8,128)(2,1)S(1)} %collective-permute-done.4, bf16[1,64,512]{2,1,0:T(8,128)(2,1)S(1)} %collective-permute-done, bf16[1,64,512]{2,1,0:T(8,128)(2,1)} %bitcast.13), kind=kLoop, calls=%fused_computation | loop fusion | flops 262144 | bytes 524288 | tf_op jit(solution)/shard_map/concatenate | solution.py:649
  19.5 1.5 %collective-permute-start.5 = (bf16[4,64,512]{2,1,0:T(8,128)(2,1)}, bf16[4,64,512]{2,1,0:T(8,128)(2,1)}, u32[]{:S(2)}, u32[]{:S(2)}) collective-permute-start(bf16[4,64,512]{2,1,0:T(8,128)(2,1)} %pad_maximum_fusion.refs_0_), channel_id=1, source_target_pairs={{0,1},{1,0},{2,3},{3,2},{4,5},{5,4},{6,7},{7,6},{8,9},{9,8},{10,11... | collective-permute-start | bytes 786440 | tf_op jit(solution)/shard_map/ppermute | solution.py:609
  21.0 1.5 %collective-permute-start.6 = (bf16[4,64,512]{2,1,0:T(8,128)(2,1)}, bf16[4,64,512]{2,1,0:T(8,128)(2,1)}, u32[]{:S(2)}, u32[]{:S(2)}) collective-permute-start(bf16[4,64,512]{2,1,0:T(8,128)(2,1)} %pad_maximum_fusion.refs_0_), channel_id=1, source_target_pairs={{0,2},{1,3},{2,0},{3,1},{4,6},{5,7},{6,4},{7,5},{8,10},{9,11},{10,... | collective-permute-start | bytes 786440 | tf_op jit(solution)/shard_map/ppermute | solution.py:609
  22.5 0.0 collective-permute-done.8
  22.5 0.0 copy-start
  22.5 0.5 %collective-permute-start.7 = (bf16[4,64,512]{2,1,0:T(8,128)(2,1)}, bf16[4,64,512]{2,1,0:T(8,128)(2,1)}, u32[]{:S(2)}, u32[]{:S(2)}) collective-permute-start(bf16[4,64,512]{2,1,0:T(8,128)(2,1)} %pad_maximum_fusion.refs_0_), channel_id=1, source_target_pairs={{0,3},{1,2},{2,1},{3,0},{4,7},{5,6},{6,5},{7,4},{8,11},{9,10},{10,... | collective-permute-start | bytes 786440 | tf_op jit(solution)/shard_map/ppermute | solution.py:609
  23.0 0.0 collective-permute-done.9
  23.0 0.0 copy-start.1
  23.0 0.0 collective-permute-done.10
  23.0 0.1 copy-done
  23.1 0.0 copy-start.2
  23.1 0.5 %copy-done.1 = s32[4,1,256]{2,0,1:T(4,128)} copy-done((s32[4,1,256]{2,0,1:T(4,128)}, s32[4,1,256]{2,0,1:T(4,128)S(1)}, u32[]{:S(2)}) %copy-start.1) | copy-done | bytes 4120
  23.6 0.1 copy-done.2
  23.7 16.2 %mixer.1.mixed_hbm = bf16[256,1024]{1,0:T(8,128)(2,1)} custom-call(s32[1]{0:T(128)} %bitcast.here_ref, s32[4]{0:T(128)} %complement_ref.1, s32[4,256]{1,0:T(4,128)} %get-tuple-element.24.refs_0_, s32[4,256]{1,0:T(4,128)} %bitcast.19, s32[4,256]{1,0:T(4,128)} %bitcast.20, s32[4,256]{1,0:T(4,128)} %bitcast.21, bf16[16,1024]{1,0:T(8,128)(2,1)} %constant.15.clone.refs_4_, ...), custom_call_target="tpu_custom_call" | custom-call | flops 10000000000 | bytes 52428800 | tf_op jit(solution)/shard_map/mixer/pallas_call | solution.py:690
  39.9 0.0 collective-permute-done.5.refs_1_
  39.9 0.0 collective-permute-done.6.refs_2_
  39.9 0.0 collective-permute-done.7.refs_3_
  39.9 0.1 collective-permute-start.11
  40.0 0.5 %collective-permute-start.12 = (bf16[4,64,512]{2,1,0:T(8,128)(2,1)}, bf16[4,64,512]{2,1,0:T(8,128)(2,1)}, u32[]{:S(2)}, u32[]{:S(2)}) collective-permute-start(bf16[4,64,512]{2,1,0:T(8,128)(2,1)} %collective-permute-done.5.refs_1_), channel_id=1, source_target_pairs={{0,16},{16,0},{1,17},{17,1},{2,18},{18,2},{3,19},{19,3},{4,20},{20... | collective-permute-start | bytes 786440 | tf_op jit(solution)/shard_map/ppermute | solution.py:609
  40.5 0.1 collective-permute-start.13
  40.6 0.4 collective-permute-start.14
  41.0 2.6 %output.2.refs_4_ = bf16[256,1024]{1,0:T(8,128)(2,1)} custom-call(s32[1]{0:T(128)} %bitcast.here_ref, s32[1]{0:T(128)} %bitcast.1.side_ref, bf16[256,1024]{1,0:T(8,128)(2,1)} %mixer.1.mixed_hbm, bf16[4,64,512]{2,1,0:T(8,128)(2,1)} %pad_maximum_fusion.refs_0_, bf16[4,64,512]{2,1,0:T(8,128)(2,1)} %collective-permute-done.5.refs_1_, ...), custom_call_target="tpu_custom_call" | custom-call | flops 268435456 | bytes 4194304 | tf_op jit(solution)/shard_map/output/pallas_call | solution.py:728
  43.6 0.0 collective-permute-done.11.refs_0_
  43.6 0.0 collective-permute-done.12.refs_1_
  43.6 0.0 collective-permute-done.13.refs_2_
  43.6 0.0 collective-permute-done.14.refs_3_
  43.6 2.6 %output.3 = bf16[256,1024]{1,0:T(8,128)(2,1)} custom-call(s32[1]{0:T(128)} %bitcast.here_ref, s32[1]{0:T(128)} %bitcast.1.side_ref, bf16[256,1024]{1,0:T(8,128)(2,1)} %mixer.1.mixed_hbm, bf16[4,64,512]{2,1,0:T(8,128)(2,1)} %collective-permute-done.11.refs_0_, bf16[4,64,512]{2,1,0:T(8,128)(2,1)} %collective-permute-done.12.refs_1_, ...), custom_call_target="tpu_custom_call", output_to_operand_aliasing={{}: (7, {})} | custom-call | flops 268435456 | bytes 4194304 | tf_op jit(solution)/shard_map/output/pallas_call | solution.py:728
Async XLA Ops:
  0.0 10.9 %collective-permute-start = (bf16[1,64,512]{2,1,0:T(8,128)(2,1)}, bf16[1,64,512]{2,1,0:T(8,128)(2,1)S(1)}, u32[]{:S(2)}, u32[]{:S(2)}) collective-permute-start(bf16[1,64,512]{2,1,0:T(8,128)(2,1)} %bitcast.11), channel_id=1, source_target_pairs={{0,8},{1,9},{2,10},{3,11},{4,12},{5,13},{6,14},{7,15},{8,0},{9,1},... | collective-permute-start | bytes 196616 | tf_op jit(solution)/shard_map/ppermute | solution.py:609
  4.0 5.6 %collective-permute-start.1 = (s32[1,1,256]{2,0,1:T(1,128)}, s32[1,1,256]{2,0,1:T(1,128)S(1)}, u32[]{:S(2)}, u32[]{:S(2)}) collective-permute-start(s32[1,1,256]{2,0,1:T(1,128)} %bitcast.14), channel_id=1, source_target_pairs={{0,12},{1,13},{2,14},{3,15},{4,8},{5,9},{6,10},{7,11},{8,4},{9,5},... | collective-permute-start | bytes 3080 | tf_op jit(solution)/shard_map/ppermute | solution.py:609
  5.4 4.7 %collective-permute-start.2 = (s32[1,1,256]{2,0,1:T(1,128)}, s32[1,1,256]{2,0,1:T(1,128)S(1)}, u32[]{:S(2)}, u32[]{:S(2)}) collective-permute-start(s32[1,1,256]{2,0,1:T(1,128)} %bitcast.15), channel_id=1, source_target_pairs={{0,8},{1,9},{2,10},{3,11},{4,12},{5,13},{6,14},{7,15},{8,0},{9,1},... | collective-permute-start | bytes 3080 | tf_op jit(solution)/shard_map/ppermute | solution.py:609
  7.1 3.8 %collective-permute-start.3 = (s32[1,1,256]{2,0,1:T(1,128)}, s32[1,1,256]{2,0,1:T(1,128)S(1)}, u32[]{:S(2)}, u32[]{:S(2)}) collective-permute-start(s32[1,1,256]{2,0,1:T(1,128)} %bitcast.16), channel_id=1, source_target_pairs={{0,4},{1,5},{2,6},{3,7},{4,0},{5,1},{6,2},{7,3},{8,12},{9,13},{10,... | collective-permute-start | bytes 3080 | tf_op jit(solution)/shard_map/ppermute | solution.py:609
  11.7 6.2 %collective-permute-start.4 = (bf16[2,64,512]{2,1,0:T(8,128)(2,1)S(1)}, bf16[2,64,512]{2,1,0:T(8,128)(2,1)S(1)}, u32[]{:S(2)}, u32[]{:S(2)}) collective-permute-start(bf16[2,64,512]{2,1,0:T(8,128)(2,1)S(1)} %pad_maximum_fusion.1), channel_id=1, source_target_pairs={{0,4},{1,5},{2,6},{3,7},{4,0},{5,1},{6,2},{7,3},{8,12},{9,13},{10,... | collective-permute-start | bytes 393224 | tf_op jit(solution)/shard_map/ppermute | solution.py:609
  14.4 8.1 %collective-permute-start.8 = (s32[4,1,256]{2,0,1:T(4,128)S(1)}, s32[4,1,256]{2,0,1:T(4,128)S(1)}, u32[]{:S(2)}, u32[]{:S(2)}) collective-permute-start(s32[4,1,256]{2,0,1:T(4,128)S(1)} %get-tuple-element.23), channel_id=1, source_target_pairs={{0,1},{1,0},{2,3},{3,2},{4,5},{5,4},{6,7},{7,6},{8,9},{9,8},{10,11... | collective-permute-start | bytes 12296 | tf_op jit(solution)/shard_map/ppermute | solution.py:609
  15.9 7.1 %collective-permute-start.9 = (s32[4,1,256]{2,0,1:T(4,128)S(1)}, s32[4,1,256]{2,0,1:T(4,128)S(1)}, u32[]{:S(2)}, u32[]{:S(2)}) collective-permute-start(s32[4,1,256]{2,0,1:T(4,128)S(1)} %get-tuple-element.23), channel_id=1, source_target_pairs={{0,2},{1,3},{2,0},{3,1},{4,6},{5,7},{6,4},{7,5},{8,10},{9,11},{10,... | collective-permute-start | bytes 12296 | tf_op jit(solution)/shard_map/ppermute | solution.py:609
  17.4 5.6 %collective-permute-start.10 = (s32[4,1,256]{2,0,1:T(4,128)S(1)}, s32[4,1,256]{2,0,1:T(4,128)S(1)}, u32[]{:S(2)}, u32[]{:S(2)}) collective-permute-start(s32[4,1,256]{2,0,1:T(4,128)S(1)} %get-tuple-element.23), channel_id=1, source_target_pairs={{0,3},{1,2},{2,1},{3,0},{4,7},{5,6},{6,5},{7,4},{8,11},{9,10},{10,... | collective-permute-start | bytes 12296 | tf_op jit(solution)/shard_map/ppermute | solution.py:609
  19.5 20.4 %collective-permute-start.5 = (bf16[4,64,512]{2,1,0:T(8,128)(2,1)}, bf16[4,64,512]{2,1,0:T(8,128)(2,1)}, u32[]{:S(2)}, u32[]{:S(2)}) collective-permute-start(bf16[4,64,512]{2,1,0:T(8,128)(2,1)} %pad_maximum_fusion.refs_0_), channel_id=1, source_target_pairs={{0,1},{1,0},{2,3},{3,2},{4,5},{5,4},{6,7},{7,6},{8,9},{9,8},{10,11... | collective-permute-start | bytes 786440 | tf_op jit(solution)/shard_map/ppermute | solution.py:609
  21.0 18.9 %collective-permute-start.6 = (bf16[4,64,512]{2,1,0:T(8,128)(2,1)}, bf16[4,64,512]{2,1,0:T(8,128)(2,1)}, u32[]{:S(2)}, u32[]{:S(2)}) collective-permute-start(bf16[4,64,512]{2,1,0:T(8,128)(2,1)} %pad_maximum_fusion.refs_0_), channel_id=1, source_target_pairs={{0,2},{1,3},{2,0},{3,1},{4,6},{5,7},{6,4},{7,5},{8,10},{9,11},{10,... | collective-permute-start | bytes 786440 | tf_op jit(solution)/shard_map/ppermute | solution.py:609
  22.5 0.6 %copy-start = (s32[4,1,256]{2,0,1:T(4,128)}, s32[4,1,256]{2,0,1:T(4,128)S(1)}, u32[]{:S(2)}) copy-start(s32[4,1,256]{2,0,1:T(4,128)S(1)} %collective-permute-done.8) | copy-start | bytes 12292
  22.5 17.4 %collective-permute-start.7 = (bf16[4,64,512]{2,1,0:T(8,128)(2,1)}, bf16[4,64,512]{2,1,0:T(8,128)(2,1)}, u32[]{:S(2)}, u32[]{:S(2)}) collective-permute-start(bf16[4,64,512]{2,1,0:T(8,128)(2,1)} %pad_maximum_fusion.refs_0_), channel_id=1, source_target_pairs={{0,3},{1,2},{2,1},{3,0},{4,7},{5,6},{6,5},{7,4},{8,11},{9,10},{10,... | collective-permute-start | bytes 786440 | tf_op jit(solution)/shard_map/ppermute | solution.py:609
  23.0 0.6 %copy-start.1 = (s32[4,1,256]{2,0,1:T(4,128)}, s32[4,1,256]{2,0,1:T(4,128)S(1)}, u32[]{:S(2)}) copy-start(s32[4,1,256]{2,0,1:T(4,128)S(1)} %collective-permute-done.9) | copy-start | bytes 12292
  23.1 0.6 %copy-start.2 = (s32[4,1,256]{2,0,1:T(4,128)}, s32[4,1,256]{2,0,1:T(4,128)S(1)}, u32[]{:S(2)}) copy-start(s32[4,1,256]{2,0,1:T(4,128)S(1)} %collective-permute-done.10) | copy-start | bytes 12292
  39.9 3.7 %collective-permute-start.11 = (bf16[4,64,512]{2,1,0:T(8,128)(2,1)}, bf16[4,64,512]{2,1,0:T(8,128)(2,1)}, u32[]{:S(2)}, u32[]{:S(2)}) collective-permute-start(bf16[4,64,512]{2,1,0:T(8,128)(2,1)} %pad_maximum_fusion.refs_0_), channel_id=1, source_target_pairs={{0,16},{16,0},{1,17},{17,1},{2,18},{18,2},{3,19},{19,3},{4,20},{20... | collective-permute-start | bytes 786440 | tf_op jit(solution)/shard_map/ppermute | solution.py:609
  40.0 3.6 %collective-permute-start.12 = (bf16[4,64,512]{2,1,0:T(8,128)(2,1)}, bf16[4,64,512]{2,1,0:T(8,128)(2,1)}, u32[]{:S(2)}, u32[]{:S(2)}) collective-permute-start(bf16[4,64,512]{2,1,0:T(8,128)(2,1)} %collective-permute-done.5.refs_1_), channel_id=1, source_target_pairs={{0,16},{16,0},{1,17},{17,1},{2,18},{18,2},{3,19},{19,3},{4,20},{20... | collective-permute-start | bytes 786440 | tf_op jit(solution)/shard_map/ppermute | solution.py:609
  40.5 3.1 %collective-permute-start.13 = (bf16[4,64,512]{2,1,0:T(8,128)(2,1)}, bf16[4,64,512]{2,1,0:T(8,128)(2,1)}, u32[]{:S(2)}, u32[]{:S(2)}) collective-permute-start(bf16[4,64,512]{2,1,0:T(8,128)(2,1)} %collective-permute-done.6.refs_2_), channel_id=1, source_target_pairs={{0,16},{16,0},{1,17},{17,1},{2,18},{18,2},{3,19},{19,3},{4,20},{20... | collective-permute-start | bytes 786440 | tf_op jit(solution)/shard_map/ppermute | solution.py:609
  40.6 3.1 %collective-permute-start.14 = (bf16[4,64,512]{2,1,0:T(8,128)(2,1)}, bf16[4,64,512]{2,1,0:T(8,128)(2,1)}, u32[]{:S(2)}, u32[]{:S(2)}) collective-permute-start(bf16[4,64,512]{2,1,0:T(8,128)(2,1)} %collective-permute-done.7.refs_3_), channel_id=1, source_target_pairs={{0,16},{16,0},{1,17},{17,1},{2,18},{18,2},{3,19},{19,3},{4,20},{20... | collective-permute-start | bytes 786440 | tf_op jit(solution)/shard_map/ppermute | solution.py:609

commit v4 on v3

--- a/solution.py
+++ b/solution.py
@@ -15,6 +15,7 @@
 WIDE = 256
 LOG2E = 1.4426950408889634
 EPSILON = 1e-05
+ORDERS = ((0, 1), (2, 3))
 VMEM_BYTES = 64 * 2**20
 F32 = jnp.float32
 BF16 = jnp.bfloat16
@@ -146,7 +147,7 @@
         conv_weight_hbm,
         conv_bias_hbm,
         gain_hbm,
-        in_weight_hbm,
+        projected_hbm,
         mixed_hbm,
         tokens_ref,
         spread_ref,
@@ -160,7 +161,7 @@
         conv_weight_ref,
         conv_bias_ref,
         gain_ref,
-        in_weight_ref,
+        projected_ref,
         mixed_ref,
         words_ref,
         gates_ref,
@@ -171,6 +172,7 @@
         base_ref,
         gated_ref,
         gate_ref,
+        scale_ref,
         in_sems,
         out_sem,
     ) = refs
@@ -188,7 +190,7 @@
             (conv_weight_hbm, conv_weight_ref),
             (conv_bias_hbm, conv_bias_ref),
             (gain_hbm, gain_ref),
-            (in_weight_hbm, in_weight_ref),
+            (projected_hbm, projected_ref),
         ),
         in_sems,
     )
@@ -205,7 +207,7 @@
     as_bf16 = lambda mask: jnp.where(mask, 1.0, 0.0).astype(BF16)
     complement = lambda letter: complement_ref[letter]
 
-    for copy in reads[:4]:
+    for copy in reads:
         copy.wait()
     tokens16 = jnp.concatenate([tokens_ref[k] for k in range(4)], axis=0).astype(F32).astype(BF16)
     place, target = iota((blocks, count), 1), iota((blocks, count), 0)
@@ -316,8 +318,6 @@
             doubled.append(jnp.where(keep, window, pltpu.roll(window, CHUNK, 1)))
         prepared.append((matches, hot, hot16, tallies, between, totals, doubled))
 
-    for copy in reads[4:11]:
-        copy.wait()
     spread = spread_ref[...]
     width = embedding_ref.shape[1]
     embedding = jnp.concatenate(
@@ -424,9 +424,7 @@
             found.append(jnp.exp2(jnp.concatenate(pieces, axis=0)).astype(BF16)[:, : 4 * heads])
         narrows.append(found)
 
-    for copy in reads[11:]:
-        copy.wait()
-    projected = dot(embedding, in_weight_ref[...]).astype(BF16).astype(F32)
+    projected = projected_ref[...].astype(F32)
     gate = silu(projected[:, :inner])
     for strand in range(2):
         gate_rows = letter_rows(gate, letters, 16, complement if strand else None)
@@ -437,8 +435,8 @@
     lane_chunk = u // CHUNK
     head_of = iota((CHUNK, WIDE), 1) // head
     head_masks = [as_bf16(head_of == h) for h in range(WIDE // head)]
-    scales = []
-    for index4, (falls, strand, param) in enumerate(PASSES):
+    def one_pass(index4):
+        falls, strand, param = PASSES[index4]
         d = int(falls)
         inputs = letter_rows(
             projected[:, inner:], letters, part_rows, complement if strand else None
@@ -453,20 +451,23 @@
         products = jnp.concatenate([*split3(weights * inputs), bias_rows.astype(BF16)], axis=0)
         select = jnp.concatenate([select_ref[...], end_selects[d]], axis=0)
         conved = silu(dot(select, products))
-        words_ref[:, :inner] = conved[:, :inner].astype(BF16)
+        yield
+        words_ref[index4, :, :inner] = conved[:, :inner].astype(BF16)
         rest = conved[:, inner:]
         rest_lane = iota(rest.shape, 1)
-        words_ref[:, inner : inner + LANES] = jnp.where(
+        words_ref[index4, :, inner : inner + LANES] = jnp.where(
             rest_lane < state, pltpu.roll(rest, LANES - state, 1), 0.0
         ).astype(BF16)
         turned = rest.T[:state].astype(BF16)
         to_lanes = spread_rows(spread, index4, 4)
+        yield
         own_weights = jnp.concatenate(
             [word_weights[:full], word_weights[full + 16 * d : full + 16 * (d + 1)]], axis=0
         )
         weighted = (dot(own_weights, to_lanes) * conved[:, :inner]).astype(BF16)
         held = dot(turned, weighted)
 
+        yield
         decay = [coefs_ref[index4, l : l + 1] for l in range(letters)]
         log_step = [coefs_ref[index4, 8 + l : 9 + l] for l in range(letters)]
         skip = coefs_ref[index4, 16:17]
@@ -476,8 +477,8 @@
             match, end_match, at = matches[d], matches[2 + d], part * BLOCK
 
             def looked_up(columns):
-                found = dot(match, words_ref[:full, columns])
-                more = dot(end_match, words_ref[full:, columns])
+                found = dot(match, words_ref[index4, :full, columns])
+                more = dot(end_match, words_ref[index4, full:, columns])
                 if falls:
                     return jnp.concatenate([found[: BLOCK - 16], found[BLOCK - 16 :] + more], axis=0)
                 return jnp.concatenate([found[:16] + more, found[16:]], axis=0)
@@ -491,7 +492,9 @@
                 bt = jnp.concatenate([bt[:, :16] + end_bt, bt[:, 16:]], axis=1)
             c_rows = looked_up(slice(inner, inner + LANES))
             values = looked_up(slice(0, inner))
+            yield
             spreads = dot(narrows[part][d], to_lanes)
+            yield
             c16, bt16 = c_rows.astype(BF16)[:, :state], bt.astype(BF16)
             all_scores = dot(c16, bt16)
             values16 = values.astype(BF16)
@@ -503,6 +506,7 @@
                 both = jnp.where(keep, window, pltpu.roll(window, CHUNK, 1))
                 causal = (small_half >= small_row) if falls else (small_half <= small_row)
                 scores.append(jnp.where(causal, both, 0.0))
+            yield
             twice = c_rows + pltpu.roll(c_rows, state, 1)
             c_chunks = jnp.concatenate([twice] * (chunks * state // LANES), axis=1)
             earlier = (lane_chunk > block_chunk) if falls else (lane_chunk < block_chunk)
@@ -527,7 +531,7 @@
                     left[chunk, low * CHUNK : high * CHUNK],
                     jnp.concatenate(blocks_of[low:high], axis=0),
                 )
-                base_ref[chunk] = carried * spreads[chunk] + skip * values[chunk]
+                base_ref[index4, chunk] = carried * spreads[chunk] + skip * values[chunk]
                 for l in range(letters):
                     row = totals[i * letters + l : i * letters + l + 1]
                     row = jnp.concatenate([row] * (inner // LANES), axis=1) * decay[l]
@@ -535,6 +539,7 @@
             if own > 1:
                 fresh = dot(bt16, (values * spreads[used : used + BLOCK]).astype(BF16))
                 held = held * jnp.exp2(power_sum) + fresh
+            yield
             square = [None] * chunks
             for group in range(inner // WIDE):
                 wide = slice(group * WIDE, (group + 1) * WIDE)
@@ -556,6 +561,7 @@
                     stacked.append(
                         jnp.concatenate([chunk_values * mask for mask in head_masks], axis=0)
                     )
+                yield
                 inside = [dot(m, v) for m, v in zip(mixed, stacked)]
                 if index4 == strand:
                     gate_ref[strand, at : at + BLOCK, wide] = dot(
@@ -564,25 +570,75 @@
                 gate = gate_ref[strand, at : at + BLOCK, wide]
                 for i in range(chunks):
                     chunk = slice(i * CHUNK, (i + 1) * CHUNK)
-                    gated = (inside[i] + base_ref[chunk, wide]) * gate[chunk]
+                    gated = (inside[i] + base_ref[index4, chunk, wide]) * gate[chunk]
                     gated_ref[index4, at + i * CHUNK : at + (i + 1) * CHUNK, wide] = gated
                     part_sum = jnp.sum(gated * gated, axis=1, keepdims=True)
                     square[i] = part_sum if square[i] is None else square[i] + part_sum
             squares.append(jnp.concatenate(square, axis=0))
         squares = squares[::-1] if falls else squares
-        scales.append(lax.rsqrt(jnp.concatenate(squares, axis=0) * (1.0 / inner) + EPSILON))
-    for group in range(inner // WIDE):
-        wide = slice(group * WIDE, (group + 1) * WIDE)
-        total = 0.0
-        for param in range(2):
-            part = sum(
-                gated_ref[k, :, wide] * scales[k] for k in range(len(PASSES)) if PASSES[k][2] == param
-            )
-            total = total + part * gain_ref[param : param + 1, wide]
-        mixed_ref[:, wide] = total.astype(BF16)
-    copy = pltpu.make_async_copy(mixed_ref, mixed_hbm, out_sem)
-    copy.start()
-    copy.wait()
+        scale = lax.rsqrt(jnp.concatenate(squares, axis=0) * (1.0 / inner) + EPSILON)
+        scale_ref[index4] = jnp.broadcast_to(scale, (rows, LANES))
+
+    def run(orders):
+        live = [one_pass(index4) for index4 in orders]
+        while live:
+            live = [p for p in live if next(p, live) is not live]
+
+    for orders in ORDERS:
+        run(orders)
+    writes = []
+    for piece in range(rows // CHUNK):
+        at = slice(piece * CHUNK, (piece + 1) * CHUNK)
+        for tile in range(inner // LANES):
+            wide = slice(tile * LANES, (tile + 1) * LANES)
+            total = 0.0
+            for param in range(2):
+                part = sum(
+                    gated_ref[k, at, wide] * scale_ref[k, at]
+                    for k in range(len(PASSES))
+                    if PASSES[k][2] == param
+                )
+                total = total + part * gain_ref[param : param + 1, wide]
+            mixed_ref[at, wide] = total.astype(BF16)
+        writes += start_all(
+            [(mixed_ref.at[at], mixed_hbm.at[at])], out_sem.at[pl.ds(piece, 1)]
+        )
+    for copy in writes:
+        copy.wait()
+
+
+def join_kernel(count, *refs):
+    total = sum(count)
+    pieces, outs = refs[:total], refs[total : total + len(count)]
+    held, (in_sems, out_sems) = refs[total + len(count) : -2], refs[-2:]
+    pairs = []
+    for n, buffer in zip(count, held):
+        at = 0
+        for piece in pieces[:n]:
+            pairs.append((piece, buffer.at[pl.ds(at, piece.shape[0])]))
+            at += piece.shape[0]
+        pieces = pieces[n:]
+    for copy in start_all(pairs, in_sems):
+        copy.wait()
+    for copy in start_all(list(zip(held, outs)), out_sems):
+        copy.wait()
+
+
+def join_all(*groups):
+    shapes = [
+        ((sum(x.shape[0] for x in group), *group[0].shape[1:]), group[0].dtype) for group in groups
+    ]
+    pieces = [x for group in groups for x in group]
+    return pl.pallas_call(
+        partial(join_kernel, [len(group) for group in groups]),
+        out_shape=[jax.ShapeDtypeStruct(*shape) for shape in shapes],
+        in_specs=[pl.BlockSpec(memory_space=pl.ANY)] * len(pieces),
+        out_specs=[pl.BlockSpec(memory_space=pl.ANY)] * len(shapes),
+        scratch_shapes=[pltpu.VMEM(*shape) for shape in shapes]
+        + [pltpu.SemaphoreType.DMA((len(pieces),)), pltpu.SemaphoreType.DMA((len(shapes),))],
+        compiler_params=pltpu.CompilerParams(vmem_limit_bytes=4 * 2**20),
+        name="join",
+    )(*pieces)
 
 
 def output_kernel(depth, places, flip, here_ref, side_ref, mixed_hbm, *refs):
@@ -655,10 +711,14 @@
     while mask > 2:
         arrived = swap(line, "seq", mask)
         if mask == count // 2:
-            arrived, token_line = lax.optimization_barrier((arrived, token_line))
-            token_line = join(tokens, *token_line[::-1])
+            projected = jnp.dot(embedding, in_weight, preferred_element_type=F32).astype(BF16)
+            arrived, token_line, projected = lax.optimization_barrier(
+                (arrived, token_line, projected)
+            )
+            line, token_line = join_all((line, arrived), (tokens, *token_line[::-1]))
             tokens = [token_line] + [swap(token_line, "seq", m) for m in (1, 2, 3)]
-        line = join(line, arrived)
+        else:
+            (line,) = join_all((line, arrived))
         line_masks = line_masks + moved(line_masks, mask)
         mask //= 2
     across_plane = [swap(line, "seq", mask) for mask in (1, 2, 3)]
@@ -684,7 +744,7 @@
             conv_weight,
             conv_bias,
             norm_gain,
-            in_weight,
+            projected,
         )
         mixed.append(
             pl.pallas_call(
@@ -696,17 +756,18 @@
                 + [pltpu.VMEM(x.shape, x.dtype) for x in inputs[4:]]
                 + [
                     pltpu.VMEM((rows, inner), BF16),
-                    pltpu.VMEM((word_rows + 16, inner + LANES), BF16),
+                    pltpu.VMEM((4, word_rows + 16, inner + LANES), BF16),
                     pltpu.VMEM((2, 32, inner), BF16),
                     pltpu.VMEM((4, 24, inner), F32),
                     pltpu.VMEM((2, LANES, LANES), BF16),
                     pltpu.VMEM((letters**taps, count * rows), BF16),
                     pltpu.VMEM((4 * heads, count * rows), BF16),
-                    pltpu.VMEM((BLOCK, inner), F32),
+                    pltpu.VMEM((4, BLOCK, inner), F32),
                     pltpu.VMEM((4, rows, inner), F32),
                     pltpu.VMEM((2, rows, inner), F32),
+                    pltpu.VMEM((4, rows, LANES), F32),
                     pltpu.SemaphoreType.DMA((len(inputs),)),
-                    pltpu.SemaphoreType.DMA,
+                    pltpu.SemaphoreType.DMA((rows // CHUNK,)),
                 ],
                 compiler_params=pltpu.CompilerParams(vmem_limit_bytes=VMEM_BYTES),
                 cost_estimate=pl.CostEstimate(

time: 46.5 us -> 44 us (0.946)
  other arithmetic: 3.7 us -> 0 us
  matrix products: 0 us -> 3.58 us
  waiting for transfers between devices: 2.46 us -> 0.04 us
    concatenate x3 -> x0, other arithmetic: 3.7 us -> none  [on_device(): join = lambda *x: jnp.concatenate(x, axis=0)]
    dot_general x0 -> x1, matrix products: none -> 3.58 us  [on_device(): jnp.dot(embedding, in_weight, preferred_element_type=F32).astype(BF16)]
    ppermute x15, waiting for transfers between devices: 2.46 us -> 0.04 us  [swap(): return lax.ppermute(x, axis, [(i, i ^ mask) for i in range(count)])]
    pallas_call x1, Pallas kernels: 16.2 us -> 14.4 us  [on_device(): pl.pallas_call(partial(mixer_kernel, letters, taps, state, count), out_sh...]
    pallas_call x0 -> x2, Pallas kernels: none -> 1.47 us  [join_all(): pl.pallas_call(partial(join_kernel, [len(group) for group in groups]), ou...]
  transfers between devices with their start and end apart: 15 -> 15, of which waited for: 3 -> 0; matrix products, arithmetic and copies ran while one was open for 6% -> 8% of each run, Pallas kernels for 41% -> 41%
where the time goes in v4:
time: 44 us; the launch traced here: 43.7 us
  Pallas kernels  21.1 us (48%)
  starting transfers between devices  18.2 us (41%)
  matrix products  3.58 us (8%)
  local copies, waits for them, and re-layouts  0.7 us (2%)
    ppermute x15, starting transfers between devices, swap(): return lax.ppermute(x, axis, [(i, i ^ mask) for i in range(count)])  18.2 us
    pallas_call x1, Pallas kernels, on_device(): pl.pallas_call(partial(mixer_kernel, letters, taps, state, count), out_sh...  14.4 us
    pallas_call x2, Pallas kernels, project(): pl.pallas_call(partial(output_kernel, depth, places, flip), out_shape=jax...  5.18 us
    dot_general x1, matrix products, on_device(): jnp.dot(embedding, in_weight, preferred_element_type=F32).astype(BF16)  3.58 us
    pallas_call x2, Pallas kernels, join_all(): pl.pallas_call(partial(join_kernel, [len(group) for group in groups]), ou...  1.47 us
  transfers between devices with their start and end apart: 15, of which 0 were waited for; matrix products, arithmetic and copies ran while one was open for 8% of the time, Pallas kernels for 41%

profile of v4, /device:TPU:0, one launch (start us, length us, event | category | flops | bytes accessed | tf_op | source)
XLA Modules:
  0.0 43.7 jit_solution(8239835248591927583)
XLA Ops:
  0.0 0.0 copy-start.1
  0.0 0.0 copy-start
  0.0 5.0 %collective-permute-start.1 = (s32[1,1,256]{2,1,0:T(1,128)}, s32[1,1,256]{2,1,0:T(1,128)S(1)}, u32[]{:S(2)}, u32[]{:S(2)}) collective-permute-start(s32[1,1,256]{2,1,0:T(1,128)} %bitcast.15), channel_id=1, source_target_pairs={{0,12},{1,13},{2,14},{3,15},{4,8},{5,9},{6,10},{7,11},{8,4},{9,5},... | collective-permute-start | bytes 3080 | tf_op jit(solution)/shard_map/ppermute | solution.py:665
  5.1 0.0 collective-permute-start.2
  5.1 0.6 %collective-permute-start.3 = (s32[1,1,256]{2,1,0:T(1,128)}, s32[1,1,256]{2,1,0:T(1,128)S(1)}, u32[]{:S(2)}, u32[]{:S(2)}) collective-permute-start(s32[1,1,256]{2,1,0:T(1,128)} %bitcast.17), channel_id=1, source_target_pairs={{0,4},{1,5},{2,6},{3,7},{4,0},{5,1},{6,2},{7,3},{8,12},{9,13},{10,... | collective-permute-start | bytes 3080 | tf_op jit(solution)/shard_map/ppermute | solution.py:665
  5.7 2.3 %collective-permute-start = (bf16[1,64,512]{2,1,0:T(8,128)(2,1)}, bf16[1,64,512]{2,1,0:T(8,128)(2,1)S(1)}, u32[]{:S(2)}, u32[]{:S(2)}) collective-permute-start(bf16[1,64,512]{2,1,0:T(8,128)(2,1)} %bitcast.13), channel_id=1, source_target_pairs={{0,8},{1,9},{2,10},{3,11},{4,12},{5,13},{6,14},{7,15},{8,0},{9,1},... | collective-permute-start | bytes 196616 | tf_op jit(solution)/shard_map/ppermute | solution.py:665
  8.0 3.6 %convolution_convert_fusion.refs_15_ = bf16[4,2176]{1,0:T(4,128)(2,1)} fusion(bf16[4,1024]{1,0:T(4,128)(2,1)} %refs_5_.1, bf16[1024,2176]{1,0:T(8,128)(2,1)} %param.18), kind=kOutput, calls=%fused_computation | convolution fusion | flops 17834496 | bytes 4482048 | tf_op jit(solution)/shard_map/dot_general | solution.py:714
  11.6 0.0 collective-permute-done.1.refs_5_
  11.6 0.0 collective-permute-done.2.refs_4_
  11.6 0.0 collective-permute-done.3.refs_3_
  11.6 0.0 collective-permute-done.refs_1_
  11.6 0.0 copy-done.1
  11.6 0.0 copy-done
  11.6 0.4 join.2
  12.0 2.1 %collective-permute-start.4 = (bf16[2,64,512]{2,1,0:T(8,128)(2,1)S(1)}, bf16[2,64,512]{2,1,0:T(8,128)(2,1)S(1)}, u32[]{:S(2)}, u32[]{:S(2)}) collective-permute-start(bf16[2,64,512]{2,1,0:T(8,128)(2,1)S(1)} %get-tuple-element.21.refs_0_), channel_id=1, source_target_pairs={{0,4},{1,5},{2,6},{3,7},{4,0},{5,1},{6,2},{7,3},{8,12},{9,13},{10,... | collective-permute-start | bytes 393224 | tf_op jit(solution)/shard_map/ppermute | solution.py:665
  14.1 0.0 copy-start.2
  14.1 1.5 %collective-permute-start.8 = (s32[4,1,256]{2,0,1:T(4,128)S(1)}, s32[4,1,256]{2,0,1:T(4,128)S(1)}, u32[]{:S(2)}, u32[]{:S(2)}) collective-permute-start(s32[4,1,256]{2,0,1:T(4,128)S(1)} %copy.23), channel_id=1, source_target_pairs={{0,1},{1,0},{2,3},{3,2},{4,5},{5,4},{6,7},{7,6},{8,9},{9,8},{10,11... | collective-permute-start | bytes 12296 | tf_op jit(solution)/shard_map/ppermute | solution.py:665
  15.6 1.5 %collective-permute-start.9 = (s32[4,1,256]{2,0,1:T(4,128)S(1)}, s32[4,1,256]{2,0,1:T(4,128)S(1)}, u32[]{:S(2)}, u32[]{:S(2)}) collective-permute-start(s32[4,1,256]{2,0,1:T(4,128)S(1)} %copy.23), channel_id=1, source_target_pairs={{0,2},{1,3},{2,0},{3,1},{4,6},{5,7},{6,4},{7,5},{8,10},{9,11},{10,... | collective-permute-start | bytes 12296 | tf_op jit(solution)/shard_map/ppermute | solution.py:665
  17.1 0.5 %collective-permute-start.10 = (s32[4,1,256]{2,0,1:T(4,128)S(1)}, s32[4,1,256]{2,0,1:T(4,128)S(1)}, u32[]{:S(2)}, u32[]{:S(2)}) collective-permute-start(s32[4,1,256]{2,0,1:T(4,128)S(1)} %copy.23), channel_id=1, source_target_pairs={{0,3},{1,2},{2,1},{3,0},{4,7},{5,6},{6,5},{7,4},{8,11},{9,10},{10,... | collective-permute-start | bytes 12296 | tf_op jit(solution)/shard_map/ppermute | solution.py:665
  17.6 0.0 collective-permute-done.4.refs_1_
  17.6 1.0 %join.3.refs_0_ = bf16[4,64,512]{2,1,0:T(8,128)(2,1)} custom-call(bf16[2,64,512]{2,1,0:T(8,128)(2,1)S(1)} %get-tuple-element.21.refs_0_, bf16[2,64,512]{2,1,0:T(8,128)(2,1)S(1)} %collective-permute-done.4.refs_1_), custom_call_target="tpu_custom_call" | custom-call | tf_op jit(solution)/shard_map/join/pallas_call | solution.py:632
  18.7 0.0 copy-done.2
  18.7 1.6 %collective-permute-start.5 = (bf16[4,64,512]{2,1,0:T(8,128)(2,1)}, bf16[4,64,512]{2,1,0:T(8,128)(2,1)}, u32[]{:S(2)}, u32[]{:S(2)}) collective-permute-start(bf16[4,64,512]{2,1,0:T(8,128)(2,1)} %join.3.refs_0_), channel_id=1, source_target_pairs={{0,1},{1,0},{2,3},{3,2},{4,5},{5,4},{6,7},{7,6},{8,9},{9,8},{10,11... | collective-permute-start | bytes 786440 | tf_op jit(solution)/shard_map/ppermute | solution.py:665
  20.2 1.5 %collective-permute-start.6 = (bf16[4,64,512]{2,1,0:T(8,128)(2,1)}, bf16[4,64,512]{2,1,0:T(8,128)(2,1)}, u32[]{:S(2)}, u32[]{:S(2)}) collective-permute-start(bf16[4,64,512]{2,1,0:T(8,128)(2,1)} %join.3.refs_0_), channel_id=1, source_target_pairs={{0,2},{1,3},{2,0},{3,1},{4,6},{5,7},{6,4},{7,5},{8,10},{9,11},{10,... | collective-permute-start | bytes 786440 | tf_op jit(solution)/shard_map/ppermute | solution.py:665
  21.8 0.0 collective-permute-done.8
  21.8 0.0 copy-start.3
  21.8 0.5 %collective-permute-start.7 = (bf16[4,64,512]{2,1,0:T(8,128)(2,1)}, bf16[4,64,512]{2,1,0:T(8,128)(2,1)}, u32[]{:S(2)}, u32[]{:S(2)}) collective-permute-start(bf16[4,64,512]{2,1,0:T(8,128)(2,1)} %join.3.refs_0_), channel_id=1, source_target_pairs={{0,3},{1,2},{2,1},{3,0},{4,7},{5,6},{6,5},{7,4},{8,11},{9,10},{10,... | collective-permute-start | bytes 786440 | tf_op jit(solution)/shard_map/ppermute | solution.py:665
  22.2 0.0 collective-permute-done.9
  22.3 0.0 copy-start.4
  22.3 0.0 collective-permute-done.10
  22.3 0.1 copy-done.3
  22.4 0.0 copy-start.5
  22.4 0.5 %copy-done.4 = s32[4,1,256]{2,0,1:T(4,128)} copy-done((s32[4,1,256]{2,0,1:T(4,128)}, s32[4,1,256]{2,0,1:T(4,128)S(1)}, u32[]{:S(2)}) %copy-start.4) | copy-done | bytes 4120
  22.8 0.1 copy-done.5
  22.9 14.4 %mixer.1.mixed_hbm = bf16[256,1024]{1,0:T(8,128)(2,1)} custom-call(s32[1]{0:T(128)} %bitcast.here_ref, s32[4]{0:T(128)} %complement_ref.1, s32[4,256]{1,0:T(4,128)} %bitcast.19, s32[4,256]{1,0:T(4,128)} %bitcast.21, s32[4,256]{1,0:T(4,128)} %bitcast.22, s32[4,256]{1,0:T(4,128)} %bitcast.23, bf16[16,1024]{1,0:T(8,128)(2,1)} %constant.15.clone.refs_4_, ...), custom_call_target="tpu_custom_call" | custom-call | flops 10000000000 | bytes 52428800 | tf_op jit(solution)/shard_map/mixer/pallas_call | solution.py:750
  37.4 0.0 collective-permute-done.5.refs_1_
  37.4 0.0 collective-permute-done.6.refs_2_
  37.4 0.0 collective-permute-done.7.refs_3_
  37.4 0.1 collective-permute-start.11
  37.5 0.5 %collective-permute-start.12 = (bf16[4,64,512]{2,1,0:T(8,128)(2,1)}, bf16[4,64,512]{2,1,0:T(8,128)(2,1)}, u32[]{:S(2)}, u32[]{:S(2)}) collective-permute-start(bf16[4,64,512]{2,1,0:T(8,128)(2,1)} %collective-permute-done.5.refs_1_), channel_id=1, source_target_pairs={{0,16},{16,0},{1,17},{17,1},{2,18},{18,2},{3,19},{19,3},{4,20},{20... | collective-permute-start | bytes 786440 | tf_op jit(solution)/shard_map/ppermute | solution.py:665
  38.0 0.1 collective-permute-start.13
  38.1 0.4 collective-permute-start.14
  38.5 2.6 %output.2.refs_4_ = bf16[256,1024]{1,0:T(8,128)(2,1)} custom-call(s32[1]{0:T(128)} %bitcast.here_ref, s32[1]{0:T(128)} %bitcast.1.side_ref, bf16[256,1024]{1,0:T(8,128)(2,1)} %mixer.1.mixed_hbm, bf16[4,64,512]{2,1,0:T(8,128)(2,1)} %join.3.refs_0_, bf16[4,64,512]{2,1,0:T(8,128)(2,1)} %collective-permute-done.5.refs_1_, ...), custom_call_target="tpu_custom_call" | custom-call | flops 268435456 | bytes 4194304 | tf_op jit(solution)/shard_map/output/pallas_call | solution.py:789
  41.1 0.0 collective-permute-done.11.refs_0_
  41.1 0.0 collective-permute-done.12.refs_1_
  41.1 0.0 collective-permute-done.13.refs_2_
  41.1 0.0 collective-permute-done.14.refs_3_
  41.1 2.6 %output.3 = bf16[256,1024]{1,0:T(8,128)(2,1)} custom-call(s32[1]{0:T(128)} %bitcast.here_ref, s32[1]{0:T(128)} %bitcast.1.side_ref, bf16[256,1024]{1,0:T(8,128)(2,1)} %mixer.1.mixed_hbm, bf16[4,64,512]{2,1,0:T(8,128)(2,1)} %collective-permute-done.11.refs_0_, bf16[4,64,512]{2,1,0:T(8,128)(2,1)} %collective-permute-done.12.refs_1_, ...), custom_call_target="tpu_custom_call", output_to_operand_aliasing={{}: (7, {})} | custom-call | flops 268435456 | bytes 4194304 | tf_op jit(solution)/shard_map/output/pallas_call | solution.py:789
  (1 shorter events, 0.0 us)
Async XLA Ops:
  0.0 11.6 %copy-start.1 = (s32[1,256]{1,0:T(1,128)S(1)}, s32[1,256]{1,0:T(1,128)}, u32[]{:S(2)}) copy-start(s32[1,256]{1,0:T(1,128)} %param.15) | copy-start | bytes 3076
  0.0 11.6 %copy-start = (bf16[64,512]{1,0:T(8,128)(2,1)S(1)}, bf16[64,512]{1,0:T(8,128)(2,1)}, u32[]{:S(2)}) copy-start(bf16[64,512]{1,0:T(8,128)(2,1)} %param.26) | copy-start | bytes 196612
  0.0 11.6 %collective-permute-start.1 = (s32[1,1,256]{2,1,0:T(1,128)}, s32[1,1,256]{2,1,0:T(1,128)S(1)}, u32[]{:S(2)}, u32[]{:S(2)}) collective-permute-start(s32[1,1,256]{2,1,0:T(1,128)} %bitcast.15), channel_id=1, source_target_pairs={{0,12},{1,13},{2,14},{3,15},{4,8},{5,9},{6,10},{7,11},{8,4},{9,5},... | collective-permute-start | bytes 3080 | tf_op jit(solution)/shard_map/ppermute | solution.py:665
  5.1 6.5 %collective-permute-start.2 = (s32[1,1,256]{2,1,0:T(1,128)}, s32[1,1,256]{2,1,0:T(1,128)S(1)}, u32[]{:S(2)}, u32[]{:S(2)}) collective-permute-start(s32[1,1,256]{2,1,0:T(1,128)} %bitcast.16), channel_id=1, source_target_pairs={{0,8},{1,9},{2,10},{3,11},{4,12},{5,13},{6,14},{7,15},{8,0},{9,1},... | collective-permute-start | bytes 3080 | tf_op jit(solution)/shard_map/ppermute | solution.py:665
  5.1 6.5 %collective-permute-start.3 = (s32[1,1,256]{2,1,0:T(1,128)}, s32[1,1,256]{2,1,0:T(1,128)S(1)}, u32[]{:S(2)}, u32[]{:S(2)}) collective-permute-start(s32[1,1,256]{2,1,0:T(1,128)} %bitcast.17), channel_id=1, source_target_pairs={{0,4},{1,5},{2,6},{3,7},{4,0},{5,1},{6,2},{7,3},{8,12},{9,13},{10,... | collective-permute-start | bytes 3080 | tf_op jit(solution)/shard_map/ppermute | solution.py:665
  5.7 5.9 %collective-permute-start = (bf16[1,64,512]{2,1,0:T(8,128)(2,1)}, bf16[1,64,512]{2,1,0:T(8,128)(2,1)S(1)}, u32[]{:S(2)}, u32[]{:S(2)}) collective-permute-start(bf16[1,64,512]{2,1,0:T(8,128)(2,1)} %bitcast.13), channel_id=1, source_target_pairs={{0,8},{1,9},{2,10},{3,11},{4,12},{5,13},{6,14},{7,15},{8,0},{9,1},... | collective-permute-start | bytes 196616 | tf_op jit(solution)/shard_map/ppermute | solution.py:665
  12.0 5.6 %collective-permute-start.4 = (bf16[2,64,512]{2,1,0:T(8,128)(2,1)S(1)}, bf16[2,64,512]{2,1,0:T(8,128)(2,1)S(1)}, u32[]{:S(2)}, u32[]{:S(2)}) collective-permute-start(bf16[2,64,512]{2,1,0:T(8,128)(2,1)S(1)} %get-tuple-element.21.refs_0_), channel_id=1, source_target_pairs={{0,4},{1,5},{2,6},{3,7},{4,0},{5,1},{6,2},{7,3},{8,12},{9,13},{10,... | collective-permute-start | bytes 393224 | tf_op jit(solution)/shard_map/ppermute | solution.py:665
  14.1 4.6 %copy-start.2 = (s32[4,1,256]{2,0,1:T(4,128)}, s32[4,1,256]{2,0,1:T(4,128)S(1)}, u32[]{:S(2)}) copy-start(s32[4,1,256]{2,0,1:T(4,128)S(1)} %copy.23) | copy-start | bytes 12292
  14.1 7.6 %collective-permute-start.8 = (s32[4,1,256]{2,0,1:T(4,128)S(1)}, s32[4,1,256]{2,0,1:T(4,128)S(1)}, u32[]{:S(2)}, u32[]{:S(2)}) collective-permute-start(s32[4,1,256]{2,0,1:T(4,128)S(1)} %copy.23), channel_id=1, source_target_pairs={{0,1},{1,0},{2,3},{3,2},{4,5},{5,4},{6,7},{7,6},{8,9},{9,8},{10,11... | collective-permute-start | bytes 12296 | tf_op jit(solution)/shard_map/ppermute | solution.py:665
  15.6 6.6 %collective-permute-start.9 = (s32[4,1,256]{2,0,1:T(4,128)S(1)}, s32[4,1,256]{2,0,1:T(4,128)S(1)}, u32[]{:S(2)}, u32[]{:S(2)}) collective-permute-start(s32[4,1,256]{2,0,1:T(4,128)S(1)} %copy.23), channel_id=1, source_target_pairs={{0,2},{1,3},{2,0},{3,1},{4,6},{5,7},{6,4},{7,5},{8,10},{9,11},{10,... | collective-permute-start | bytes 12296 | tf_op jit(solution)/shard_map/ppermute | solution.py:665
  17.1 5.1 %collective-permute-start.10 = (s32[4,1,256]{2,0,1:T(4,128)S(1)}, s32[4,1,256]{2,0,1:T(4,128)S(1)}, u32[]{:S(2)}, u32[]{:S(2)}) collective-permute-start(s32[4,1,256]{2,0,1:T(4,128)S(1)} %copy.23), channel_id=1, source_target_pairs={{0,3},{1,2},{2,1},{3,0},{4,7},{5,6},{6,5},{7,4},{8,11},{9,10},{10,... | collective-permute-start | bytes 12296 | tf_op jit(solution)/shard_map/ppermute | solution.py:665
  18.7 18.7 %collective-permute-start.5 = (bf16[4,64,512]{2,1,0:T(8,128)(2,1)}, bf16[4,64,512]{2,1,0:T(8,128)(2,1)}, u32[]{:S(2)}, u32[]{:S(2)}) collective-permute-start(bf16[4,64,512]{2,1,0:T(8,128)(2,1)} %join.3.refs_0_), channel_id=1, source_target_pairs={{0,1},{1,0},{2,3},{3,2},{4,5},{5,4},{6,7},{7,6},{8,9},{9,8},{10,11... | collective-permute-start | bytes 786440 | tf_op jit(solution)/shard_map/ppermute | solution.py:665
  20.2 17.2 %collective-permute-start.6 = (bf16[4,64,512]{2,1,0:T(8,128)(2,1)}, bf16[4,64,512]{2,1,0:T(8,128)(2,1)}, u32[]{:S(2)}, u32[]{:S(2)}) collective-permute-start(bf16[4,64,512]{2,1,0:T(8,128)(2,1)} %join.3.refs_0_), channel_id=1, source_target_pairs={{0,2},{1,3},{2,0},{3,1},{4,6},{5,7},{6,4},{7,5},{8,10},{9,11},{10,... | collective-permute-start | bytes 786440 | tf_op jit(solution)/shard_map/ppermute | solution.py:665
  21.8 0.6 %copy-start.3 = (s32[4,1,256]{2,0,1:T(4,128)}, s32[4,1,256]{2,0,1:T(4,128)S(1)}, u32[]{:S(2)}) copy-start(s32[4,1,256]{2,0,1:T(4,128)S(1)} %collective-permute-done.8) | copy-start | bytes 12292
  21.8 15.6 %collective-permute-start.7 = (bf16[4,64,512]{2,1,0:T(8,128)(2,1)}, bf16[4,64,512]{2,1,0:T(8,128)(2,1)}, u32[]{:S(2)}, u32[]{:S(2)}) collective-permute-start(bf16[4,64,512]{2,1,0:T(8,128)(2,1)} %join.3.refs_0_), channel_id=1, source_target_pairs={{0,3},{1,2},{2,1},{3,0},{4,7},{5,6},{6,5},{7,4},{8,11},{9,10},{10,... | collective-permute-start | bytes 786440 | tf_op jit(solution)/shard_map/ppermute | solution.py:665
  22.3 0.6 %copy-start.4 = (s32[4,1,256]{2,0,1:T(4,128)}, s32[4,1,256]{2,0,1:T(4,128)S(1)}, u32[]{:S(2)}) copy-start(s32[4,1,256]{2,0,1:T(4,128)S(1)} %collective-permute-done.9) | copy-start | bytes 12292
  22.4 0.6 %copy-start.5 = (s32[4,1,256]{2,0,1:T(4,128)}, s32[4,1,256]{2,0,1:T(4,128)S(1)}, u32[]{:S(2)}) copy-start(s32[4,1,256]{2,0,1:T(4,128)S(1)} %collective-permute-done.10) | copy-start | bytes 12292
  37.4 3.7 %collective-permute-start.11 = (bf16[4,64,512]{2,1,0:T(8,128)(2,1)}, bf16[4,64,512]{2,1,0:T(8,128)(2,1)}, u32[]{:S(2)}, u32[]{:S(2)}) collective-permute-start(bf16[4,64,512]{2,1,0:T(8,128)(2,1)} %join.3.refs_0_), channel_id=1, source_target_pairs={{0,16},{16,0},{1,17},{17,1},{2,18},{18,2},{3,19},{19,3},{4,20},{20... | collective-permute-start | bytes 786440 | tf_op jit(solution)/shard_map/ppermute | solution.py:665
  37.5 3.6 %collective-permute-start.12 = (bf16[4,64,512]{2,1,0:T(8,128)(2,1)}, bf16[4,64,512]{2,1,0:T(8,128)(2,1)}, u32[]{:S(2)}, u32[]{:S(2)}) collective-permute-start(bf16[4,64,512]{2,1,0:T(8,128)(2,1)} %collective-permute-done.5.refs_1_), channel_id=1, source_target_pairs={{0,16},{16,0},{1,17},{17,1},{2,18},{18,2},{3,19},{19,3},{4,20},{20... | collective-permute-start | bytes 786440 | tf_op jit(solution)/shard_map/ppermute | solution.py:665
  38.0 3.1 %collective-permute-start.13 = (bf16[4,64,512]{2,1,0:T(8,128)(2,1)}, bf16[4,64,512]{2,1,0:T(8,128)(2,1)}, u32[]{:S(2)}, u32[]{:S(2)}) collective-permute-start(bf16[4,64,512]{2,1,0:T(8,128)(2,1)} %collective-permute-done.6.refs_2_), channel_id=1, source_target_pairs={{0,16},{16,0},{1,17},{17,1},{2,18},{18,2},{3,19},{19,3},{4,20},{20... | collective-permute-start | bytes 786440 | tf_op jit(solution)/shard_map/ppermute | solution.py:665
  38.1 3.1 %collective-permute-start.14 = (bf16[4,64,512]{2,1,0:T(8,128)(2,1)}, bf16[4,64,512]{2,1,0:T(8,128)(2,1)}, u32[]{:S(2)}, u32[]{:S(2)}) collective-permute-start(bf16[4,64,512]{2,1,0:T(8,128)(2,1)} %collective-permute-done.7.refs_3_), channel_id=1, source_target_pairs={{0,16},{16,0},{1,17},{17,1},{2,18},{18,2},{3,19},{19,3},{4,20},{20... | collective-permute-start | bytes 786440 | tf_op jit(solution)/shard_map/ppermute | solution.py:665

commit v5 on v4

--- a/solution.py
+++ b/solution.py
@@ -16,7 +16,7 @@
 LOG2E = 1.4426950408889634
 EPSILON = 1e-05
 ORDERS = ((0, 1), (2, 3))
-VMEM_BYTES = 64 * 2**20
+VMEM_BYTES = 36 * 2**20
 F32 = jnp.float32
 BF16 = jnp.bfloat16
 
@@ -134,22 +134,8 @@
     complement_ref,
     *refs,
 ):
-    token_hbms, refs = refs[:4], refs[4:]
+    token_refs, refs = refs[:4], refs[4:]
     (
-        spread_hbm,
-        embedding_hbm,
-        step_weight_hbm,
-        step_bias_hbm,
-        rate_hbm,
-        skip_hbm,
-        last_hbm,
-        select_hbm,
-        conv_weight_hbm,
-        conv_bias_hbm,
-        gain_hbm,
-        projected_hbm,
-        mixed_hbm,
-        tokens_ref,
         spread_ref,
         embedding_ref,
         step_weight_ref,
@@ -173,29 +159,9 @@
         gated_ref,
         gate_ref,
         scale_ref,
-        in_sems,
-        out_sem,
     ) = refs
-    reads = start_all(
-        (
-            *((hbm, tokens_ref.at[k]) for k, hbm in enumerate(token_hbms)),
-            (spread_hbm, spread_ref),
-            (embedding_hbm, embedding_ref),
-            (step_weight_hbm, step_weight_ref),
-            (step_bias_hbm, step_bias_ref),
-            (rate_hbm, rate_ref),
-            (skip_hbm, skip_ref),
-            (last_hbm, last_ref),
-            (select_hbm, select_ref),
-            (conv_weight_hbm, conv_weight_ref),
-            (conv_bias_hbm, conv_bias_ref),
-            (gain_hbm, gain_ref),
-            (projected_hbm, projected_ref),
-        ),
-        in_sems,
-    )
     here = here_ref[0]
-    rows = tokens_ref.shape[2]
+    rows = mixed_ref.shape[0]
     own = rows // BLOCK
     blocks = count * own
     heads, inner = spread_ref.shape
@@ -207,9 +173,7 @@
     as_bf16 = lambda mask: jnp.where(mask, 1.0, 0.0).astype(BF16)
     complement = lambda letter: complement_ref[letter]
 
-    for copy in reads:
-        copy.wait()
-    tokens16 = jnp.concatenate([tokens_ref[k] for k in range(4)], axis=0).astype(F32).astype(BF16)
+    tokens16 = jnp.concatenate([ref[...] for ref in token_refs], axis=0).astype(F32).astype(BF16)
     place, target = iota((blocks, count), 1), iota((blocks, count), 0)
     source = here ^ (place % (count // 4) * 4 + place // (count // 4))
     around = jnp.zeros((3 * blocks, BLOCK), F32)
@@ -586,7 +550,6 @@
 
     for orders in ORDERS:
         run(orders)
-    writes = []
     for piece in range(rows // CHUNK):
         at = slice(piece * CHUNK, (piece + 1) * CHUNK)
         for tile in range(inner // LANES):
@@ -600,11 +563,6 @@
                 )
                 total = total + part * gain_ref[param : param + 1, wide]
             mixed_ref[at, wide] = total.astype(BF16)
-        writes += start_all(
-            [(mixed_ref.at[at], mixed_hbm.at[at])], out_sem.at[pl.ds(piece, 1)]
-        )
-    for copy in writes:
-        copy.wait()
 
 
 def join_kernel(count, *refs):
@@ -641,23 +599,26 @@
     )(*pieces)
 
 
-def output_kernel(depth, places, flip, here_ref, side_ref, mixed_hbm, *refs):
+def output_kernel(depth, places, flip, here_ref, side_ref, mixed_ref, *refs):
     pieces = refs[: len(places)]
-    out_hbm, weight_ref, mixed_ref, out_ref, sem, out_sem = refs[-6:]
+    out_hbm, weight_ref, out_ref, out_sem = refs[-4:]
     here, side = here_ref[0], side_ref[0]
-    pairs = [(mixed_hbm, mixed_ref)]
     for piece, masks in zip(pieces, places):
         for k, mask in enumerate(masks):
             row = pl.multiple_of((here ^ mask) * depth, depth)
-            pairs.append((piece.at[k], weight_ref.at[pl.ds(row, depth)]))
-    for copy in start_all(pairs, sem):
+            weight_ref[pl.ds(row, depth), :] = piece[k]
+    rows, columns = out_ref.shape
+    lane = pl.multiple_of((side ^ flip) * columns, columns)
+    copies = []
+    for part in range(rows // LANES):
+        at = slice(part * LANES, (part + 1) * LANES)
+        out_ref[at] = dot(mixed_ref[at], weight_ref[...]).astype(BF16)
+        copies += start_all(
+            [(out_ref.at[at], out_hbm.at[pl.ds(part * LANES, LANES), pl.ds(lane, columns)])],
+            out_sem.at[pl.ds(part, 1)],
+        )
+    for copy in copies:
         copy.wait()
-    out_ref[...] = dot(mixed_ref[...], weight_ref[...]).astype(BF16)
-    columns = out_ref.shape[1]
-    lane = pl.multiple_of((side ^ flip) * columns, columns)
-    copy = pltpu.make_async_copy(out_ref, out_hbm.at[:, pl.ds(lane, columns)], out_sem)
-    copy.start()
-    copy.wait()
 
 
 def swap(x, axis, mask):
@@ -750,12 +711,9 @@
             pl.pallas_call(
                 partial(mixer_kernel, letters, taps, state, count),
                 out_shape=jax.ShapeDtypeStruct((rows, inner), BF16),
-                in_specs=[smem(), smem()] + [hbm()] * len(inputs),
-                out_specs=hbm(),
-                scratch_shapes=[pltpu.VMEM((4, *inputs[0].shape), jnp.int32)]
-                + [pltpu.VMEM(x.shape, x.dtype) for x in inputs[4:]]
-                + [
-                    pltpu.VMEM((rows, inner), BF16),
+                in_specs=[smem(), smem()] + [vmem()] * len(inputs),
+                out_specs=vmem(),
+                scratch_shapes=[
                     pltpu.VMEM((4, word_rows + 16, inner + LANES), BF16),
                     pltpu.VMEM((2, 32, inner), BF16),
                     pltpu.VMEM((4, 24, inner), F32),
@@ -766,8 +724,6 @@
                     pltpu.VMEM((4, rows, inner), F32),
                     pltpu.VMEM((2, rows, inner), F32),
                     pltpu.VMEM((4, rows, LANES), F32),
-                    pltpu.SemaphoreType.DMA((len(inputs),)),
-                    pltpu.SemaphoreType.DMA((rows // CHUNK,)),
                 ],
                 compiler_params=pltpu.CompilerParams(vmem_limit_bytes=VMEM_BYTES),
                 cost_estimate=pl.CostEstimate(
@@ -789,17 +745,17 @@
         return pl.pallas_call(
             partial(output_kernel, depth, places, flip),
             out_shape=jax.ShapeDtypeStruct((rows, columns * sides), BF16),
-            in_specs=[smem(), smem()] + [hbm()] * (len(operands) - 2),
+            in_specs=[smem(), smem()]
+            + [vmem()] * (1 + len(found))
+            + [hbm()] * (out is not None),
             out_specs=hbm(),
             scratch_shapes=[
                 pltpu.VMEM((depth * count, columns), BF16),
-                pltpu.VMEM((rows, inner), BF16),
                 pltpu.VMEM((rows, columns), BF16),
-                pltpu.SemaphoreType.DMA((count + 1,)),
-                pltpu.SemaphoreType.DMA,
+                pltpu.SemaphoreType.DMA((rows // LANES,)),
             ],
             input_output_aliases={} if out is None else {len(operands) - 1: 0},
-            compiler_params=pltpu.CompilerParams(vmem_limit_bytes=VMEM_BYTES),
+            compiler_params=pltpu.CompilerParams(vmem_limit_bytes=8 * 2**20),
             cost_estimate=pl.CostEstimate(
                 flops=2 * rows * inner * columns, bytes_accessed=2**22, transcendentals=0
             ),

time: 44 us -> 38 us (0.86)
  Pallas kernels: 21.1 us -> 15.6 us
  waiting for transfers between devices: 0.04 us -> 0.75 us
  local copies, waits for them, and re-layouts: 0.7 us -> 0.06 us
  matrix products: 3.58 us -> 2.96 us
    pallas_call x2, Pallas kernels: 5.18 us -> 2.39 us  [project(): pl.pallas_call(partial(output_kernel, depth, places, flip), out_shape=jax...]
    pallas_call x1, Pallas kernels: 14.4 us -> 12.5 us  [on_device(): pl.pallas_call(partial(mixer_kernel, letters, taps, state, count), out_sh...]
    ppermute x15, waiting for transfers between devices: 0.04 us -> 0.75 us  [swap(): return lax.ppermute(x, axis, [(i, i ^ mask) for i in range(count)])]
    pallas_call x2, Pallas kernels: 1.47 us -> 0.78 us  [join_all(): pl.pallas_call(partial(join_kernel, [len(group) for group in groups]), ou...]
    unnamed x13 -> x29, local copies, waits for them, and re-layouts: 0.7 us -> 0.06 us
    dot_general x1, matrix products: 3.58 us -> 2.96 us  [on_device(): jnp.dot(embedding, in_weight, preferred_element_type=F32).astype(BF16)]
  transfers between devices with their start and end apart: 15 -> 15, of which waited for: 0 -> 3; matrix products, arithmetic and copies ran while one was open for 8% -> 8% of each run, Pallas kernels for 41% -> 37%
where the time goes in v5:
time: 38 us; the launch traced here: 37.9 us
  starting transfers between devices  18.2 us (48%)
  Pallas kernels  15.6 us (41%)
  matrix products  2.96 us (8%)
  waiting for transfers between devices  0.75 us (2%)
    ppermute x15, starting transfers between devices, swap(): return lax.ppermute(x, axis, [(i, i ^ mask) for i in range(count)])  18.2 us
    pallas_call x1, Pallas kernels, on_device(): pl.pallas_call(partial(mixer_kernel, letters, taps, state, count), out_sh...  12.5 us
    dot_general x1, matrix products, on_device(): jnp.dot(embedding, in_weight, preferred_element_type=F32).astype(BF16)  2.96 us
    pallas_call x2, Pallas kernels, project(): pl.pallas_call(partial(output_kernel, depth, places, flip), out_shape=jax...  2.39 us
    pallas_call x2, Pallas kernels, join_all(): pl.pallas_call(partial(join_kernel, [len(group) for group in groups]), ou...  0.78 us
  transfers between devices with their start and end apart: 15, of which 3 were waited for; matrix products, arithmetic and copies ran while one was open for 8% of the time, Pallas kernels for 37%

profile of v5, /device:TPU:0, one launch (start us, length us, event | category | flops | bytes accessed | tf_op | source)
XLA Modules:
  0.0 37.9 jit_solution(8483090492426559568)
XLA Ops:
  0.0 0.0 copy-start.1
  0.0 0.0 copy-start.4
  0.0 0.0 copy-start.10
  0.0 0.0 copy-start.3
  0.1 0.0 copy-start.5
  0.1 0.0 copy-start.7
  0.1 0.0 copy-start.8
  0.1 0.0 copy-start.9
  0.1 0.0 copy-start.6
  0.1 5.1 %collective-permute-start.1 = (s32[1,1,256]{2,1,0:T(1,128)}, s32[1,1,256]{2,1,0:T(1,128)S(1)}, u32[]{:S(2)}, u32[]{:S(2)}) collective-permute-start(s32[1,1,256]{2,1,0:T(1,128)} %bitcast.16), channel_id=1, source_target_pairs={{0,12},{1,13},{2,14},{3,15},{4,8},{5,9},{6,10},{7,11},{8,4},{9,5},... | collective-permute-start | bytes 3080 | tf_op jit(solution)/shard_map/ppermute | solution.py:626
  5.2 0.0 collective-permute-start.2
  5.2 0.6 %collective-permute-start.3 = (s32[1,1,256]{2,1,0:T(1,128)}, s32[1,1,256]{2,1,0:T(1,128)S(1)}, u32[]{:S(2)}, u32[]{:S(2)}) collective-permute-start(s32[1,1,256]{2,1,0:T(1,128)} %bitcast.18), channel_id=1, source_target_pairs={{0,4},{1,5},{2,6},{3,7},{4,0},{5,1},{6,2},{7,3},{8,12},{9,13},{10,... | collective-permute-start | bytes 3080 | tf_op jit(solution)/shard_map/ppermute | solution.py:626
  5.9 2.3 %collective-permute-start = (bf16[1,64,512]{2,1,0:T(8,128)(2,1)}, bf16[1,64,512]{2,1,0:T(8,128)(2,1)S(1)}, u32[]{:S(2)}, u32[]{:S(2)}) collective-permute-start(bf16[1,64,512]{2,1,0:T(8,128)(2,1)} %bitcast.13), channel_id=1, source_target_pairs={{0,8},{1,9},{2,10},{3,11},{4,12},{5,13},{6,14},{7,15},{8,0},{9,1},... | collective-permute-start | bytes 196616 | tf_op jit(solution)/shard_map/ppermute | solution.py:626
  8.2 3.0 %convolution_convert_fusion.refs_15_ = bf16[4,2176]{1,0:T(4,128)(2,1)S(1)} fusion(bf16[4,1024]{1,0:T(4,128)(2,1)} %refs_5_.1, bf16[1024,2176]{1,0:T(8,128)(2,1)} %param.18), kind=kOutput, calls=%fused_computation | convolution fusion | flops 17834496 | bytes 4482048 | tf_op jit(solution)/shard_map/dot_general | solution.py:675
  11.1 0.0 collective-permute-done.1.refs_5_
  11.1 0.0 collective-permute-done.2.refs_4_
  11.1 0.0 collective-permute-done.3.refs_3_
  11.2 0.1 collective-permute-done.refs_1_
  11.3 0.0 copy-done.2
  11.3 0.0 copy-done
  11.3 0.4 %join.2 = (bf16[2,64,512]{2,1,0:T(8,128)(2,1)S(1)}, s32[4,1,256]{2,1,0:T(1,128)S(1)}) custom-call(bf16[1,64,512]{2,1,0:T(8,128)(2,1)S(1)} %bitcast.14, bf16[1,64,512]{2,1,0:T(8,128)(2,1)S(1)} %collective-permute-done.refs_1_, s32[1,1,256]{2,1,0:T(1,128)S(1)} %bitcast.19, s32[1,1,256]{2,1,0:T(1,128)S(1)} %collective-permute-done.3.refs_3_, ...), custom_call_target="tpu_custom_call" | custom-call | tf_op jit(solution)/shard_map/join/pallas_call | solution.py:590
  11.7 2.0 %collective-permute-start.4 = (bf16[2,64,512]{2,1,0:T(8,128)(2,1)S(1)}, bf16[2,64,512]{2,1,0:T(8,128)(2,1)S(1)}, u32[]{:S(2)}, u32[]{:S(2)}) collective-permute-start(bf16[2,64,512]{2,1,0:T(8,128)(2,1)S(1)} %get-tuple-element.21.refs_0_), channel_id=1, source_target_pairs={{0,4},{1,5},{2,6},{3,7},{4,0},{5,1},{6,2},{7,3},{8,12},{9,13},{10,... | collective-permute-start | bytes 393224 | tf_op jit(solution)/shard_map/ppermute | solution.py:626
  13.7 1.5 %collective-permute-start.8 = (s32[4,1,256]{2,0,1:T(4,128)S(1)}, s32[4,1,256]{2,0,1:T(4,128)S(1)}, u32[]{:S(2)}, u32[]{:S(2)}) collective-permute-start(s32[4,1,256]{2,0,1:T(4,128)S(1)} %copy.23), channel_id=1, source_target_pairs={{0,1},{1,0},{2,3},{3,2},{4,5},{5,4},{6,7},{7,6},{8,9},{9,8},{10,11... | collective-permute-start | bytes 12296 | tf_op jit(solution)/shard_map/ppermute | solution.py:626
  15.2 1.5 %collective-permute-start.9 = (s32[4,1,256]{2,0,1:T(4,128)S(1)}, s32[4,1,256]{2,0,1:T(4,128)S(1)}, u32[]{:S(2)}, u32[]{:S(2)}) collective-permute-start(s32[4,1,256]{2,0,1:T(4,128)S(1)} %copy.23), channel_id=1, source_target_pairs={{0,2},{1,3},{2,0},{3,1},{4,6},{5,7},{6,4},{7,5},{8,10},{9,11},{10,... | collective-permute-start | bytes 12296 | tf_op jit(solution)/shard_map/ppermute | solution.py:626
  16.7 0.5 %collective-permute-start.10 = (s32[4,1,256]{2,0,1:T(4,128)S(1)}, s32[4,1,256]{2,0,1:T(4,128)S(1)}, u32[]{:S(2)}, u32[]{:S(2)}) collective-permute-start(s32[4,1,256]{2,0,1:T(4,128)S(1)} %copy.23), channel_id=1, source_target_pairs={{0,3},{1,2},{2,1},{3,0},{4,7},{5,6},{6,5},{7,4},{8,11},{9,10},{10,... | collective-permute-start | bytes 12296 | tf_op jit(solution)/shard_map/ppermute | solution.py:626
  17.2 0.0 collective-permute-done.4.refs_1_
  17.2 0.4 join.3.refs_0_
  17.6 1.6 %collective-permute-start.5 = (bf16[4,64,512]{2,1,0:T(8,128)(2,1)S(1)}, bf16[4,64,512]{2,1,0:T(8,128)(2,1)S(1)}, u32[]{:S(2)}, u32[]{:S(2)}) collective-permute-start(bf16[4,64,512]{2,1,0:T(8,128)(2,1)S(1)} %join.3.refs_0_), channel_id=1, source_target_pairs={{0,1},{1,0},{2,3},{3,2},{4,5},{5,4},{6,7},{7,6},{8,9},{9,8},{10,11... | collective-permute-start | bytes 786440 | tf_op jit(solution)/shard_map/ppermute | solution.py:626
  19.1 1.5 %collective-permute-start.6 = (bf16[4,64,512]{2,1,0:T(8,128)(2,1)S(1)}, bf16[4,64,512]{2,1,0:T(8,128)(2,1)S(1)}, u32[]{:S(2)}, u32[]{:S(2)}) collective-permute-start(bf16[4,64,512]{2,1,0:T(8,128)(2,1)S(1)} %join.3.refs_0_), channel_id=1, source_target_pairs={{0,2},{1,3},{2,0},{3,1},{4,6},{5,7},{6,4},{7,5},{8,10},{9,11},{10,... | collective-permute-start | bytes 786440 | tf_op jit(solution)/shard_map/ppermute | solution.py:626
  20.7 0.0 collective-permute-done.8
  20.7 0.5 %collective-permute-start.7 = (bf16[4,64,512]{2,1,0:T(8,128)(2,1)S(1)}, bf16[4,64,512]{2,1,0:T(8,128)(2,1)S(1)}, u32[]{:S(2)}, u32[]{:S(2)}) collective-permute-start(bf16[4,64,512]{2,1,0:T(8,128)(2,1)S(1)} %join.3.refs_0_), channel_id=1, source_target_pairs={{0,3},{1,2},{2,1},{3,0},{4,7},{5,6},{6,5},{7,4},{8,11},{9,10},{10,... | collective-permute-start | bytes 786440 | tf_op jit(solution)/shard_map/ppermute | solution.py:626
  21.1 0.0 collective-permute-done.9
  21.1 0.2 collective-permute-done.10
  21.3 0.0 copy-done.13
  21.4 12.5 %mixer.1.mixed_ref = bf16[256,1024]{1,0:T(8,128)(2,1)S(1)} custom-call(s32[1]{0:T(128)} %bitcast.here_ref, s32[4]{0:T(128)S(1)} %copy-done.10, s32[4,256]{1,0:T(4,128)S(1)} %bitcast.15, s32[4,256]{1,0:T(4,128)S(1)} %bitcast.21, s32[4,256]{1,0:T(4,128)S(1)} %bitcast.22, s32[4,256]{1,0:T(4,128)S(1)} %bitcast.23, bf16[16,1024]{1,0:T(8,128)(2,1)S(1)} %copy-done.13, ...), custom_call_target="tpu_custom_call" | custom-call | flops 10000000000 | bytes 52428800 | tf_op jit(solution)/shard_map/mixer/pallas_call | solution.py:711
  33.9 0.0 collective-permute-done.5.refs_1_
  33.9 0.0 collective-permute-done.6.refs_2_
  33.9 0.0 collective-permute-done.7.refs_3_
  34.0 0.1 collective-permute-start.11
  34.0 0.5 %collective-permute-start.12 = (bf16[4,64,512]{2,1,0:T(8,128)(2,1)S(1)}, bf16[4,64,512]{2,1,0:T(8,128)(2,1)S(1)}, u32[]{:S(2)}, u32[]{:S(2)}) collective-permute-start(bf16[4,64,512]{2,1,0:T(8,128)(2,1)S(1)} %collective-permute-done.5.refs_1_), channel_id=1, source_target_pairs={{0,16},{16,0},{1,17},{17,1},{2,18},{18,2},{3,19},{19,3},{4,20},{20... | collective-permute-start | bytes 786440 | tf_op jit(solution)/shard_map/ppermute | solution.py:626
  34.5 0.1 collective-permute-start.13
  34.6 0.4 %collective-permute-start.14 = (bf16[4,64,512]{2,1,0:T(8,128)(2,1)S(1)}, bf16[4,64,512]{2,1,0:T(8,128)(2,1)S(1)}, u32[]{:S(2)}, u32[]{:S(2)}) collective-permute-start(bf16[4,64,512]{2,1,0:T(8,128)(2,1)S(1)} %collective-permute-done.7.refs_3_), channel_id=1, source_target_pairs={{0,16},{16,0},{1,17},{17,1},{2,18},{18,2},{3,19},{19,3},{4,20},{20... | collective-permute-start | bytes 786440 | tf_op jit(solution)/shard_map/ppermute | solution.py:626
  35.0 1.2 %output.2.refs_4_ = bf16[256,1024]{1,0:T(8,128)(2,1)} custom-call(s32[1]{0:T(128)} %bitcast.here_ref, s32[1]{0:T(128)} %bitcast.1.side_ref, bf16[256,1024]{1,0:T(8,128)(2,1)S(1)} %mixer.1.mixed_ref, bf16[4,64,512]{2,1,0:T(8,128)(2,1)S(1)} %join.3.refs_0_, bf16[4,64,512]{2,1,0:T(8,128)(2,1)S(1)} %collective-permute-done.5.refs_1_, ...), custom_call_target="tpu_custom_call" | custom-call | flops 268435456 | bytes 4194304 | tf_op jit(solution)/shard_map/output/pallas_call | solution.py:745
  36.2 0.0 collective-permute-done.11.refs_0_
  36.3 0.0 collective-permute-done.12.refs_1_
  36.3 0.0 collective-permute-done.13.refs_2_
  36.3 0.4 collective-permute-done.14.refs_3_
  36.7 1.2 %output.3 = bf16[256,1024]{1,0:T(8,128)(2,1)} custom-call(s32[1]{0:T(128)} %bitcast.here_ref, s32[1]{0:T(128)} %bitcast.1.side_ref, bf16[256,1024]{1,0:T(8,128)(2,1)S(1)} %mixer.1.mixed_ref, bf16[4,64,512]{2,1,0:T(8,128)(2,1)S(1)} %collective-permute-done.11.refs_0_, ...), custom_call_target="tpu_custom_call", output_to_operand_aliasing={{}: (7, {})} | custom-call | flops 268435456 | bytes 4194304 | tf_op jit(solution)/shard_map/output/pallas_call | solution.py:745
  (17 shorter events, 0.0 us)
Async XLA Ops:
  0.0 21.3 %copy-start.13 = (bf16[16,1024]{1,0:T(8,128)(2,1)S(1)}, bf16[16,1024]{1,0:T(8,128)(2,1)}, u32[]{:S(2)}) copy-start(bf16[16,1024]{1,0:T(8,128)(2,1)} %constant.15.clone.refs_4_) | copy-start | bytes 98308
  0.0 21.3 %copy-start.11 = (bf16[256,32]{1,0:T(8,128)(2,1)S(1)}, bf16[256,32]{1,0:T(8,128)(2,1)}, u32[]{:S(2)}) copy-start(bf16[256,32]{1,0:T(8,128)(2,1)} %constant.16.clone.refs_10_) | copy-start | bytes 49156
  0.0 21.3 %copy-start.12 = (bf16[256,64]{1,0:T(8,128)(2,1)S(1)}, bf16[256,64]{1,0:T(8,128)(2,1)}, u32[]{:S(2)}) copy-start(bf16[256,64]{1,0:T(8,128)(2,1)} %constant.17.clone.refs_11_) | copy-start | bytes 98308
  0.0 11.2 %copy-start.2 = (s32[1,256]{1,0:T(1,128)S(1)}, s32[1,256]{1,0:T(1,128)}, u32[]{:S(2)}) copy-start(s32[1,256]{1,0:T(1,128)} %param.15) | copy-start | bytes 3076
  0.0 11.2 %copy-start = (bf16[64,512]{1,0:T(8,128)(2,1)S(1)}, bf16[64,512]{1,0:T(8,128)(2,1)}, u32[]{:S(2)}) copy-start(bf16[64,512]{1,0:T(8,128)(2,1)} %param.26) | copy-start | bytes 196612
  0.0 21.3 %copy-start.1 = (bf16[4,1024]{1,0:T(4,128)(2,1)S(1)}, bf16[4,1024]{1,0:T(4,128)(2,1)}, u32[]{:S(2)}) copy-start(bf16[4,1024]{1,0:T(4,128)(2,1)} %refs_5_.1) | copy-start | bytes 24580
  0.0 21.3 %copy-start.4 = (bf16[1024,16]{0,1:T(8,128)(2,1)S(1)}, bf16[1024,16]{0,1:T(8,128)(2,1)}, u32[]{:S(2)}) copy-start(bf16[1024,16]{0,1:T(8,128)(2,1)} %param.19) | copy-start | bytes 98308
  0.0 21.3 %copy-start.10 = (s32[4]{0:T(128)S(1)}, s32[4]{0:T(128)}, u32[]{:S(2)}) copy-start(s32[4]{0:T(128)} %complement_ref.1) | copy-start | bytes 52
  0.0 21.3 %copy-start.3 = (f32[2,4,1152]{2,1,0:T(4,128)S(1)}, f32[2,4,1152]{2,1,0:T(4,128)}, u32[]{:S(2)}) copy-start(f32[2,4,1152]{2,1,0:T(4,128)} %refs_12_.1) | copy-start | bytes 110596
  0.1 21.3 %copy-start.5 = (f32[2,1152]{1,0:T(2,128)S(1)}, f32[2,1152]{1,0:T(2,128)}, u32[]{:S(2)}) copy-start(f32[2,1152]{1,0:T(2,128)} %refs_13_.1) | copy-start | bytes 27652
  0.1 21.3 %copy-start.7 = (f32[2,16]{1,0:T(2,128)S(1)}, f32[2,16]{1,0:T(2,128)}, u32[]{:S(2)}) copy-start(f32[2,16]{1,0:T(2,128)} %refs_7_.1) | copy-start | bytes 388
  0.1 21.3 %copy-start.8 = (f32[2,16]{1,0:T(2,128)S(1)}, f32[2,16]{1,0:T(2,128)}, u32[]{:S(2)}) copy-start(f32[2,16]{1,0:T(2,128)} %refs_8_.1) | copy-start | bytes 388
  0.1 21.3 %copy-start.9 = (f32[2,16]{1,0:T(2,128)S(1)}, f32[2,16]{1,0:T(2,128)}, u32[]{:S(2)}) copy-start(f32[2,16]{1,0:T(2,128)} %refs_9_.1) | copy-start | bytes 388
  0.1 21.3 %copy-start.6 = (f32[2,1024]{1,0:T(2,128)S(1)}, f32[2,1024]{1,0:T(2,128)}, u32[]{:S(2)}) copy-start(f32[2,1024]{1,0:T(2,128)} %refs_14_.1) | copy-start | bytes 24580
  0.1 11.0 %collective-permute-start.1 = (s32[1,1,256]{2,1,0:T(1,128)}, s32[1,1,256]{2,1,0:T(1,128)S(1)}, u32[]{:S(2)}, u32[]{:S(2)}) collective-permute-start(s32[1,1,256]{2,1,0:T(1,128)} %bitcast.16), channel_id=1, source_target_pairs={{0,12},{1,13},{2,14},{3,15},{4,8},{5,9},{6,10},{7,11},{8,4},{9,5},... | collective-permute-start | bytes 3080 | tf_op jit(solution)/shard_map/ppermute | solution.py:626
  5.2 5.9 %collective-permute-start.2 = (s32[1,1,256]{2,1,0:T(1,128)}, s32[1,1,256]{2,1,0:T(1,128)S(1)}, u32[]{:S(2)}, u32[]{:S(2)}) collective-permute-start(s32[1,1,256]{2,1,0:T(1,128)} %bitcast.17), channel_id=1, source_target_pairs={{0,8},{1,9},{2,10},{3,11},{4,12},{5,13},{6,14},{7,15},{8,0},{9,1},... | collective-permute-start | bytes 3080 | tf_op jit(solution)/shard_map/ppermute | solution.py:626
  5.2 5.9 %collective-permute-start.3 = (s32[1,1,256]{2,1,0:T(1,128)}, s32[1,1,256]{2,1,0:T(1,128)S(1)}, u32[]{:S(2)}, u32[]{:S(2)}) collective-permute-start(s32[1,1,256]{2,1,0:T(1,128)} %bitcast.18), channel_id=1, source_target_pairs={{0,4},{1,5},{2,6},{3,7},{4,0},{5,1},{6,2},{7,3},{8,12},{9,13},{10,... | collective-permute-start | bytes 3080 | tf_op jit(solution)/shard_map/ppermute | solution.py:626
  5.9 5.4 %collective-permute-start = (bf16[1,64,512]{2,1,0:T(8,128)(2,1)}, bf16[1,64,512]{2,1,0:T(8,128)(2,1)S(1)}, u32[]{:S(2)}, u32[]{:S(2)}) collective-permute-start(bf16[1,64,512]{2,1,0:T(8,128)(2,1)} %bitcast.13), channel_id=1, source_target_pairs={{0,8},{1,9},{2,10},{3,11},{4,12},{5,13},{6,14},{7,15},{8,0},{9,1},... | collective-permute-start | bytes 196616 | tf_op jit(solution)/shard_map/ppermute | solution.py:626
  11.7 5.5 %collective-permute-start.4 = (bf16[2,64,512]{2,1,0:T(8,128)(2,1)S(1)}, bf16[2,64,512]{2,1,0:T(8,128)(2,1)S(1)}, u32[]{:S(2)}, u32[]{:S(2)}) collective-permute-start(bf16[2,64,512]{2,1,0:T(8,128)(2,1)S(1)} %get-tuple-element.21.refs_0_), channel_id=1, source_target_pairs={{0,4},{1,5},{2,6},{3,7},{4,0},{5,1},{6,2},{7,3},{8,12},{9,13},{10,... | collective-permute-start | bytes 393224 | tf_op jit(solution)/shard_map/ppermute | solution.py:626
  13.7 6.9 %collective-permute-start.8 = (s32[4,1,256]{2,0,1:T(4,128)S(1)}, s32[4,1,256]{2,0,1:T(4,128)S(1)}, u32[]{:S(2)}, u32[]{:S(2)}) collective-permute-start(s32[4,1,256]{2,0,1:T(4,128)S(1)} %copy.23), channel_id=1, source_target_pairs={{0,1},{1,0},{2,3},{3,2},{4,5},{5,4},{6,7},{7,6},{8,9},{9,8},{10,11... | collective-permute-start | bytes 12296 | tf_op jit(solution)/shard_map/ppermute | solution.py:626
  15.2 5.9 %collective-permute-start.9 = (s32[4,1,256]{2,0,1:T(4,128)S(1)}, s32[4,1,256]{2,0,1:T(4,128)S(1)}, u32[]{:S(2)}, u32[]{:S(2)}) collective-permute-start(s32[4,1,256]{2,0,1:T(4,128)S(1)} %copy.23), channel_id=1, source_target_pairs={{0,2},{1,3},{2,0},{3,1},{4,6},{5,7},{6,4},{7,5},{8,10},{9,11},{10,... | collective-permute-start | bytes 12296 | tf_op jit(solution)/shard_map/ppermute | solution.py:626
  16.7 4.6 %collective-permute-start.10 = (s32[4,1,256]{2,0,1:T(4,128)S(1)}, s32[4,1,256]{2,0,1:T(4,128)S(1)}, u32[]{:S(2)}, u32[]{:S(2)}) collective-permute-start(s32[4,1,256]{2,0,1:T(4,128)S(1)} %copy.23), channel_id=1, source_target_pairs={{0,3},{1,2},{2,1},{3,0},{4,7},{5,6},{6,5},{7,4},{8,11},{9,10},{10,... | collective-permute-start | bytes 12296 | tf_op jit(solution)/shard_map/ppermute | solution.py:626
  17.6 16.3 %collective-permute-start.5 = (bf16[4,64,512]{2,1,0:T(8,128)(2,1)S(1)}, bf16[4,64,512]{2,1,0:T(8,128)(2,1)S(1)}, u32[]{:S(2)}, u32[]{:S(2)}) collective-permute-start(bf16[4,64,512]{2,1,0:T(8,128)(2,1)S(1)} %join.3.refs_0_), channel_id=1, source_target_pairs={{0,1},{1,0},{2,3},{3,2},{4,5},{5,4},{6,7},{7,6},{8,9},{9,8},{10,11... | collective-permute-start | bytes 786440 | tf_op jit(solution)/shard_map/ppermute | solution.py:626
  19.1 14.8 %collective-permute-start.6 = (bf16[4,64,512]{2,1,0:T(8,128)(2,1)S(1)}, bf16[4,64,512]{2,1,0:T(8,128)(2,1)S(1)}, u32[]{:S(2)}, u32[]{:S(2)}) collective-permute-start(bf16[4,64,512]{2,1,0:T(8,128)(2,1)S(1)} %join.3.refs_0_), channel_id=1, source_target_pairs={{0,2},{1,3},{2,0},{3,1},{4,6},{5,7},{6,4},{7,5},{8,10},{9,11},{10,... | collective-permute-start | bytes 786440 | tf_op jit(solution)/shard_map/ppermute | solution.py:626
  20.7 13.3 %collective-permute-start.7 = (bf16[4,64,512]{2,1,0:T(8,128)(2,1)S(1)}, bf16[4,64,512]{2,1,0:T(8,128)(2,1)S(1)}, u32[]{:S(2)}, u32[]{:S(2)}) collective-permute-start(bf16[4,64,512]{2,1,0:T(8,128)(2,1)S(1)} %join.3.refs_0_), channel_id=1, source_target_pairs={{0,3},{1,2},{2,1},{3,0},{4,7},{5,6},{6,5},{7,4},{8,11},{9,10},{10,... | collective-permute-start | bytes 786440 | tf_op jit(solution)/shard_map/ppermute | solution.py:626
  34.0 2.3 %collective-permute-start.11 = (bf16[4,64,512]{2,1,0:T(8,128)(2,1)S(1)}, bf16[4,64,512]{2,1,0:T(8,128)(2,1)S(1)}, u32[]{:S(2)}, u32[]{:S(2)}) collective-permute-start(bf16[4,64,512]{2,1,0:T(8,128)(2,1)S(1)} %join.3.refs_0_), channel_id=1, source_target_pairs={{0,16},{16,0},{1,17},{17,1},{2,18},{18,2},{3,19},{19,3},{4,20},{20... | collective-permute-start | bytes 786440 | tf_op jit(solution)/shard_map/ppermute | solution.py:626
  34.0 2.2 %collective-permute-start.12 = (bf16[4,64,512]{2,1,0:T(8,128)(2,1)S(1)}, bf16[4,64,512]{2,1,0:T(8,128)(2,1)S(1)}, u32[]{:S(2)}, u32[]{:S(2)}) collective-permute-start(bf16[4,64,512]{2,1,0:T(8,128)(2,1)S(1)} %collective-permute-done.5.refs_1_), channel_id=1, source_target_pairs={{0,16},{16,0},{1,17},{17,1},{2,18},{18,2},{3,19},{19,3},{4,20},{20... | collective-permute-start | bytes 786440 | tf_op jit(solution)/shard_map/ppermute | solution.py:626
  34.5 1.8 %collective-permute-start.13 = (bf16[4,64,512]{2,1,0:T(8,128)(2,1)S(1)}, bf16[4,64,512]{2,1,0:T(8,128)(2,1)S(1)}, u32[]{:S(2)}, u32[]{:S(2)}) collective-permute-start(bf16[4,64,512]{2,1,0:T(8,128)(2,1)S(1)} %collective-permute-done.6.refs_2_), channel_id=1, source_target_pairs={{0,16},{16,0},{1,17},{17,1},{2,18},{18,2},{3,19},{19,3},{4,20},{20... | collective-permute-start | bytes 786440 | tf_op jit(solution)/shard_map/ppermute | solution.py:626
  34.6 2.1 %collective-permute-start.14 = (bf16[4,64,512]{2,1,0:T(8,128)(2,1)S(1)}, bf16[4,64,512]{2,1,0:T(8,128)(2,1)S(1)}, u32[]{:S(2)}, u32[]{:S(2)}) collective-permute-start(bf16[4,64,512]{2,1,0:T(8,128)(2,1)S(1)} %collective-permute-done.7.refs_3_), channel_id=1, source_target_pairs={{0,16},{16,0},{1,17},{17,1},{2,18},{18,2},{3,19},{19,3},{4,20},{20... | collective-permute-start | bytes 786440 | tf_op jit(solution)/shard_map/ppermute | solution.py:626

commit v6 on v5

--- a/solution.py
+++ b/solution.py
@@ -305,8 +305,8 @@
         rows8 = letter_rows(raw_rows, letters, 8, complement if strand else None)
         shifted = rows8 + vector_rows[param : param + 1]
         step = jnp.maximum(shifted, 0.0) + jnp.log1p(jnp.exp(-jnp.abs(shifted)))
-        decay = -vector_rows[2 + param : 3 + param] * step * LOG2E
-        return step, decay, jnp.log2(step)
+        decay = jnp.maximum(-vector_rows[2 + param : 3 + param] * step * LOG2E, -1e30)
+        return step, decay, jnp.maximum(jnp.log2(step), -1000.0)
 
     lane8 = iota((8, LANES), 1)
     exponents = [jnp.zeros((8, LANES), F32)] * 3

time: 38 us -> 38 us (level)
  no operation moved by 1% of the time
where the time goes in v6:
time: 38 us; the launch traced here: 37.8 us
  starting transfers between devices  18.2 us (48%)
  Pallas kernels  15.6 us (41%)
  matrix products  2.96 us (8%)
  waiting for transfers between devices  0.75 us (2%)
    ppermute x15, starting transfers between devices, swap(): return lax.ppermute(x, axis, [(i, i ^ mask) for i in range(count)])  18.2 us
    pallas_call x1, Pallas kernels, on_device(): pl.pallas_call(partial(mixer_kernel, letters, taps, state, count), out_sh...  12.4 us
    dot_general x1, matrix products, on_device(): jnp.dot(embedding, in_weight, preferred_element_type=F32).astype(BF16)  2.96 us
    pallas_call x2, Pallas kernels, project(): pl.pallas_call(partial(output_kernel, depth, places, flip), out_shape=jax...  2.39 us
    pallas_call x2, Pallas kernels, join_all(): pl.pallas_call(partial(join_kernel, [len(group) for group in groups]), ou...  0.78 us
  transfers between devices with their start and end apart: 15, of which 3 were waited for; matrix products, arithmetic and copies ran while one was open for 8% of the time, Pallas kernels for 37%

profile of v6, /device:TPU:0, one launch (start us, length us, event | category | flops | bytes accessed | tf_op | source)
XLA Modules:
  0.0 37.8 jit_solution(3943434671907635311)
XLA Ops:
  0.0 0.0 copy-start.1
  0.0 0.0 copy-start.4
  0.0 0.0 copy-start.10
  0.0 0.0 copy-start.3
  0.1 0.0 copy-start.5
  0.1 0.0 copy-start.7
  0.1 0.0 copy-start.8
  0.1 0.0 copy-start.9
  0.1 0.0 copy-start.6
  0.1 5.1 %collective-permute-start.1 = (s32[1,1,256]{2,1,0:T(1,128)}, s32[1,1,256]{2,1,0:T(1,128)S(1)}, u32[]{:S(2)}, u32[]{:S(2)}) collective-permute-start(s32[1,1,256]{2,1,0:T(1,128)} %bitcast.16), channel_id=1, source_target_pairs={{0,12},{1,13},{2,14},{3,15},{4,8},{5,9},{6,10},{7,11},{8,4},{9,5},... | collective-permute-start | bytes 3080 | tf_op jit(solution)/shard_map/ppermute | solution.py:626
  5.2 0.0 collective-permute-start.2
  5.2 0.6 %collective-permute-start.3 = (s32[1,1,256]{2,1,0:T(1,128)}, s32[1,1,256]{2,1,0:T(1,128)S(1)}, u32[]{:S(2)}, u32[]{:S(2)}) collective-permute-start(s32[1,1,256]{2,1,0:T(1,128)} %bitcast.18), channel_id=1, source_target_pairs={{0,4},{1,5},{2,6},{3,7},{4,0},{5,1},{6,2},{7,3},{8,12},{9,13},{10,... | collective-permute-start | bytes 3080 | tf_op jit(solution)/shard_map/ppermute | solution.py:626
  5.9 2.3 %collective-permute-start = (bf16[1,64,512]{2,1,0:T(8,128)(2,1)}, bf16[1,64,512]{2,1,0:T(8,128)(2,1)S(1)}, u32[]{:S(2)}, u32[]{:S(2)}) collective-permute-start(bf16[1,64,512]{2,1,0:T(8,128)(2,1)} %bitcast.13), channel_id=1, source_target_pairs={{0,8},{1,9},{2,10},{3,11},{4,12},{5,13},{6,14},{7,15},{8,0},{9,1},... | collective-permute-start | bytes 196616 | tf_op jit(solution)/shard_map/ppermute | solution.py:626
  8.2 3.0 %convolution_convert_fusion.refs_15_ = bf16[4,2176]{1,0:T(4,128)(2,1)S(1)} fusion(bf16[4,1024]{1,0:T(4,128)(2,1)} %refs_5_.1, bf16[1024,2176]{1,0:T(8,128)(2,1)} %param.18), kind=kOutput, calls=%fused_computation | convolution fusion | flops 17834496 | bytes 4482048 | tf_op jit(solution)/shard_map/dot_general | solution.py:675
  11.1 0.0 collective-permute-done.1.refs_5_
  11.1 0.0 collective-permute-done.2.refs_4_
  11.1 0.0 collective-permute-done.3.refs_3_
  11.2 0.1 collective-permute-done.refs_1_
  11.3 0.0 copy-done.2
  11.3 0.0 copy-done
  11.3 0.4 %join.2 = (bf16[2,64,512]{2,1,0:T(8,128)(2,1)S(1)}, s32[4,1,256]{2,1,0:T(1,128)S(1)}) custom-call(bf16[1,64,512]{2,1,0:T(8,128)(2,1)S(1)} %bitcast.14, bf16[1,64,512]{2,1,0:T(8,128)(2,1)S(1)} %collective-permute-done.refs_1_, s32[1,1,256]{2,1,0:T(1,128)S(1)} %bitcast.19, s32[1,1,256]{2,1,0:T(1,128)S(1)} %collective-permute-done.3.refs_3_, ...), custom_call_target="tpu_custom_call" | custom-call | tf_op jit(solution)/shard_map/join/pallas_call | solution.py:590
  11.7 2.0 %collective-permute-start.4 = (bf16[2,64,512]{2,1,0:T(8,128)(2,1)S(1)}, bf16[2,64,512]{2,1,0:T(8,128)(2,1)S(1)}, u32[]{:S(2)}, u32[]{:S(2)}) collective-permute-start(bf16[2,64,512]{2,1,0:T(8,128)(2,1)S(1)} %get-tuple-element.21.refs_0_), channel_id=1, source_target_pairs={{0,4},{1,5},{2,6},{3,7},{4,0},{5,1},{6,2},{7,3},{8,12},{9,13},{10,... | collective-permute-start | bytes 393224 | tf_op jit(solution)/shard_map/ppermute | solution.py:626
  13.7 1.5 %collective-permute-start.8 = (s32[4,1,256]{2,0,1:T(4,128)S(1)}, s32[4,1,256]{2,0,1:T(4,128)S(1)}, u32[]{:S(2)}, u32[]{:S(2)}) collective-permute-start(s32[4,1,256]{2,0,1:T(4,128)S(1)} %copy.23), channel_id=1, source_target_pairs={{0,1},{1,0},{2,3},{3,2},{4,5},{5,4},{6,7},{7,6},{8,9},{9,8},{10,11... | collective-permute-start | bytes 12296 | tf_op jit(solution)/shard_map/ppermute | solution.py:626
  15.2 1.5 %collective-permute-start.9 = (s32[4,1,256]{2,0,1:T(4,128)S(1)}, s32[4,1,256]{2,0,1:T(4,128)S(1)}, u32[]{:S(2)}, u32[]{:S(2)}) collective-permute-start(s32[4,1,256]{2,0,1:T(4,128)S(1)} %copy.23), channel_id=1, source_target_pairs={{0,2},{1,3},{2,0},{3,1},{4,6},{5,7},{6,4},{7,5},{8,10},{9,11},{10,... | collective-permute-start | bytes 12296 | tf_op jit(solution)/shard_map/ppermute | solution.py:626
  16.7 0.5 %collective-permute-start.10 = (s32[4,1,256]{2,0,1:T(4,128)S(1)}, s32[4,1,256]{2,0,1:T(4,128)S(1)}, u32[]{:S(2)}, u32[]{:S(2)}) collective-permute-start(s32[4,1,256]{2,0,1:T(4,128)S(1)} %copy.23), channel_id=1, source_target_pairs={{0,3},{1,2},{2,1},{3,0},{4,7},{5,6},{6,5},{7,4},{8,11},{9,10},{10,... | collective-permute-start | bytes 12296 | tf_op jit(solution)/shard_map/ppermute | solution.py:626
  17.2 0.0 collective-permute-done.4.refs_1_
  17.2 0.4 join.3.refs_0_
  17.6 1.6 %collective-permute-start.5 = (bf16[4,64,512]{2,1,0:T(8,128)(2,1)S(1)}, bf16[4,64,512]{2,1,0:T(8,128)(2,1)S(1)}, u32[]{:S(2)}, u32[]{:S(2)}) collective-permute-start(bf16[4,64,512]{2,1,0:T(8,128)(2,1)S(1)} %join.3.refs_0_), channel_id=1, source_target_pairs={{0,1},{1,0},{2,3},{3,2},{4,5},{5,4},{6,7},{7,6},{8,9},{9,8},{10,11... | collective-permute-start | bytes 786440 | tf_op jit(solution)/shard_map/ppermute | solution.py:626
  19.1 1.5 %collective-permute-start.6 = (bf16[4,64,512]{2,1,0:T(8,128)(2,1)S(1)}, bf16[4,64,512]{2,1,0:T(8,128)(2,1)S(1)}, u32[]{:S(2)}, u32[]{:S(2)}) collective-permute-start(bf16[4,64,512]{2,1,0:T(8,128)(2,1)S(1)} %join.3.refs_0_), channel_id=1, source_target_pairs={{0,2},{1,3},{2,0},{3,1},{4,6},{5,7},{6,4},{7,5},{8,10},{9,11},{10,... | collective-permute-start | bytes 786440 | tf_op jit(solution)/shard_map/ppermute | solution.py:626
  20.7 0.0 collective-permute-done.8
  20.7 0.5 %collective-permute-start.7 = (bf16[4,64,512]{2,1,0:T(8,128)(2,1)S(1)}, bf16[4,64,512]{2,1,0:T(8,128)(2,1)S(1)}, u32[]{:S(2)}, u32[]{:S(2)}) collective-permute-start(bf16[4,64,512]{2,1,0:T(8,128)(2,1)S(1)} %join.3.refs_0_), channel_id=1, source_target_pairs={{0,3},{1,2},{2,1},{3,0},{4,7},{5,6},{6,5},{7,4},{8,11},{9,10},{10,... | collective-permute-start | bytes 786440 | tf_op jit(solution)/shard_map/ppermute | solution.py:626
  21.1 0.0 collective-permute-done.9
  21.1 0.2 collective-permute-done.10
  21.3 0.0 copy-done.13
  21.4 12.4 %mixer.1.mixed_ref = bf16[256,1024]{1,0:T(8,128)(2,1)S(1)} custom-call(s32[1]{0:T(128)} %bitcast.here_ref, s32[4]{0:T(128)S(1)} %copy-done.10, s32[4,256]{1,0:T(4,128)S(1)} %bitcast.15, s32[4,256]{1,0:T(4,128)S(1)} %bitcast.21, s32[4,256]{1,0:T(4,128)S(1)} %bitcast.22, s32[4,256]{1,0:T(4,128)S(1)} %bitcast.23, bf16[16,1024]{1,0:T(8,128)(2,1)S(1)} %copy-done.13, ...), custom_call_target="tpu_custom_call" | custom-call | flops 10000000000 | bytes 52428800 | tf_op jit(solution)/shard_map/mixer/pallas_call | solution.py:711
  33.9 0.0 collective-permute-done.5.refs_1_
  33.9 0.0 collective-permute-done.6.refs_2_
  33.9 0.0 collective-permute-done.7.refs_3_
  33.9 0.1 collective-permute-start.11
  34.0 0.5 %collective-permute-start.12 = (bf16[4,64,512]{2,1,0:T(8,128)(2,1)S(1)}, bf16[4,64,512]{2,1,0:T(8,128)(2,1)S(1)}, u32[]{:S(2)}, u32[]{:S(2)}) collective-permute-start(bf16[4,64,512]{2,1,0:T(8,128)(2,1)S(1)} %collective-permute-done.5.refs_1_), channel_id=1, source_target_pairs={{0,16},{16,0},{1,17},{17,1},{2,18},{18,2},{3,19},{19,3},{4,20},{20... | collective-permute-start | bytes 786440 | tf_op jit(solution)/shard_map/ppermute | solution.py:626
  34.5 0.1 collective-permute-start.13
  34.6 0.4 %collective-permute-start.14 = (bf16[4,64,512]{2,1,0:T(8,128)(2,1)S(1)}, bf16[4,64,512]{2,1,0:T(8,128)(2,1)S(1)}, u32[]{:S(2)}, u32[]{:S(2)}) collective-permute-start(bf16[4,64,512]{2,1,0:T(8,128)(2,1)S(1)} %collective-permute-done.7.refs_3_), channel_id=1, source_target_pairs={{0,16},{16,0},{1,17},{17,1},{2,18},{18,2},{3,19},{19,3},{4,20},{20... | collective-permute-start | bytes 786440 | tf_op jit(solution)/shard_map/ppermute | solution.py:626
  35.0 1.2 %output.2.refs_4_ = bf16[256,1024]{1,0:T(8,128)(2,1)} custom-call(s32[1]{0:T(128)} %bitcast.here_ref, s32[1]{0:T(128)} %bitcast.1.side_ref, bf16[256,1024]{1,0:T(8,128)(2,1)S(1)} %mixer.1.mixed_ref, bf16[4,64,512]{2,1,0:T(8,128)(2,1)S(1)} %join.3.refs_0_, bf16[4,64,512]{2,1,0:T(8,128)(2,1)S(1)} %collective-permute-done.5.refs_1_, ...), custom_call_target="tpu_custom_call" | custom-call | flops 268435456 | bytes 4194304 | tf_op jit(solution)/shard_map/output/pallas_call | solution.py:745
  36.2 0.0 collective-permute-done.11.refs_0_
  36.2 0.0 collective-permute-done.12.refs_1_
  36.2 0.0 collective-permute-done.13.refs_2_
  36.3 0.4 collective-permute-done.14.refs_3_
  36.6 1.2 %output.3 = bf16[256,1024]{1,0:T(8,128)(2,1)} custom-call(s32[1]{0:T(128)} %bitcast.here_ref, s32[1]{0:T(128)} %bitcast.1.side_ref, bf16[256,1024]{1,0:T(8,128)(2,1)S(1)} %mixer.1.mixed_ref, bf16[4,64,512]{2,1,0:T(8,128)(2,1)S(1)} %collective-permute-done.11.refs_0_, ...), custom_call_target="tpu_custom_call", output_to_operand_aliasing={{}: (7, {})} | custom-call | flops 268435456 | bytes 4194304 | tf_op jit(solution)/shard_map/output/pallas_call | solution.py:745
  (17 shorter events, 0.0 us)
Async XLA Ops:
  0.0 21.3 %copy-start.13 = (bf16[16,1024]{1,0:T(8,128)(2,1)S(1)}, bf16[16,1024]{1,0:T(8,128)(2,1)}, u32[]{:S(2)}) copy-start(bf16[16,1024]{1,0:T(8,128)(2,1)} %constant.15.clone.refs_4_) | copy-start | bytes 98308
  0.0 21.3 %copy-start.11 = (bf16[256,32]{1,0:T(8,128)(2,1)S(1)}, bf16[256,32]{1,0:T(8,128)(2,1)}, u32[]{:S(2)}) copy-start(bf16[256,32]{1,0:T(8,128)(2,1)} %constant.16.clone.refs_10_) | copy-start | bytes 49156
  0.0 21.3 %copy-start.12 = (bf16[256,64]{1,0:T(8,128)(2,1)S(1)}, bf16[256,64]{1,0:T(8,128)(2,1)}, u32[]{:S(2)}) copy-start(bf16[256,64]{1,0:T(8,128)(2,1)} %constant.17.clone.refs_11_) | copy-start | bytes 98308
  0.0 11.2 %copy-start.2 = (s32[1,256]{1,0:T(1,128)S(1)}, s32[1,256]{1,0:T(1,128)}, u32[]{:S(2)}) copy-start(s32[1,256]{1,0:T(1,128)} %param.15) | copy-start | bytes 3076
  0.0 11.2 %copy-start = (bf16[64,512]{1,0:T(8,128)(2,1)S(1)}, bf16[64,512]{1,0:T(8,128)(2,1)}, u32[]{:S(2)}) copy-start(bf16[64,512]{1,0:T(8,128)(2,1)} %param.26) | copy-start | bytes 196612
  0.0 21.3 %copy-start.1 = (bf16[4,1024]{1,0:T(4,128)(2,1)S(1)}, bf16[4,1024]{1,0:T(4,128)(2,1)}, u32[]{:S(2)}) copy-start(bf16[4,1024]{1,0:T(4,128)(2,1)} %refs_5_.1) | copy-start | bytes 24580
  0.0 21.3 %copy-start.4 = (bf16[1024,16]{0,1:T(8,128)(2,1)S(1)}, bf16[1024,16]{0,1:T(8,128)(2,1)}, u32[]{:S(2)}) copy-start(bf16[1024,16]{0,1:T(8,128)(2,1)} %param.19) | copy-start | bytes 98308
  0.0 21.3 %copy-start.10 = (s32[4]{0:T(128)S(1)}, s32[4]{0:T(128)}, u32[]{:S(2)}) copy-start(s32[4]{0:T(128)} %complement_ref.1) | copy-start | bytes 52
  0.0 21.3 %copy-start.3 = (f32[2,4,1152]{2,1,0:T(4,128)S(1)}, f32[2,4,1152]{2,1,0:T(4,128)}, u32[]{:S(2)}) copy-start(f32[2,4,1152]{2,1,0:T(4,128)} %refs_12_.1) | copy-start | bytes 110596
  0.1 21.3 %copy-start.5 = (f32[2,1152]{1,0:T(2,128)S(1)}, f32[2,1152]{1,0:T(2,128)}, u32[]{:S(2)}) copy-start(f32[2,1152]{1,0:T(2,128)} %refs_13_.1) | copy-start | bytes 27652
  0.1 21.3 %copy-start.7 = (f32[2,16]{1,0:T(2,128)S(1)}, f32[2,16]{1,0:T(2,128)}, u32[]{:S(2)}) copy-start(f32[2,16]{1,0:T(2,128)} %refs_7_.1) | copy-start | bytes 388
  0.1 21.3 %copy-start.8 = (f32[2,16]{1,0:T(2,128)S(1)}, f32[2,16]{1,0:T(2,128)}, u32[]{:S(2)}) copy-start(f32[2,16]{1,0:T(2,128)} %refs_8_.1) | copy-start | bytes 388
  0.1 21.3 %copy-start.9 = (f32[2,16]{1,0:T(2,128)S(1)}, f32[2,16]{1,0:T(2,128)}, u32[]{:S(2)}) copy-start(f32[2,16]{1,0:T(2,128)} %refs_9_.1) | copy-start | bytes 388
  0.1 21.3 %copy-start.6 = (f32[2,1024]{1,0:T(2,128)S(1)}, f32[2,1024]{1,0:T(2,128)}, u32[]{:S(2)}) copy-start(f32[2,1024]{1,0:T(2,128)} %refs_14_.1) | copy-start | bytes 24580
  0.1 11.0 %collective-permute-start.1 = (s32[1,1,256]{2,1,0:T(1,128)}, s32[1,1,256]{2,1,0:T(1,128)S(1)}, u32[]{:S(2)}, u32[]{:S(2)}) collective-permute-start(s32[1,1,256]{2,1,0:T(1,128)} %bitcast.16), channel_id=1, source_target_pairs={{0,12},{1,13},{2,14},{3,15},{4,8},{5,9},{6,10},{7,11},{8,4},{9,5},... | collective-permute-start | bytes 3080 | tf_op jit(solution)/shard_map/ppermute | solution.py:626
  5.2 5.9 %collective-permute-start.2 = (s32[1,1,256]{2,1,0:T(1,128)}, s32[1,1,256]{2,1,0:T(1,128)S(1)}, u32[]{:S(2)}, u32[]{:S(2)}) collective-permute-start(s32[1,1,256]{2,1,0:T(1,128)} %bitcast.17), channel_id=1, source_target_pairs={{0,8},{1,9},{2,10},{3,11},{4,12},{5,13},{6,14},{7,15},{8,0},{9,1},... | collective-permute-start | bytes 3080 | tf_op jit(solution)/shard_map/ppermute | solution.py:626
  5.2 5.9 %collective-permute-start.3 = (s32[1,1,256]{2,1,0:T(1,128)}, s32[1,1,256]{2,1,0:T(1,128)S(1)}, u32[]{:S(2)}, u32[]{:S(2)}) collective-permute-start(s32[1,1,256]{2,1,0:T(1,128)} %bitcast.18), channel_id=1, source_target_pairs={{0,4},{1,5},{2,6},{3,7},{4,0},{5,1},{6,2},{7,3},{8,12},{9,13},{10,... | collective-permute-start | bytes 3080 | tf_op jit(solution)/shard_map/ppermute | solution.py:626
  5.9 5.4 %collective-permute-start = (bf16[1,64,512]{2,1,0:T(8,128)(2,1)}, bf16[1,64,512]{2,1,0:T(8,128)(2,1)S(1)}, u32[]{:S(2)}, u32[]{:S(2)}) collective-permute-start(bf16[1,64,512]{2,1,0:T(8,128)(2,1)} %bitcast.13), channel_id=1, source_target_pairs={{0,8},{1,9},{2,10},{3,11},{4,12},{5,13},{6,14},{7,15},{8,0},{9,1},... | collective-permute-start | bytes 196616 | tf_op jit(solution)/shard_map/ppermute | solution.py:626
  11.7 5.5 %collective-permute-start.4 = (bf16[2,64,512]{2,1,0:T(8,128)(2,1)S(1)}, bf16[2,64,512]{2,1,0:T(8,128)(2,1)S(1)}, u32[]{:S(2)}, u32[]{:S(2)}) collective-permute-start(bf16[2,64,512]{2,1,0:T(8,128)(2,1)S(1)} %get-tuple-element.21.refs_0_), channel_id=1, source_target_pairs={{0,4},{1,5},{2,6},{3,7},{4,0},{5,1},{6,2},{7,3},{8,12},{9,13},{10,... | collective-permute-start | bytes 393224 | tf_op jit(solution)/shard_map/ppermute | solution.py:626
  13.7 6.9 %collective-permute-start.8 = (s32[4,1,256]{2,0,1:T(4,128)S(1)}, s32[4,1,256]{2,0,1:T(4,128)S(1)}, u32[]{:S(2)}, u32[]{:S(2)}) collective-permute-start(s32[4,1,256]{2,0,1:T(4,128)S(1)} %copy.23), channel_id=1, source_target_pairs={{0,1},{1,0},{2,3},{3,2},{4,5},{5,4},{6,7},{7,6},{8,9},{9,8},{10,11... | collective-permute-start | bytes 12296 | tf_op jit(solution)/shard_map/ppermute | solution.py:626
  15.2 5.9 %collective-permute-start.9 = (s32[4,1,256]{2,0,1:T(4,128)S(1)}, s32[4,1,256]{2,0,1:T(4,128)S(1)}, u32[]{:S(2)}, u32[]{:S(2)}) collective-permute-start(s32[4,1,256]{2,0,1:T(4,128)S(1)} %copy.23), channel_id=1, source_target_pairs={{0,2},{1,3},{2,0},{3,1},{4,6},{5,7},{6,4},{7,5},{8,10},{9,11},{10,... | collective-permute-start | bytes 12296 | tf_op jit(solution)/shard_map/ppermute | solution.py:626
  16.7 4.6 %collective-permute-start.10 = (s32[4,1,256]{2,0,1:T(4,128)S(1)}, s32[4,1,256]{2,0,1:T(4,128)S(1)}, u32[]{:S(2)}, u32[]{:S(2)}) collective-permute-start(s32[4,1,256]{2,0,1:T(4,128)S(1)} %copy.23), channel_id=1, source_target_pairs={{0,3},{1,2},{2,1},{3,0},{4,7},{5,6},{6,5},{7,4},{8,11},{9,10},{10,... | collective-permute-start | bytes 12296 | tf_op jit(solution)/shard_map/ppermute | solution.py:626
  17.6 16.3 %collective-permute-start.5 = (bf16[4,64,512]{2,1,0:T(8,128)(2,1)S(1)}, bf16[4,64,512]{2,1,0:T(8,128)(2,1)S(1)}, u32[]{:S(2)}, u32[]{:S(2)}) collective-permute-start(bf16[4,64,512]{2,1,0:T(8,128)(2,1)S(1)} %join.3.refs_0_), channel_id=1, source_target_pairs={{0,1},{1,0},{2,3},{3,2},{4,5},{5,4},{6,7},{7,6},{8,9},{9,8},{10,11... | collective-permute-start | bytes 786440 | tf_op jit(solution)/shard_map/ppermute | solution.py:626
  19.1 14.7 %collective-permute-start.6 = (bf16[4,64,512]{2,1,0:T(8,128)(2,1)S(1)}, bf16[4,64,512]{2,1,0:T(8,128)(2,1)S(1)}, u32[]{:S(2)}, u32[]{:S(2)}) collective-permute-start(bf16[4,64,512]{2,1,0:T(8,128)(2,1)S(1)} %join.3.refs_0_), channel_id=1, source_target_pairs={{0,2},{1,3},{2,0},{3,1},{4,6},{5,7},{6,4},{7,5},{8,10},{9,11},{10,... | collective-permute-start | bytes 786440 | tf_op jit(solution)/shard_map/ppermute | solution.py:626
  20.7 13.2 %collective-permute-start.7 = (bf16[4,64,512]{2,1,0:T(8,128)(2,1)S(1)}, bf16[4,64,512]{2,1,0:T(8,128)(2,1)S(1)}, u32[]{:S(2)}, u32[]{:S(2)}) collective-permute-start(bf16[4,64,512]{2,1,0:T(8,128)(2,1)S(1)} %join.3.refs_0_), channel_id=1, source_target_pairs={{0,3},{1,2},{2,1},{3,0},{4,7},{5,6},{6,5},{7,4},{8,11},{9,10},{10,... | collective-permute-start | bytes 786440 | tf_op jit(solution)/shard_map/ppermute | solution.py:626
  33.9 2.3 %collective-permute-start.11 = (bf16[4,64,512]{2,1,0:T(8,128)(2,1)S(1)}, bf16[4,64,512]{2,1,0:T(8,128)(2,1)S(1)}, u32[]{:S(2)}, u32[]{:S(2)}) collective-permute-start(bf16[4,64,512]{2,1,0:T(8,128)(2,1)S(1)} %join.3.refs_0_), channel_id=1, source_target_pairs={{0,16},{16,0},{1,17},{17,1},{2,18},{18,2},{3,19},{19,3},{4,20},{20... | collective-permute-start | bytes 786440 | tf_op jit(solution)/shard_map/ppermute | solution.py:626
  34.0 2.2 %collective-permute-start.12 = (bf16[4,64,512]{2,1,0:T(8,128)(2,1)S(1)}, bf16[4,64,512]{2,1,0:T(8,128)(2,1)S(1)}, u32[]{:S(2)}, u32[]{:S(2)}) collective-permute-start(bf16[4,64,512]{2,1,0:T(8,128)(2,1)S(1)} %collective-permute-done.5.refs_1_), channel_id=1, source_target_pairs={{0,16},{16,0},{1,17},{17,1},{2,18},{18,2},{3,19},{19,3},{4,20},{20... | collective-permute-start | bytes 786440 | tf_op jit(solution)/shard_map/ppermute | solution.py:626
  34.5 1.8 %collective-permute-start.13 = (bf16[4,64,512]{2,1,0:T(8,128)(2,1)S(1)}, bf16[4,64,512]{2,1,0:T(8,128)(2,1)S(1)}, u32[]{:S(2)}, u32[]{:S(2)}) collective-permute-start(bf16[4,64,512]{2,1,0:T(8,128)(2,1)S(1)} %collective-permute-done.6.refs_2_), channel_id=1, source_target_pairs={{0,16},{16,0},{1,17},{17,1},{2,18},{18,2},{3,19},{19,3},{4,20},{20... | collective-permute-start | bytes 786440 | tf_op jit(solution)/shard_map/ppermute | solution.py:626
  34.6 2.1 %collective-permute-start.14 = (bf16[4,64,512]{2,1,0:T(8,128)(2,1)S(1)}, bf16[4,64,512]{2,1,0:T(8,128)(2,1)S(1)}, u32[]{:S(2)}, u32[]{:S(2)}) collective-permute-start(bf16[4,64,512]{2,1,0:T(8,128)(2,1)S(1)} %collective-permute-done.7.refs_3_), channel_id=1, source_target_pairs={{0,16},{16,0},{1,17},{17,1},{2,18},{18,2},{3,19},{19,3},{4,20},{20... | collective-permute-start | bytes 786440 | tf_op jit(solution)/shard_map/ppermute | solution.py:626
